TPU v7x, 32 devices: a whole 2x2x4 slice. The times are simulated.
32 devices in a mesh: section: 2 (over x), dp: 4 (over z), tensor: 4 (over y, core).
Axes of the slice: x: 2, y: 2, z: 4, core: 2. Of those that a mesh axis runs over, the one named last changes fastest.
Arguments:
- section_input: bfloat16 [2, 4, 256, 4096], P('section', 'dp', 'tensor'), may hold values from -6 to 6
- carried_grad: bfloat16 [2, 4, 256, 4096], P('section', 'dp', 'tensor'), may hold values from -6 to 6
- hidden_grad: bfloat16 [2, 4, 256, 3584], P('section', 'dp', None, 'tensor'), may hold values from -6 to 6
- saved_gate: bfloat16 [2, 4, 256, 3584], P('section', 'dp', None, 'tensor'), may hold values from -8 to 8
- w_up: bfloat16 [2, 4096, 3584], P('section', 'dp', 'tensor'), may hold values from -0.09375 to 0.09375
Outputs:
- passed_grad: bfloat16 [2, 4, 256, 4096], P('section', 'dp', 'tensor')
- up_weight_grad: bfloat16 [2, 4096, 3584], P('section', 'dp', 'tensor')
All inputs are finite; a program needn't handle non-finite values.
Results may differ from a plain program's by a relative error of at most 0.015.
Values may be sent and summed in bfloat16 or wider, within the bound.
No kernel may reach another device: no remote copies, remote signals or barrier semaphores. Data moves between devices by JAX's collectives and lax.ppermute only.
A program may use at most 64 MiB of HBM per device.

v0:
```python
import jax
import jax.numpy as jnp
from jax import lax
from jax.sharding import PartitionSpec as P


def from_behind(value, axis, steps):
    count = lax.axis_size(axis)
    initial, last = (max(0, -steps), min(count, count - steps))
    return lax.ppermute(value, axis, [(source, source + steps) for source in range(initial, last)])


def body(section_input, carried_grad, hidden_grad, saved_gate, w_up):
    input_rows_local = section_input[0, 0]
    carried = carried_grad[0, 0].astype(jnp.float32)
    gate = saved_gate[0, 0].astype(jnp.float32)
    grad_vals = hidden_grad[0, 0].astype(jnp.float32)
    up_weight = w_up[0]
    replicas = lax.axis_size("dp")
    shards = lax.axis_size("tensor")
    tokens = gate.shape[0]
    hidden_width = gate.shape[1]
    width = input_rows_local.shape[1]
    slice_width = up_weight.shape[0]
    sig = jax.nn.sigmoid(gate)
    up_grad = (grad_vals * gate * sig).astype(jnp.bfloat16)
    all_up_grads = lax.all_gather(up_grad, "dp", axis=0, tiled=True)
    shaped = all_up_grads.reshape(replicas, tokens, hidden_width)
    summed = lax.psum_scatter(
        jnp.einsum("rtf,df->trd", shaped, up_weight, preferred_element_type=jnp.float32).astype(
            jnp.bfloat16
        ),
        "tensor",
        scatter_dimension=0,
        tiled=True,
    ).astype(jnp.float32)
    moved = lax.all_to_all(
        summed.astype(jnp.bfloat16), "dp", split_axis=1, concat_axis=2, tiled=True
    ).astype(summed.dtype)
    input_grad = (moved.reshape(tokens // shards, width) + carried).astype(jnp.bfloat16)
    passed = from_behind(input_grad, "section", -1)
    full_input = lax.all_gather(input_rows_local, "tensor", axis=0, tiled=True)
    input_columns = lax.all_to_all(full_input, "dp", split_axis=1, concat_axis=0, tiled=True)
    weight_grad = lax.dot_general(
        input_columns, all_up_grads, (((0,), (0,)), ((), ())), preferred_element_type=jnp.float32
    )
    weight_grad = (weight_grad / replicas).astype(jnp.bfloat16)
    return (
        passed.reshape(1, 1, tokens // shards, width),
        weight_grad.reshape(1, slice_width, hidden_width),
    )


def solution(mesh):
    return jax.shard_map(
        body,
        mesh=mesh,
        in_specs=(
            P("section", "dp", "tensor", None),
            P("section", "dp", "tensor", None),
            P("section", "dp", None, "tensor"),
            P("section", "dp", None, "tensor"),
            P("section", "dp", "tensor"),
        ),
        out_specs=(P("section", "dp", "tensor", None), P("section", "dp", "tensor")),
        check_vma=False,
    )
```

profile of v0, /device:TPU:0, one launch (start us, length us, event | category | flops | bytes accessed | tf_op | source)
XLA Modules:
  0.0 192.3 jit_solution(17325260614228086612)
XLA Ops:
  7.2 0.0 copy-start
  7.2 0.0 all-gather.5.cloned.1.call-start
  7.2 2.3 %fusion.7 = bf16[1,1,256,896]{3,2,1,0:T(8,128)(2,1)} fusion(bf16[1,1,256,896]{3,2,1,0:T(8,128)(2,1)} %param.8, bf16[1,1,256,896]{3,2,1,0:T(8,128)(2,1)} %param.7), kind=kLoop, calls=%fused_computation.11 | loop fusion | flops 1835008 | bytes 1376256 | tf_op jit(solution)/shard_map/convert_element_type | solution.py:26
  9.5 0.0 all-gather.5.cloned.1.call-update
  9.6 0.0 reduce-scatter.2.cloned.1.call-start
  9.6 44.7 %all-gather.5.cloned.1.call-done = bf16[1,1,1024,896]{3,2,1,0:T(8,128)(2,1)} async-done(((bf16[1,1,256,896]{3,2,1,0:T(8,128)(2,1)}), bf16[1,1,1024,896]{3,2,1,0:T(8,128)(2,1)}) %all-gather.5.cloned.1.call-update) | async-done | bytes 1835024 | tf_op jit(solution)/shard_map/all_gather | solution.py:27
  54.3 0.0 copy-done
  54.3 5.2 %convert_bitcast_fusion = bf16[256,4,1024]{2,0,1:T(8,128)(2,1)} fusion(bf16[4,256,896]{2,1,0:T(8,128)(2,1)} %bitcast.32, bf16[1,1024,896]{2,1,0:T(8,128)(2,1)S(1)} %copy-done), kind=kOutput, calls=%fused_computation.1 | convolution fusion | flops 1880096768 | bytes 5767168 | tf_op jit(solution)/shard_map/rtf,df->trd/dot_general | solution.py:30
  59.5 0.0 reduce-scatter.2.cloned.1.call-update
  59.5 0.0 all-gather.7.cloned.1.call-start
  59.6 0.7 all-gather.7.cloned.1.call-update
  60.2 29.7 %reduce-scatter.2.cloned.1.call-done = bf16[64,4,1024]{2,0,1:T(8,128)(2,1)} async-done(((bf16[256,4,1024]{2,0,1:T(8,128)(2,1)}), bf16[64,4,1024]{2,0,1:T(8,128)(2,1)}) %reduce-scatter.2.cloned.1.call-update) | async-done | bytes 524304 | tf_op jit(solution)/shard_map/reduce_scatter | solution.py:29
  90.0 4.6 %all-to-all-start = ((bf16[64,4,1024]{2,0,1:T(8,128)(2,1)}), bf16[64,4,1024]{2,0,1:T(8,128)(2,1)S(1)}, u32[]{:S(2)}, u32[]{:S(2)}) async-start(bf16[64,4,1024]{2,0,1:T(8,128)(2,1)} %reduce-scatter.2.cloned.1.call-done), calls=%async_computation.1 | async-start | bytes 1048576 | tf_op jit(solution)/shard_map/all_to_all | solution.py:37
  94.5 19.7 %all-gather.7.cloned.1.call-done = bf16[1,1,256,4096]{3,2,1,0:T(8,128)(2,1)} async-done(((bf16[1,1,64,4096]{3,2,1,0:T(8,128)(2,1)}), bf16[1,1,256,4096]{3,2,1,0:T(8,128)(2,1)}) %all-gather.7.cloned.1.call-update) | async-done | bytes 2097168 | tf_op jit(solution)/shard_map/all_gather | solution.py:42
  114.2 4.1 %copy.15 = bf16[1,1,256,4096]{2,3,1,0:T(8,128)(2,1)} copy(bf16[1,1,256,4096]{3,2,1,0:T(8,128)(2,1)} %all-gather.7.cloned.1.call-done) | data formatting | bytes 4194304 | tf_op jit(solution)/shard_map/all_gather | solution.py:42
  118.3 0.0 all-to-all-done
  118.3 4.6 %all-to-all-start.1 = ((bf16[256,4,1024]{0,2,1:T(8,128)(2,1)}), bf16[256,4,1024]{0,2,1:T(8,128)(2,1)}, u32[]{:S(2)}, u32[]{:S(2)}) async-start(bf16[256,4,1024]{0,2,1:T(8,128)(2,1)} %bitcast.28), calls=%async_computation.2 | async-start | bytes 4194304 | tf_op jit(solution)/shard_map/all_to_all | solution.py:43
  122.9 0.0 copy-start.1
  122.9 0.1 convert_bitcast_fusion.1
  123.0 0.1 copy.18
  123.1 0.8 copy-done.1
  123.9 0.1 fusion.5
  124.0 1.3 collective-permute-start
  125.3 46.4 %all-to-all-done.1 = bf16[256,4,1024]{0,2,1:T(8,128)(2,1)} async-done(((bf16[256,4,1024]{0,2,1:T(8,128)(2,1)}), bf16[256,4,1024]{0,2,1:T(8,128)(2,1)}, u32[]{:S(2)}, u32[]{:S(2)}) %all-to-all-start.1) | async-done | bytes 2097184 | tf_op jit(solution)/shard_map/all_to_all | solution.py:43
  171.7 4.0 %copy.16 = bf16[4,256,1024]{2,1,0:T(8,128)(2,1)} copy(bf16[4,256,1024]{1,2,0:T(8,128)(2,1)} %bitcast.8) | data formatting | bytes 4194304 | tf_op jit(solution)/shard_map/all_to_all | solution.py:43
  175.7 5.5 %fusion.2 = bf16[1,1024,896]{1,2,0:T(8,128)(2,1)} fusion(bf16[1024,1024]{1,0:T(8,128)(2,1)} %bitcast.30, bf16[1,1,1024,896]{3,2,1,0:T(8,128)(2,1)} %all-gather.5.cloned.1.call-done), kind=kOutput, calls=%fused_computation.4 | convolution fusion | flops 1880883200 | bytes 5767168 | tf_op jit(solution)/shard_map/dot_general | solution.py:44
  181.1 3.8 %copy.17 = bf16[1,1024,896]{2,1,0:T(8,128)(2,1)} copy(bf16[1,1024,896]{1,2,0:T(8,128)(2,1)} %fusion.2) | data formatting | bytes 3670016
  184.9 0.0 collective-permute-done
  184.9 0.8 copy.20
Async XLA Ops:
  7.2 47.1 %copy-start = (bf16[1,1024,896]{2,1,0:T(8,128)(2,1)S(1)}, bf16[1,1024,896]{2,1,0:T(8,128)(2,1)}, u32[]{:S(2)}) copy-start(bf16[1,1024,896]{2,1,0:T(8,128)(2,1)} %param.9) | copy-start | bytes 5505028
  7.2 47.1 %all-gather.5.cloned.1.call-start = ((), (), s32[]{:S(2)}) async-start(), calls=%async_computation.4 | async-start | bytes 2293760 | tf_op jit(solution)/shard_map/all_gather | solution.py:27
  9.6 80.4 %reduce-scatter.2.cloned.1.call-start = ((), (), s32[]{:S(2)}) async-start(), calls=%async_computation.3 | async-start | bytes 2621440 | tf_op jit(solution)/shard_map/reduce_scatter | solution.py:29
  59.5 54.7 %all-gather.7.cloned.1.call-start = ((), (), s32[]{:S(2)}) async-start(), calls=%async_computation.5 | async-start | bytes 2621440 | tf_op jit(solution)/shard_map/all_gather | solution.py:42
  90.0 28.3 %all-to-all-start = ((bf16[64,4,1024]{2,0,1:T(8,128)(2,1)}), bf16[64,4,1024]{2,0,1:T(8,128)(2,1)S(1)}, u32[]{:S(2)}, u32[]{:S(2)}) async-start(bf16[64,4,1024]{2,0,1:T(8,128)(2,1)} %reduce-scatter.2.cloned.1.call-done), calls=%async_computation.1 | async-start | bytes 1048576 | tf_op jit(solution)/shard_map/all_to_all | solution.py:37
  118.3 53.4 %all-to-all-start.1 = ((bf16[256,4,1024]{0,2,1:T(8,128)(2,1)}), bf16[256,4,1024]{0,2,1:T(8,128)(2,1)}, u32[]{:S(2)}, u32[]{:S(2)}) async-start(bf16[256,4,1024]{0,2,1:T(8,128)(2,1)} %bitcast.28), calls=%async_computation.2 | async-start | bytes 4194304 | tf_op jit(solution)/shard_map/all_to_all | solution.py:43
  122.9 1.0 copy-start.1
  124.0 60.9 %collective-permute-start = (bf16[64,4096]{1,0:T(8,128)(2,1)S(1)}, bf16[64,4096]{1,0:T(8,128)(2,1)S(1)}, u32[]{:S(2)}, u32[]{:S(2)}) collective-permute-start(bf16[64,4096]{1,0:T(8,128)(2,1)S(1)} %fusion.5), channel_id=1, source_target_pairs={{16,0},{17,1},{18,2},{19,3},{20,4},{21,5},{22,6},{23,7},{24,8},{25... | collective-permute-start | bytes 1572872 | tf_op jit(solution)/shard_map/ppermute | solution.py:10
Sparse Core Ops, SparseCore 0:
  10.2 44.0 all-gather.4
  59.6 30.2 reduce-scatter.1
  91.6 22.5 all-gather.6
where the time goes:
time: 193 us; the launch traced here: 192 us
  waiting for transfers between devices  141 us (73%)
  between operations  13.8 us (7%)
  local copies, waits for them, and re-layouts  13.6 us (7%)
  matrix products  10.7 us (6%)
  starting transfers between devices  10.6 us (5%)
  other arithmetic  2.51 us (1%)
    all_to_all x1, waiting for transfers between devices, body(): lax.all_to_all(full_input, 'dp', split_axis=1, concat_axis=0, tiled=True)  46.4 us
    all_gather x1, waiting for transfers between devices, body(): all_up_grads = lax.all_gather(up_grad, 'dp', axis=0, tiled=True)  44.7 us
    reduce_scatter x1, waiting for transfers between devices, body(): lax.psum_scatter(jnp.einsum('rtf,df->trd', shaped, up_weight, preferred_e...  29.7 us
    all_gather x1, waiting for transfers between devices, body(): full_input = lax.all_gather(input_rows_local, 'tensor', axis=0, tiled=True)  19.7 us
    dot_general x1, matrix products, body(): lax.dot_general(input_columns, all_up_grads, (((0,), (0,)), ((), ())), pr...  5.46 us
    unnamed x6, local copies, waits for them, and re-layouts  5.45 us
    dot_general x1, matrix products, body(): jnp.einsum('rtf,df->trd', shaped, up_weight, preferred_element_type=jnp.f...  5.19 us
    all_to_all x1, starting transfers between devices, body(): lax.all_to_all(full_input, 'dp', split_axis=1, concat_axis=0, tiled=True)  4.6 us
  transfers between devices with their start and end apart: 6, of which 4 were waited for; matrix products, arithmetic and copies ran while one was open for 9% of the time, Pallas kernels for 0%

commit v1 on v0

v1 whole, which is shorter than its diff:
```python
import jax
import jax.numpy as jnp
from jax import lax
from jax.sharding import PartitionSpec as P

AXES = ("section", "dp", "tensor")
BF16 = jnp.bfloat16
F32 = jnp.float32


def moved(value, sizes, target):
    sections, replicas, shards = sizes
    pairs = []
    for s in range(sections):
        for r in range(replicas):
            for t in range(shards):
                to = target(s, r, t)
                if to is not None:
                    source = (s * replicas + r) * shards + t
                    pairs.append((source, (to[0] * replicas + to[1]) * shards + to[2]))
    return lax.ppermute(value, AXES, pairs)


def after(value, *others):
    return lax.optimization_barrier((value, *others))[0]


def gathered(block, sizes, t):
    shards = sizes[2]
    step = shards // 2
    while step:
        other = moved(block, sizes, lambda s, r, i: (s, r, i ^ step))
        mine_first = (t & step) == 0
        a = block[None] if block.ndim == 2 else block
        b = other[None] if other.ndim == 2 else other
        first = jnp.where(mine_first, a, b)
        second = jnp.where(mine_first, b, a)
        block = jnp.stack([first, second], axis=1).reshape(-1, *a.shape[1:])
        step //= 2
    return block.reshape(-1, block.shape[-1])


def scattered(parts, sizes, t):
    shards = sizes[2]
    rows, columns = parts.shape
    value = parts.reshape(shards, rows // shards, columns)
    step = 1
    while step < shards:
        value = value.reshape(-1, 2, rows // shards, columns)
        bit = (t // step) & 1
        keep = lax.dynamic_index_in_dim(value, bit, 1, keepdims=False)
        give = lax.dynamic_index_in_dim(value, 1 - bit, 1, keepdims=False)
        got = moved(give, sizes, lambda s, r, i: (s, r, i ^ step) if s > 0 else None)
        value = (keep.astype(F32) + got.astype(F32)).astype(BF16)
        step *= 2
    return value.reshape(rows // shards, columns)


def body(section_input, carried_grad, hidden_grad, saved_gate, w_up):
    sizes = tuple(lax.axis_size(a) for a in AXES)
    sections, replicas, shards = sizes
    r, t = lax.axis_index("dp"), lax.axis_index("tensor")
    x = section_input[0, 0]
    w = w_up[0]
    width = w.shape[0]
    rows = x.shape[0]

    gate = saved_gate[0, 0].astype(F32)
    ug = (hidden_grad[0, 0].astype(F32) * gate * jax.nn.sigmoid(gate)).astype(BF16)

    carried = moved(carried_grad[0, 0], sizes, lambda s, i, j: (s - 1, i, j) if s > 0 else None)

    def x_columns(k):
        return lax.dynamic_slice(x, (0, ((r + k) % replicas) * width), (rows, width))

    def turned(value, k):
        return moved(value, sizes, lambda s, i, j: (s, (i + k) % replicas, j))

    ugs, xs, pieces = [ug], [x_columns(0)], []
    xs.append(turned(x_columns(1), 1))
    for k in range(1, replicas):
        ugs.append(turned(ugs[-1], 1))
    for k in range(2, replicas):
        xs.append(turned(after(x_columns(k), ugs[-1]), k))
    for k in range(replicas):
        part = lax.dot_general(ugs[k], w, (((1,), (1,)), ((), ())), preferred_element_type=F32).astype(BF16)
        piece = scattered(part, sizes, t)
        pieces.append(
            moved(piece, sizes, lambda s, i, j: (s - 1, (i - k) % replicas, j) if s > 0 else None)
        )
    total = 0
    for k in range(replicas):
        total = total + lax.dot_general(
            gathered(xs[k], sizes, t), ugs[k], (((0,), (0,)), ((), ())), preferred_element_type=F32
        )
    weight_grad = (total / replicas).astype(BF16)

    stacked = jnp.stack(pieces, axis=1)
    ordered = jnp.roll(stacked, r, axis=1).reshape(rows, -1)
    passed = (carried.astype(F32) + ordered.astype(F32)).astype(BF16)
    return passed[None, None], weight_grad[None]


def solution(mesh):
    return jax.shard_map(
        body,
        mesh=mesh,
        in_specs=(
            P("section", "dp", "tensor", None),
            P("section", "dp", "tensor", None),
            P("section", "dp", None, "tensor"),
            P("section", "dp", None, "tensor"),
            P("section", "dp", "tensor"),
        ),
        out_specs=(P("section", "dp", "tensor", None), P("section", "dp", "tensor")),
        check_vma=False,
    )
```

time: 193 us -> 106 us (0.55)
  waiting for transfers between devices: 141 us -> 58.7 us
  starting transfers between devices: 10.6 us -> 27.1 us
  between operations: 13.8 us -> 1.28 us
  local copies, waits for them, and re-layouts: 13.6 us -> 2.99 us
  other arithmetic: 2.51 us -> 6.32 us
    all_gather x2 -> x0, waiting for transfers between devices: 64.3 us -> none  [the longest x1 44.7 us: body(): all_up_grads = lax.all_gather(up_grad, 'dp', axis=0, tiled=True)]
    ppermute x1 -> x27, waiting for transfers between devices: 0.01 us -> 58.7 us  [moved(): return lax.ppermute(value, AXES, pairs)]
    all_to_all x2 -> x0, waiting for transfers between devices: 46.4 us -> none  [the longest x1 46.4 us: body(): lax.all_to_all(full_input, 'dp', split_axis=1, concat_axis=0, tiled=True)]
    reduce_scatter x1 -> x0, waiting for transfers between devices: 29.7 us -> none  [body(): lax.psum_scatter(jnp.einsum('rtf,df->trd', shaped, up_weight, preferred_e...]
    ppermute x1 -> x27, starting transfers between devices: 1.29 us -> 27.1 us  [moved(): return lax.ppermute(value, AXES, pairs)]
    all_to_all x2 -> x0, starting transfers between devices: 9.19 us -> none  [the longest x1 4.6 us: body(): lax.all_to_all(full_input, 'dp', split_axis=1, concat_axis=0, tiled=True)]
    unnamed x6 -> x13, local copies, waits for them, and re-layouts: 5.45 us -> 0.09 us
    all_gather x1 -> x0, local copies, waits for them, and re-layouts: 4.07 us -> none  [body(): full_input = lax.all_gather(input_rows_local, 'tensor', axis=0, tiled=True)]
  transfers between devices with their start and end apart: 6 -> 27, of which waited for: 4 -> 11; matrix products, arithmetic and copies ran while one was open for 9% -> 15% of each run, Pallas kernels for 0% -> 0%
where the time goes in v1:
time: 106 us
  waiting for transfers between devices  58.7 us (55%)
  starting transfers between devices  27.1 us (26%)
  matrix products  9.27 us (9%)
  other arithmetic  6.32 us (6%)
  local copies, waits for them, and re-layouts  2.99 us (3%)
  between operations  1.28 us (1%)
    ppermute x27, waiting for transfers between devices, moved(): return lax.ppermute(value, AXES, pairs)  58.7 us
    ppermute x27, starting transfers between devices, moved(): return lax.ppermute(value, AXES, pairs)  27.1 us
    dot_general x4, matrix products, body(): lax.dot_general(gathered(xs[k], sizes, t), ugs[k], (((0,), (0,)), ((), ()...  5.31 us
    dot_general x4, matrix products, body(): lax.dot_general(ugs[k], w, (((1,), (1,)), ((), ())), preferred_element_ty...  3.96 us
    another operation x11, other arithmetic, gathered(): block = jnp.stack([first, second], axis=1).reshape(-1, *a.shape[1:])  2.28 us
  transfers between devices with their start and end apart: 27, of which 11 were waited for; matrix products, arithmetic and copies ran while one was open for 15% of the time, Pallas kernels for 0%

profile of v1, /device:TPU:0, one launch (start us, length us, event | category | flops | bytes accessed | tf_op | source)
XLA Modules:
  0.0 105.6 jit_solution(6719853169431394310)
XLA Ops:
  0.6 1.6 %fusion.31 = bf16[256,896]{1,0:T(8,128)(2,1)S(1)} fusion(bf16[1,1,256,896]{3,2,1,0:T(8,128)(2,1)} %param.8, bf16[1,1,256,896]{3,2,1,0:T(8,128)(2,1)} %param.7), kind=kLoop, calls=%fused_computation.36 | loop fusion | flops 1835008 | bytes 1376256 | tf_op jit(solution)/shard_map/convert_element_type | solution.py:69
  2.2 3.1 %collective-permute-start.4 = (bf16[256,896]{1,0:T(8,128)(2,1)S(1)}, bf16[256,896]{1,0:T(8,128)(2,1)}, u32[]{:S(2)}, u32[]{:S(2)}) collective-permute-start(bf16[256,896]{1,0:T(8,128)(2,1)S(1)} %fusion.31), channel_id=1, source_target_pairs={{0,4},{1,5},{2,6},{3,7},{4,8},{5,9},{6,10},{7,11},{8,12},{9,13},{1... | collective-permute-start | bytes 1376264 | tf_op jit(solution)/shard_map/ppermute | solution.py:21
  5.3 1.8 %dynamic-slice_bitcast_fusion.6 = (bf16[64,1024]{1,0:T(8,128)(2,1)}, bf16[64,1024]{1,0:T(8,128)(2,1)S(1)}, bf16[64,1024]{1,0:T(8,128)(2,1)}, bf16[64,1024]{1,0:T(8,128)(2,1)}) fusion(bf16[1,1,64,4096]{3,2,1,0:T(8,128)(2,1)} %param.5, s32[]{:T(128)S(6)} %select_n.173, s32[]{:T(128)S(6)} %select_n.167, s32[]{:T(128)S(6)} %select_n.185, s32[]{:T(128)S(6)} %select_n.179), kind=kLoop, calls=%fused_computation.77 | loop fusion | bytes 1048592 | tf_op jit(solution)/shard_map/dynamic_slice | solution.py:74
  7.1 1.6 %collective-permute-start.18 = (bf16[64,1024]{1,0:T(8,128)(2,1)}, bf16[64,1024]{1,0:T(8,128)(2,1)}, u32[]{:S(2)}, u32[]{:S(2)}) collective-permute-start(bf16[64,1024]{1,0:T(8,128)(2,1)} %get-tuple-element.8), channel_id=1, source_target_pairs={{0,4},{1,5},{2,6},{3,7},{4,8},{5,9},{6,10},{7,11},{8,12},{9,13},{1... | collective-permute-start | bytes 393224 | tf_op jit(solution)/shard_map/ppermute | solution.py:21
  8.7 1.5 %collective-permute-start.16 = (bf16[64,1024]{1,0:T(8,128)(2,1)S(1)}, bf16[64,1024]{1,0:T(8,128)(2,1)}, u32[]{:S(2)}, u32[]{:S(2)}) collective-permute-start(bf16[64,1024]{1,0:T(8,128)(2,1)S(1)} %get-tuple-element.9), channel_id=1, source_target_pairs={{0,2},{1,3},{2,0},{3,1},{4,6},{5,7},{6,4},{7,5},{8,10},{9,11},{10,... | collective-permute-start | bytes 393224 | tf_op jit(solution)/shard_map/ppermute | solution.py:21
  11.7 1.4 %collective-permute-start.1 = (bf16[2,64,1024]{2,1,0:T(8,128)(2,1)}, bf16[2,64,1024]{2,1,0:T(8,128)(2,1)}, u32[]{:S(2)}, u32[]{:S(2)}) collective-permute-start(bf16[2,64,1024]{2,1,0:T(8,128)(2,1)} %dynamic-slice_bitcast_fusion.3), channel_id=1, source_target_pairs={{16,17},{17,16},{18,19},{19,18},{20,21},{21,20},{22,23},{23,22},{2... | collective-permute-start | bytes 786440 | tf_op jit(solution)/shard_map/ppermute | solution.py:21
  13.1 1.3 %collective-permute-start = (bf16[64,4096]{1,0:T(8,128)(2,1)}, bf16[64,4096]{1,0:T(8,128)(2,1)S(1)}, u32[]{:S(2)}, u32[]{:S(2)}) collective-permute-start(bf16[64,4096]{1,0:T(8,128)(2,1)} %bitcast.172), channel_id=1, source_target_pairs={{16,0},{17,1},{18,2},{19,3},{20,4},{21,5},{22,6},{23,7},{24,8},{25... | collective-permute-start | bytes 1572872 | tf_op jit(solution)/shard_map/ppermute | solution.py:21
  14.4 0.9 select_bitcast_fusion.15
  15.4 5.3 %collective-permute-done.18 = bf16[64,1024]{1,0:T(8,128)(2,1)} collective-permute-done((bf16[64,1024]{1,0:T(8,128)(2,1)}, bf16[64,1024]{1,0:T(8,128)(2,1)}, u32[]{:S(2)}, u32[]{:S(2)}) %collective-permute-start.18) | collective-permute-done | bytes 131104 | tf_op jit(solution)/shard_map/ppermute | solution.py:21
  20.7 1.5 %collective-permute-start.19 = (bf16[64,1024]{1,0:T(8,128)(2,1)}, bf16[64,1024]{1,0:T(8,128)(2,1)S(1)}, u32[]{:S(2)}, u32[]{:S(2)}) collective-permute-start(bf16[64,1024]{1,0:T(8,128)(2,1)} %collective-permute-done.18), channel_id=1, source_target_pairs={{0,2},{1,3},{2,0},{3,1},{4,6},{5,7},{6,4},{7,5},{8,10},{9,11},{10,... | collective-permute-start | bytes 393224 | tf_op jit(solution)/shard_map/ppermute | solution.py:21
  22.3 1.0 fusion.30
  24.0 1.9 %collective-permute-done.19 = bf16[64,1024]{1,0:T(8,128)(2,1)S(1)} collective-permute-done((bf16[64,1024]{1,0:T(8,128)(2,1)}, bf16[64,1024]{1,0:T(8,128)(2,1)S(1)}, u32[]{:S(2)}, u32[]{:S(2)}) %collective-permute-start.19) | collective-permute-done | bytes 131104 | tf_op jit(solution)/shard_map/ppermute | solution.py:21
  25.9 0.9 select_bitcast_fusion.13
  27.0 1.3 %collective-permute-start.3 = (bf16[64,1024]{1,0:T(8,128)(2,1)S(1)}, bf16[64,1024]{1,0:T(8,128)(2,1)S(1)}, u32[]{:S(2)}, u32[]{:S(2)}) collective-permute-start(bf16[64,1024]{1,0:T(8,128)(2,1)S(1)} %fusion.32), channel_id=1, source_target_pairs={{16,0},{17,1},{18,2},{19,3},{20,4},{21,5},{22,6},{23,7},{24,8},{25... | collective-permute-start | bytes 393224 | tf_op jit(solution)/shard_map/ppermute | solution.py:21
  29.2 1.8 %fusion.12 = bf16[256,1024]{1,0:T(8,128)(2,1)S(1)} fusion(bf16[256,896]{1,0:T(8,128)(2,1)} %collective-permute-done.4, bf16[1,1024,896]{2,1,0:T(8,128)(2,1)S(1)} %copy-done), kind=kOutput, calls=%fused_computation.11 | convolution fusion | flops 470024192 | bytes 2818048 | tf_op jit(solution)/shard_map/dot_general | solution.py:86
  31.9 4.0 %collective-permute-done.3 = bf16[64,1024]{1,0:T(8,128)(2,1)S(1)} collective-permute-done((bf16[64,1024]{1,0:T(8,128)(2,1)S(1)}, bf16[64,1024]{1,0:T(8,128)(2,1)S(1)}, u32[]{:S(2)}, u32[]{:S(2)}) %collective-permute-start.3) | collective-permute-done | bytes 131104 | tf_op jit(solution)/shard_map/ppermute | solution.py:21
  35.9 1.8 %fusion.37 = f32[1024,896]{1,0:T(8,128)S(1)} fusion(bf16[256,1024]{1,0:T(8,128)(2,1)S(1)} %bitcast.161, bf16[256,896]{1,0:T(8,128)(2,1)} %collective-permute-done.4), kind=kOutput, calls=%fused_computation.86 | convolution fusion | flops 469762048 | bytes 4653056 | tf_op jit(solution)/shard_map/dot_general | solution.py:93
  37.7 8.9 %collective-permute-done.8 = bf16[256,896]{1,0:T(8,128)(2,1)S(1)} collective-permute-done((bf16[256,896]{1,0:T(8,128)(2,1)}, bf16[256,896]{1,0:T(8,128)(2,1)S(1)}, u32[]{:S(2)}, u32[]{:S(2)}) %collective-permute-start.8) | collective-permute-done | bytes 458784 | tf_op jit(solution)/shard_map/ppermute | solution.py:21
  50.0 1.3 %collective-permute-start.7 = (bf16[64,1024]{1,0:T(8,128)(2,1)S(1)}, bf16[64,1024]{1,0:T(8,128)(2,1)S(1)}, u32[]{:S(2)}, u32[]{:S(2)}) collective-permute-start(bf16[64,1024]{1,0:T(8,128)(2,1)S(1)} %fusion.33), channel_id=1, source_target_pairs={{16,12},{17,13},{18,14},{19,15},{20,0},{21,1},{22,2},{23,3},{24,4}... | collective-permute-start | bytes 393224 | tf_op jit(solution)/shard_map/ppermute | solution.py:21
  51.3 1.3 %collective-permute-start.11 = (bf16[64,1024]{1,0:T(8,128)(2,1)S(1)}, bf16[64,1024]{1,0:T(8,128)(2,1)S(1)}, u32[]{:S(2)}, u32[]{:S(2)}) collective-permute-start(bf16[64,1024]{1,0:T(8,128)(2,1)S(1)} %fusion.34), channel_id=1, source_target_pairs={{16,8},{17,9},{18,10},{19,11},{20,12},{21,13},{22,14},{23,15},{24,... | collective-permute-start | bytes 393224 | tf_op jit(solution)/shard_map/ppermute | solution.py:21
  52.6 10.4 %collective-permute-done.12 = bf16[256,896]{1,0:T(8,128)(2,1)S(1)} collective-permute-done((bf16[256,896]{1,0:T(8,128)(2,1)S(1)}, bf16[256,896]{1,0:T(8,128)(2,1)S(1)}, u32[]{:S(2)}, u32[]{:S(2)}) %collective-permute-start.12) | collective-permute-done | bytes 458784 | tf_op jit(solution)/shard_map/ppermute | solution.py:21
  64.5 10.2 %collective-permute-done.7 = bf16[64,1024]{1,0:T(8,128)(2,1)S(1)} collective-permute-done((bf16[64,1024]{1,0:T(8,128)(2,1)S(1)}, bf16[64,1024]{1,0:T(8,128)(2,1)S(1)}, u32[]{:S(2)}, u32[]{:S(2)}) %collective-permute-start.7) | collective-permute-done | bytes 131104 | tf_op jit(solution)/shard_map/ppermute | solution.py:21
  74.7 2.3 %collective-permute-start.21 = (bf16[64,1024]{1,0:T(8,128)(2,1)S(1)}, bf16[64,1024]{1,0:T(8,128)(2,1)S(1)}, u32[]{:S(2)}, u32[]{:S(2)}) collective-permute-start(bf16[64,1024]{1,0:T(8,128)(2,1)S(1)} %copy-done.2), channel_id=1, source_target_pairs={{0,8},{1,9},{2,10},{3,11},{4,12},{5,13},{6,14},{7,15},{8,0},{9,1},... | collective-permute-start | bytes 393224 | tf_op jit(solution)/shard_map/ppermute | solution.py:21
  77.0 1.5 %collective-permute-start.24 = (bf16[64,1024]{1,0:T(8,128)(2,1)S(1)}, bf16[64,1024]{1,0:T(8,128)(2,1)S(1)}, u32[]{:S(2)}, u32[]{:S(2)}) collective-permute-start(bf16[64,1024]{1,0:T(8,128)(2,1)S(1)} %copy-done.1), channel_id=1, source_target_pairs={{0,12},{1,13},{2,14},{3,15},{4,0},{5,1},{6,2},{7,3},{8,4},{9,5},{1... | collective-permute-start | bytes 393224 | tf_op jit(solution)/shard_map/ppermute | solution.py:21
  78.6 4.8 %collective-permute-done.11 = bf16[64,1024]{1,0:T(8,128)(2,1)S(1)} collective-permute-done((bf16[64,1024]{1,0:T(8,128)(2,1)S(1)}, bf16[64,1024]{1,0:T(8,128)(2,1)S(1)}, u32[]{:S(2)}, u32[]{:S(2)}) %collective-permute-start.11) | collective-permute-done | bytes 131104 | tf_op jit(solution)/shard_map/ppermute | solution.py:21
  83.4 1.2 %collective-permute-done.21 = bf16[64,1024]{1,0:T(8,128)(2,1)S(1)} collective-permute-done((bf16[64,1024]{1,0:T(8,128)(2,1)S(1)}, bf16[64,1024]{1,0:T(8,128)(2,1)S(1)}, u32[]{:S(2)}, u32[]{:S(2)}) %collective-permute-start.21) | collective-permute-done | bytes 131104 | tf_op jit(solution)/shard_map/ppermute | solution.py:21
  84.6 1.5 %collective-permute-start.22 = (bf16[64,1024]{1,0:T(8,128)(2,1)S(1)}, bf16[64,1024]{1,0:T(8,128)(2,1)S(1)}, u32[]{:S(2)}, u32[]{:S(2)}) collective-permute-start(bf16[64,1024]{1,0:T(8,128)(2,1)S(1)} %collective-permute-done.21), channel_id=1, source_target_pairs={{0,2},{1,3},{2,0},{3,1},{4,6},{5,7},{6,4},{7,5},{8,10},{9,11},{10,... | collective-permute-start | bytes 393224 | tf_op jit(solution)/shard_map/ppermute | solution.py:21
  87.4 2.8 %collective-permute-done.22 = bf16[64,1024]{1,0:T(8,128)(2,1)S(1)} collective-permute-done((bf16[64,1024]{1,0:T(8,128)(2,1)S(1)}, bf16[64,1024]{1,0:T(8,128)(2,1)S(1)}, u32[]{:S(2)}, u32[]{:S(2)}) %collective-permute-start.22) | collective-permute-done | bytes 131104 | tf_op jit(solution)/shard_map/ppermute | solution.py:21
  90.2 1.4 %collective-permute-done.25 = bf16[64,1024]{1,0:T(8,128)(2,1)S(1)} collective-permute-done((bf16[64,1024]{1,0:T(8,128)(2,1)S(1)}, bf16[64,1024]{1,0:T(8,128)(2,1)S(1)}, u32[]{:S(2)}, u32[]{:S(2)}) %collective-permute-start.25) | collective-permute-done | bytes 131104 | tf_op jit(solution)/shard_map/ppermute | solution.py:21
  92.4 1.3 %collective-permute-start.15 = (bf16[64,1024]{1,0:T(8,128)(2,1)S(1)}, bf16[64,1024]{1,0:T(8,128)(2,1)S(1)}, u32[]{:S(2)}, u32[]{:S(2)}) collective-permute-start(bf16[64,1024]{1,0:T(8,128)(2,1)S(1)} %fusion.35), channel_id=1, source_target_pairs={{16,4},{17,5},{18,6},{19,7},{20,8},{21,9},{22,10},{23,11},{24,12},... | collective-permute-start | bytes 393224 | tf_op jit(solution)/shard_map/ppermute | solution.py:21
  94.8 2.0 %fusion.8 = bf16[1,1024,896]{2,1,0:T(8,128)(2,1)} fusion(bf16[256,1024]{1,0:T(8,128)(2,1)S(1)} %bitcast.163, bf16[256,896]{1,0:T(8,128)(2,1)S(1)} %collective-permute-done.12, f32[1024,896]{1,0:T(8,128)S(1)} %fusion.38, f32[1024,896]{1,0:T(8,128)S(1)} %fusion.36, f32[1024,896]{1,0:T(8,128)S(1)} %fusion.37), kind=kOutput, calls=%fused_computation.9 | convolution fusion | flops 474349568 | bytes 13828096 | tf_op jit(solution)/shard_map/dot_general | solution.py:93
  96.8 7.6 %collective-permute-done.15 = bf16[64,1024]{1,0:T(8,128)(2,1)S(1)} collective-permute-done((bf16[64,1024]{1,0:T(8,128)(2,1)S(1)}, bf16[64,1024]{1,0:T(8,128)(2,1)S(1)}, u32[]{:S(2)}, u32[]{:S(2)}) %collective-permute-start.15) | collective-permute-done | bytes 131104 | tf_op jit(solution)/shard_map/ppermute | solution.py:21
  (83 shorter events, 13.0 us)
Async XLA Ops:
  0.6 9.6 %copy-start = (bf16[1,1024,896]{2,1,0:T(8,128)(2,1)S(1)}, bf16[1,1024,896]{2,1,0:T(8,128)(2,1)}, u32[]{:S(2)}) copy-start(bf16[1,1024,896]{2,1,0:T(8,128)(2,1)} %param.9) | copy-start | bytes 5505028
  2.2 27.0 %collective-permute-start.4 = (bf16[256,896]{1,0:T(8,128)(2,1)S(1)}, bf16[256,896]{1,0:T(8,128)(2,1)}, u32[]{:S(2)}, u32[]{:S(2)}) collective-permute-start(bf16[256,896]{1,0:T(8,128)(2,1)S(1)} %fusion.31), channel_id=1, source_target_pairs={{0,4},{1,5},{2,6},{3,7},{4,8},{5,9},{6,10},{7,11},{8,12},{9,13},{1... | collective-permute-start | bytes 1376264 | tf_op jit(solution)/shard_map/ppermute | solution.py:21
  7.1 13.6 %collective-permute-start.18 = (bf16[64,1024]{1,0:T(8,128)(2,1)}, bf16[64,1024]{1,0:T(8,128)(2,1)}, u32[]{:S(2)}, u32[]{:S(2)}) collective-permute-start(bf16[64,1024]{1,0:T(8,128)(2,1)} %get-tuple-element.8), channel_id=1, source_target_pairs={{0,4},{1,5},{2,6},{3,7},{4,8},{5,9},{6,10},{7,11},{8,12},{9,13},{1... | collective-permute-start | bytes 393224 | tf_op jit(solution)/shard_map/ppermute | solution.py:21
  8.7 5.7 %collective-permute-start.16 = (bf16[64,1024]{1,0:T(8,128)(2,1)S(1)}, bf16[64,1024]{1,0:T(8,128)(2,1)}, u32[]{:S(2)}, u32[]{:S(2)}) collective-permute-start(bf16[64,1024]{1,0:T(8,128)(2,1)S(1)} %get-tuple-element.9), channel_id=1, source_target_pairs={{0,2},{1,3},{2,0},{3,1},{4,6},{5,7},{6,4},{7,5},{8,10},{9,11},{10,... | collective-permute-start | bytes 393224 | tf_op jit(solution)/shard_map/ppermute | solution.py:21
  11.7 10.6 %collective-permute-start.1 = (bf16[2,64,1024]{2,1,0:T(8,128)(2,1)}, bf16[2,64,1024]{2,1,0:T(8,128)(2,1)}, u32[]{:S(2)}, u32[]{:S(2)}) collective-permute-start(bf16[2,64,1024]{2,1,0:T(8,128)(2,1)} %dynamic-slice_bitcast_fusion.3), channel_id=1, source_target_pairs={{16,17},{17,16},{18,19},{19,18},{20,21},{21,20},{22,23},{23,22},{2... | collective-permute-start | bytes 786440 | tf_op jit(solution)/shard_map/ppermute | solution.py:21
  13.1 91.7 %collective-permute-start = (bf16[64,4096]{1,0:T(8,128)(2,1)}, bf16[64,4096]{1,0:T(8,128)(2,1)S(1)}, u32[]{:S(2)}, u32[]{:S(2)}) collective-permute-start(bf16[64,4096]{1,0:T(8,128)(2,1)} %bitcast.172), channel_id=1, source_target_pairs={{16,0},{17,1},{18,2},{19,3},{20,4},{21,5},{22,6},{23,7},{24,8},{25... | collective-permute-start | bytes 1572872 | tf_op jit(solution)/shard_map/ppermute | solution.py:21
  15.4 13.0 %collective-permute-start.17 = (bf16[2,64,1024]{2,1,0:T(8,128)(2,1)S(1)}, bf16[2,64,1024]{2,1,0:T(8,128)(2,1)S(1)}, u32[]{:S(2)}, u32[]{:S(2)}) collective-permute-start(bf16[2,64,1024]{2,1,0:T(8,128)(2,1)S(1)} %maximum_bitcast_fusion), channel_id=1, source_target_pairs={{0,1},{1,0},{2,3},{3,2},{4,5},{5,4},{6,7},{7,6},{8,9},{9,8},{10,11... | collective-permute-start | bytes 786440 | tf_op jit(solution)/shard_map/ppermute | solution.py:21
  20.7 5.2 %collective-permute-start.19 = (bf16[64,1024]{1,0:T(8,128)(2,1)}, bf16[64,1024]{1,0:T(8,128)(2,1)S(1)}, u32[]{:S(2)}, u32[]{:S(2)}) collective-permute-start(bf16[64,1024]{1,0:T(8,128)(2,1)} %collective-permute-done.18), channel_id=1, source_target_pairs={{0,2},{1,3},{2,0},{3,1},{4,6},{5,7},{6,4},{7,5},{8,10},{9,11},{10,... | collective-permute-start | bytes 393224 | tf_op jit(solution)/shard_map/ppermute | solution.py:21
  23.3 3.7 %collective-permute-start.2 = (bf16[1,64,1024]{2,1,0:T(8,128)(2,1)S(1)}, bf16[1,64,1024]{2,1,0:T(8,128)(2,1)S(1)}, u32[]{:S(2)}, u32[]{:S(2)}) collective-permute-start(bf16[1,64,1024]{2,1,0:T(8,128)(2,1)S(1)} %constant_dynamic-slice_fusion.3), channel_id=1, source_target_pairs={{16,18},{17,19},{18,16},{19,17},{20,22},{21,23},{22,20},{23,21},{2... | collective-permute-start | bytes 393224 | tf_op jit(solution)/shard_map/ppermute | solution.py:21
  26.9 4.9 %collective-permute-start.20 = (bf16[2,64,1024]{2,1,0:T(8,128)(2,1)S(1)}, bf16[2,64,1024]{2,1,0:T(8,128)(2,1)S(1)}, u32[]{:S(2)}, u32[]{:S(2)}) collective-permute-start(bf16[2,64,1024]{2,1,0:T(8,128)(2,1)S(1)} %maximum_bitcast_fusion.1), channel_id=1, source_target_pairs={{0,1},{1,0},{2,3},{3,2},{4,5},{5,4},{6,7},{7,6},{8,9},{9,8},{10,11... | collective-permute-start | bytes 786440 | tf_op jit(solution)/shard_map/ppermute | solution.py:21
  27.0 8.9 %collective-permute-start.3 = (bf16[64,1024]{1,0:T(8,128)(2,1)S(1)}, bf16[64,1024]{1,0:T(8,128)(2,1)S(1)}, u32[]{:S(2)}, u32[]{:S(2)}) collective-permute-start(bf16[64,1024]{1,0:T(8,128)(2,1)S(1)} %fusion.32), channel_id=1, source_target_pairs={{16,0},{17,1},{18,2},{19,3},{20,4},{21,5},{22,6},{23,7},{24,8},{25... | collective-permute-start | bytes 393224 | tf_op jit(solution)/shard_map/ppermute | solution.py:21
  31.0 17.3 %collective-permute-start.5 = (bf16[2,64,1024]{2,1,0:T(8,128)(2,1)S(1)}, bf16[2,64,1024]{2,1,0:T(8,128)(2,1)S(1)}, u32[]{:S(2)}, u32[]{:S(2)}) collective-permute-start(bf16[2,64,1024]{2,1,0:T(8,128)(2,1)S(1)} %dynamic-slice_bitcast_fusion.2), channel_id=1, source_target_pairs={{16,17},{17,16},{18,19},{19,18},{20,21},{21,20},{22,23},{23,22},{2... | collective-permute-start | bytes 786440 | tf_op jit(solution)/shard_map/ppermute | solution.py:21
  31.7 15.0 %collective-permute-start.8 = (bf16[256,896]{1,0:T(8,128)(2,1)}, bf16[256,896]{1,0:T(8,128)(2,1)S(1)}, u32[]{:S(2)}, u32[]{:S(2)}) collective-permute-start(bf16[256,896]{1,0:T(8,128)(2,1)} %collective-permute-done.4), channel_id=1, source_target_pairs={{0,4},{1,5},{2,6},{3,7},{4,8},{5,9},{6,10},{7,11},{8,12},{9,13},{1... | collective-permute-start | bytes 1376264 | tf_op jit(solution)/shard_map/ppermute | solution.py:21
  47.4 27.3 %copy-start.2 = (bf16[64,1024]{1,0:T(8,128)(2,1)S(1)}, bf16[64,1024]{1,0:T(8,128)(2,1)}, u32[]{:S(2)}) copy-start(bf16[64,1024]{1,0:T(8,128)(2,1)} %get-tuple-element.4) | copy-start | bytes 393220
  47.4 29.6 %copy-start.1 = (bf16[64,1024]{1,0:T(8,128)(2,1)S(1)}, bf16[64,1024]{1,0:T(8,128)(2,1)}, u32[]{:S(2)}) copy-start(bf16[64,1024]{1,0:T(8,128)(2,1)} %get-tuple-element.5) | copy-start | bytes 393220
  47.5 1.7 %collective-permute-start.9 = (bf16[2,64,1024]{2,1,0:T(8,128)(2,1)S(1)}, bf16[2,64,1024]{2,1,0:T(8,128)(2,1)S(1)}, u32[]{:S(2)}, u32[]{:S(2)}) collective-permute-start(bf16[2,64,1024]{2,1,0:T(8,128)(2,1)S(1)} %dynamic-slice_bitcast_fusion.1), channel_id=1, source_target_pairs={{16,17},{17,16},{18,19},{19,18},{20,21},{21,20},{22,23},{23,22},{2... | collective-permute-start | bytes 786440 | tf_op jit(solution)/shard_map/ppermute | solution.py:21
  48.4 1.5 %collective-permute-start.6 = (bf16[1,64,1024]{2,1,0:T(8,128)(2,1)S(1)}, bf16[1,64,1024]{2,1,0:T(8,128)(2,1)S(1)}, u32[]{:S(2)}, u32[]{:S(2)}) collective-permute-start(bf16[1,64,1024]{2,1,0:T(8,128)(2,1)S(1)} %constant_dynamic-slice_fusion.2), channel_id=1, source_target_pairs={{16,18},{17,19},{18,16},{19,17},{20,22},{21,23},{22,20},{23,21},{2... | collective-permute-start | bytes 393224 | tf_op jit(solution)/shard_map/ppermute | solution.py:21
  49.1 14.0 %collective-permute-start.12 = (bf16[256,896]{1,0:T(8,128)(2,1)S(1)}, bf16[256,896]{1,0:T(8,128)(2,1)S(1)}, u32[]{:S(2)}, u32[]{:S(2)}) collective-permute-start(bf16[256,896]{1,0:T(8,128)(2,1)S(1)} %collective-permute-done.8), channel_id=1, source_target_pairs={{0,4},{1,5},{2,6},{3,7},{4,8},{5,9},{6,10},{7,11},{8,12},{9,13},{1... | collective-permute-start | bytes 1376264 | tf_op jit(solution)/shard_map/ppermute | solution.py:21
  49.2 2.0 %collective-permute-start.10 = (bf16[1,64,1024]{2,1,0:T(8,128)(2,1)S(1)}, bf16[1,64,1024]{2,1,0:T(8,128)(2,1)S(1)}, u32[]{:S(2)}, u32[]{:S(2)}) collective-permute-start(bf16[1,64,1024]{2,1,0:T(8,128)(2,1)S(1)} %constant_dynamic-slice_fusion.1), channel_id=1, source_target_pairs={{16,18},{17,19},{18,16},{19,17},{20,22},{21,23},{22,20},{23,21},{2... | collective-permute-start | bytes 393224 | tf_op jit(solution)/shard_map/ppermute | solution.py:21
  50.0 24.7 %collective-permute-start.7 = (bf16[64,1024]{1,0:T(8,128)(2,1)S(1)}, bf16[64,1024]{1,0:T(8,128)(2,1)S(1)}, u32[]{:S(2)}, u32[]{:S(2)}) collective-permute-start(bf16[64,1024]{1,0:T(8,128)(2,1)S(1)} %fusion.33), channel_id=1, source_target_pairs={{16,12},{17,13},{18,14},{19,15},{20,0},{21,1},{22,2},{23,3},{24,4}... | collective-permute-start | bytes 393224 | tf_op jit(solution)/shard_map/ppermute | solution.py:21
  51.3 32.0 %collective-permute-start.11 = (bf16[64,1024]{1,0:T(8,128)(2,1)S(1)}, bf16[64,1024]{1,0:T(8,128)(2,1)S(1)}, u32[]{:S(2)}, u32[]{:S(2)}) collective-permute-start(bf16[64,1024]{1,0:T(8,128)(2,1)S(1)} %fusion.34), channel_id=1, source_target_pairs={{16,8},{17,9},{18,10},{19,11},{20,12},{21,13},{22,14},{23,15},{24,... | collective-permute-start | bytes 393224 | tf_op jit(solution)/shard_map/ppermute | solution.py:21
  63.8 22.8 %collective-permute-start.13 = (bf16[2,64,1024]{2,1,0:T(8,128)(2,1)S(1)}, bf16[2,64,1024]{2,1,0:T(8,128)(2,1)S(1)}, u32[]{:S(2)}, u32[]{:S(2)}) collective-permute-start(bf16[2,64,1024]{2,1,0:T(8,128)(2,1)S(1)} %dynamic-slice_bitcast_fusion), channel_id=1, source_target_pairs={{16,17},{17,16},{18,19},{19,18},{20,21},{21,20},{22,23},{23,22},{2... | collective-permute-start | bytes 786440 | tf_op jit(solution)/shard_map/ppermute | solution.py:21
  74.7 9.9 %collective-permute-start.21 = (bf16[64,1024]{1,0:T(8,128)(2,1)S(1)}, bf16[64,1024]{1,0:T(8,128)(2,1)S(1)}, u32[]{:S(2)}, u32[]{:S(2)}) collective-permute-start(bf16[64,1024]{1,0:T(8,128)(2,1)S(1)} %copy-done.2), channel_id=1, source_target_pairs={{0,8},{1,9},{2,10},{3,11},{4,12},{5,13},{6,14},{7,15},{8,0},{9,1},... | collective-permute-start | bytes 393224 | tf_op jit(solution)/shard_map/ppermute | solution.py:21
  77.0 9.1 %collective-permute-start.24 = (bf16[64,1024]{1,0:T(8,128)(2,1)S(1)}, bf16[64,1024]{1,0:T(8,128)(2,1)S(1)}, u32[]{:S(2)}, u32[]{:S(2)}) collective-permute-start(bf16[64,1024]{1,0:T(8,128)(2,1)S(1)} %copy-done.1), channel_id=1, source_target_pairs={{0,12},{1,13},{2,14},{3,15},{4,0},{5,1},{6,2},{7,3},{8,4},{9,5},{1... | collective-permute-start | bytes 393224 | tf_op jit(solution)/shard_map/ppermute | solution.py:21
  84.6 5.6 %collective-permute-start.22 = (bf16[64,1024]{1,0:T(8,128)(2,1)S(1)}, bf16[64,1024]{1,0:T(8,128)(2,1)S(1)}, u32[]{:S(2)}, u32[]{:S(2)}) collective-permute-start(bf16[64,1024]{1,0:T(8,128)(2,1)S(1)} %collective-permute-done.21), channel_id=1, source_target_pairs={{0,2},{1,3},{2,0},{3,1},{4,6},{5,7},{6,4},{7,5},{8,10},{9,11},{10,... | collective-permute-start | bytes 393224 | tf_op jit(solution)/shard_map/ppermute | solution.py:21
  86.1 5.5 %collective-permute-start.25 = (bf16[64,1024]{1,0:T(8,128)(2,1)S(1)}, bf16[64,1024]{1,0:T(8,128)(2,1)S(1)}, u32[]{:S(2)}, u32[]{:S(2)}) collective-permute-start(bf16[64,1024]{1,0:T(8,128)(2,1)S(1)} %collective-permute-done.24), channel_id=1, source_target_pairs={{0,2},{1,3},{2,0},{3,1},{4,6},{5,7},{6,4},{7,5},{8,10},{9,11},{10,... | collective-permute-start | bytes 393224 | tf_op jit(solution)/shard_map/ppermute | solution.py:21
  86.7 5.6 %collective-permute-start.14 = (bf16[1,64,1024]{2,1,0:T(8,128)(2,1)S(1)}, bf16[1,64,1024]{2,1,0:T(8,128)(2,1)S(1)}, u32[]{:S(2)}, u32[]{:S(2)}) collective-permute-start(bf16[1,64,1024]{2,1,0:T(8,128)(2,1)S(1)} %constant_dynamic-slice_fusion), channel_id=1, source_target_pairs={{16,18},{17,19},{18,16},{19,17},{20,22},{21,23},{22,20},{23,21},{2... | collective-permute-start | bytes 393224 | tf_op jit(solution)/shard_map/ppermute | solution.py:21
  91.7 2.0 %collective-permute-start.23 = (bf16[2,64,1024]{2,1,0:T(8,128)(2,1)S(1)}, bf16[2,64,1024]{2,1,0:T(8,128)(2,1)S(1)}, u32[]{:S(2)}, u32[]{:S(2)}) collective-permute-start(bf16[2,64,1024]{2,1,0:T(8,128)(2,1)S(1)} %maximum_bitcast_fusion.2), channel_id=1, source_target_pairs={{0,1},{1,0},{2,3},{3,2},{4,5},{5,4},{6,7},{7,6},{8,9},{9,8},{10,11... | collective-permute-start | bytes 786440 | tf_op jit(solution)/shard_map/ppermute | solution.py:21
  91.8 2.1 %collective-permute-start.26 = (bf16[2,64,1024]{2,1,0:T(8,128)(2,1)S(1)}, bf16[2,64,1024]{2,1,0:T(8,128)(2,1)S(1)}, u32[]{:S(2)}, u32[]{:S(2)}) collective-permute-start(bf16[2,64,1024]{2,1,0:T(8,128)(2,1)S(1)} %maximum_bitcast_fusion.3), channel_id=1, source_target_pairs={{0,1},{1,0},{2,3},{3,2},{4,5},{5,4},{6,7},{7,6},{8,9},{9,8},{10,11... | collective-permute-start | bytes 786440 | tf_op jit(solution)/shard_map/ppermute | solution.py:21
  92.4 12.0 %collective-permute-start.15 = (bf16[64,1024]{1,0:T(8,128)(2,1)S(1)}, bf16[64,1024]{1,0:T(8,128)(2,1)S(1)}, u32[]{:S(2)}, u32[]{:S(2)}) collective-permute-start(bf16[64,1024]{1,0:T(8,128)(2,1)S(1)} %fusion.35), channel_id=1, source_target_pairs={{16,4},{17,5},{18,6},{19,7},{20,8},{21,9},{22,10},{23,11},{24,12},... | collective-permute-start | bytes 393224 | tf_op jit(solution)/shard_map/ppermute | solution.py:21

commit v2 on v0

v2 whole, which is shorter than its diff:
```python
import functools

import jax
import jax.numpy as jnp
from jax import lax
from jax.experimental import pallas as pl
from jax.experimental.pallas import tpu as pltpu
from jax.sharding import PartitionSpec as P

AXES = ("section", "dp", "tensor")
BF16 = jnp.bfloat16
F32 = jnp.float32
VMEM = pl.BlockSpec(memory_space=pltpu.VMEM)
HBM = pl.BlockSpec(memory_space=pltpu.HBM)
NT = (((1,), (1,)), ((), ()))
TN = (((0,), (0,)), ((), ()))
LANES = 128
START = 58


def moved(value, sizes, target):
    sections, replicas, shards = sizes
    pairs = []
    for s in range(sections):
        for r in range(replicas):
            for t in range(shards):
                to_s, to_r, to_t = target(s, r, t)
                pairs.append(
                    ((s * replicas + r) * shards + t, (to_s * replicas + to_r) * shards + to_t)
                )
    return lax.ppermute(value, AXES, pairs)


def together(*values):
    return lax.optimization_barrier(values)


def call(kernel, outputs, *arrays, limit=8, **more):
    options = dict(in_specs=[VMEM] * len(arrays), out_specs=[VMEM] * len(outputs))
    return pl.pallas_call(
        kernel,
        out_shape=[v if hasattr(v, "dtype") else jax.ShapeDtypeStruct(v, BF16) for v in outputs],
        compiler_params=pltpu.CompilerParams(vmem_limit_bytes=limit * 2**20),
        **{**options, **more},
    )(*arrays)


def added(a, b):
    return (a.astype(F32) + b.astype(F32)).astype(BF16)


def start_kernel(cut, shards, items, grad, gate, x, *refs):
    *outs, grad_here, gate_here, x_here, arrived, x_arrived = refs
    tokens, hidden = grad.shape
    replicas = len(x_here)
    width = x.shape[1] // replicas
    half = outs[0].shape[1]
    copies = []
    for shard in range(shards):
        here = pl.ds((2 * shard + cut) * half, half) if half % 16 == 0 else pl.ds(2 * shard * half, 2 * half)
        for i, (source, to) in enumerate(((grad, grad_here), (gate, gate_here))):
            copies.append(pltpu.make_async_copy(source.at[here], to.at[here], arrived.at[i, shard]))
            copies[-1].start()
    x_copies = {}
    for of in items:
        for device, _ in of:
            if device not in x_copies:
                block = lax.rem(lax.axis_index("dp") + device, replicas)
                columns = pl.ds(pl.multiple_of(block * width, width), width)
                x_copies[device] = pltpu.make_async_copy(x.at[:, columns], x_here[device], x_arrived.at[device])
                x_copies[device].start()
    at = outs[-1].shape[0] - hidden // LANES * shards
    for shard in range(shards):
        copies[2 * shard].wait()
        copies[2 * shard + 1].wait()
        here = pl.ds((2 * shard + cut) * half, half)
        for column in range(hidden // LANES):
            lanes = pl.ds(column * LANES, LANES)
            g = gate_here[here, lanes].astype(F32)
            value = grad_here[here, lanes].astype(F32) * g * (0.5 + 0.5 * jnp.tanh(0.5 * g))
            outs[-1][at + column * shards + shard] = value.astype(BF16)
    for copy in x_copies.values():
        copy.wait()
    for out, of in zip(outs, items):
        at = 0
        for device, cuts in of:
            for column in range(width // LANES):
                for c in cuts:
                    out[at] = x_here[device][c * half : (c + 1) * half, column * LANES : (column + 1) * LANES]
                    at += 1


def held_kernel(source, out, done):
    copy = pltpu.make_async_copy(source, out, done)
    copy.start()
    copy.wait()


def stack_kernel(places, *refs):
    *sources, out = refs
    for source, first, count, to, step in places:
        for i in range(count):
            out[to + i * step] = sources[source][first + i]


def product_kernel(shards, offsets, *refs):
    *pieces, w, keep, give = refs
    columns = w.shape[1] // LANES
    bit = lax.rem(lax.axis_index("tensor"), 2)
    left = [
        jnp.concatenate([piece[at + c * shards + 2 * m + start] for c in range(columns)], axis=1)
        for start in (bit, 1 - bit)
        for piece, at in zip(pieces, offsets)
        for m in range(shards // 2)
    ]
    out = lax.dot_general(jnp.concatenate(left), w[...], NT, preferred_element_type=F32).astype(BF16)
    rows = out.shape[0] // 2
    keep[...] = out[:rows].reshape(keep.shape)
    give[...] = out[rows:].reshape(give.shape)


def fold_kernel(step, *refs):
    *pairs, keep, give = refs
    bit = lax.rem(lax.div(lax.axis_index("tensor"), step), 2)
    at = 0
    for mine, got in zip(pairs[::2], pairs[1::2]):
        n, shards = mine.shape[:2]
        for i in range(n):
            for m in range(shards // 2):
                for to, start in ((keep, bit), (give, 1 - bit)):
                    to[at + i, m] = added(mine[i, 2 * m + start], got[i, 2 * m + start])
        at += n


def sum_kernel(mine, got, *outs):
    at = 0
    for out in outs:
        n = out.shape[0] // mine.shape[2]
        here = pl.ds(at, n)
        out[...] = added(mine[here], got[here]).reshape(out.shape)
        at += n


def weight_kernel(order, pairs, scale, xs, *refs):
    inputs, rest = refs[: 2 * xs], refs[2 * xs :]
    *rest, out, right = rest
    count = 1 + max(p[0] for p in pairs)
    parts, so_far = rest[:count], rest[count:]
    half = parts[0].shape[1]
    hidden = out.shape[1]
    shards = 2 * len(order)
    blocks = [(i, j, other) for other in (0, 1) for i, j in enumerate(order)]

    @pl.when(pl.program_id(0) == 0)
    def _():
        row = 0
        for part, at, _, _ in pairs:
            for _, j, other in blocks:
                shard = lax.axis_index("tensor") ^ j ^ other
                for c in range(hidden // LANES):
                    right[pl.ds(row, half), pl.ds(c * LANES, LANES)] = parts[part][at + c * shards + shard]
                row += half

    tile = out.shape[0]
    first = pl.program_id(0) * (tile // LANES)
    left = []
    for _, _, x, at in pairs:
        for i, _, other in blocks:
            block = inputs[2 * x + other]
            start = i * (block.shape[0] // len(order)) + at
            left.append(
                jnp.concatenate([block[start + 2 * (first + c)] for c in range(tile // LANES)], axis=1)
            )
    total = lax.dot_general(jnp.concatenate(left), right[...], TN, preferred_element_type=F32)
    for already in so_far:
        total += already[pl.ds(pl.multiple_of(pl.program_id(0) * tile, tile), tile)]
    out[...] = (total / scale).astype(out.dtype)


def passed_kernel(blocks, base, *refs):
    *pieces, out = refs
    width = pieces[0].shape[1]
    replicas = base.shape[1] // width
    sent = lax.axis_index("section") < lax.axis_size("section") - 1
    out[...] = jnp.where(sent, base[...], jnp.zeros(base.shape, BF16))
    for block, piece in zip(blocks, pieces):
        device = lax.rem(lax.axis_index("dp") + block, replicas)
        here = (slice(None), pl.ds(pl.multiple_of(device * width, width), width))
        out[here] = jnp.where(sent, added(base[here], piece[...]), jnp.zeros(piece.shape, BF16))


def last_kernel(base, piece, _, out, total, done):
    width = total.shape[1]
    replicas = base.shape[1] // width
    device = lax.rem(lax.axis_index("dp") + 1, replicas)
    columns = pl.ds(pl.multiple_of(device * width, width), width)
    sent = lax.axis_index("section") < lax.axis_size("section") - 1
    total[...] = jnp.where(sent, added(base[:, columns], piece[...]), jnp.zeros(piece.shape, BF16))
    copy = pltpu.make_async_copy(total, out.at[:, columns], done)
    copy.start()
    copy.wait()


def body(section_input, carried_grad, hidden_grad, saved_gate, w_up):
    sizes = tuple(lax.axis_size(a) for a in AXES)
    sections, replicas, shards = sizes
    grad, gate, x = hidden_grad[0, 0], saved_gate[0, 0], section_input[0, 0]
    w = w_up[0]
    width, hidden = w.shape
    tokens, rows = grad.shape[0], x.shape[0]
    half = rows // 2
    last, middle = replicas - 1, replicas // 2
    up_count, x_count = hidden // LANES * shards, width // LANES

    def up(value):
        return moved(value, sizes, lambda s, i, j: (s, (i + 1) % replicas, j))

    def down(value):
        return moved(value, sizes, lambda s, i, j: (s, (i - 1) % replicas, j))

    def returned(value, k):
        return moved(
            value,
            sizes,
            lambda s, i, j: (s - 1, (i - k) % replicas, j) if s else (sections - 1, i, j),
        )

    def across(value, step):
        return moved(value, sizes, lambda s, i, j: (s, i, j ^ step))

    def product(*pieces):
        share = (len(pieces), shards // 2, half, width)
        kernel = functools.partial(product_kernel, shards, [at for _, at in pieces])
        return call(kernel, [share, share], *[piece for piece, _ in pieces], w)

    def fold(step, *pairs):
        n, m = sum(v.shape[0] for v in pairs[::2]), pairs[0].shape[1]
        share = (n, m // 2, half, width)
        return call(functools.partial(fold_kernel, step), [share, share], *pairs)

    def finished(mine, got, *halves):
        step = 4
        while step < shards:
            mine, give = fold(step, mine, got)
            got = across(give, step)
            step *= 2
        return call(sum_kernel, [(n * half, width) for n in halves], mine, got)

    def stacked(count, places, *sources):
        return call(functools.partial(stack_kernel, places), [(count, half, LANES)], *sources)[0]

    def doubled(block, step, steps):
        for _ in range(steps):
            n = block.shape[0]
            places = [(i, 0, n, i * n, 1) for i in range(2)]
            block = stacked(2 * n, places, block, across(block, step))
            step //= 2
        return block

    far_step, steps = shards // 2, shards.bit_length() - 1
    order = [0]
    for i in range(steps - 1):
        order += [j + (far_step >> i) for j in order]

    def started(cut, *more):
        mine = [(d if cut == 0 else replicas - d, (0, 1)) for d in range(1, (replicas + 1) // 2)]
        if replicas % 2 == 0:
            mine.append((middle, (cut,)))
        items = [*more, mine]
        counts = [sum(x_count * len(cuts) for _, cuts in of) for of in items]
        counts[-1] += up_count
        return call(
            functools.partial(start_kernel, cut, shards, items),
            [(n, half, LANES) for n in counts],
            grad,
            gate,
            x,
            in_specs=[HBM] * 3,
            scratch_shapes=[pltpu.VMEM((tokens, hidden), BF16)] * 2
            + [[pltpu.VMEM((rows, width), BF16)] * replicas]
            + [pltpu.SemaphoreType.DMA((2, shards)), pltpu.SemaphoreType.DMA((replicas,))],
            limit=START,
        )

    tile = 256

    def weight_product(xs, pairs, parts, *so_far, final):
        kernel = functools.partial(weight_kernel, order, pairs, replicas if final else 1, len(xs))
        return call(
            kernel,
            [jax.ShapeDtypeStruct((width, hidden), BF16 if final else F32)],
            *[v for x in xs for v in x],
            *parts,
            *so_far,
            grid=(width // tile,),
            out_specs=[pl.BlockSpec((tile, hidden), lambda i: (i, 0))],
            scratch_shapes=[pltpu.VMEM((len(pairs) * shards * half, hidden), BF16)],
            limit=20,
        )[0]

    a = started(0)[0]
    a_next = up(a)
    x_own, b = started(1, [(0, (0, 1))])
    b_next = down(b)
    base = returned(carried_grad[0, 0], 0)
    w = call(held_kernel, [w.shape], w, in_specs=[HBM], scratch_shapes=[pltpu.SemaphoreType.DMA])[0]
    at = a.shape[0] - up_count
    a_parts, b_parts, ats = [a], [b], [at]
    keep, give = product((a, at), (b, at))
    keep, give = fold(2, keep, across(give, 1))
    out = finished(keep, across(give, 2), 2)[0]
    x_own = doubled(x_own, far_step, steps - 1)
    x_own = [x_own, across(x_own, 1)]

    a, b, base, out, *x_own = together(a_next, b_next, base, out, *x_own)
    a_parts.append(a)
    b_parts.append(b)
    ats.append(at)
    a_next, b_next = up(a[2 * x_count :]), down(b[2 * x_count :])
    zero = returned(out, 0)
    keep, give = product((a, at), (b, at))
    keep, give = fold(2, keep, across(give, 1))
    x_near = stacked(4 * x_count, [(i, 0, 2 * x_count, 2 * i * x_count, 1) for i in range(2)], a, b)
    x_near = doubled(x_near, far_step, steps - 1)

    at -= 2 * x_count
    a, b, keep, give, zero, x_near = together(a_next, b_next, keep, give, zero, x_near)
    a_parts.append(a)
    b_parts.append(b)
    ats.append(at)
    a_next, b_next = up(a[x_count:]), down(b[x_count:])
    nears = finished(keep, across(give, 2), 1, 1)
    keep, give = product((a, at), (b, at))
    keep, give = fold(2, keep, across(give, 1))
    x_far = stacked(2 * x_count, [(i, 0, x_count, i, 2) for i in range(2)], a, b)
    x_far = doubled(x_far, far_step, steps - 1)

    at -= x_count
    a, *nears = together(a_next, *nears)
    a_parts.append(a)
    ats.append(at)
    out = finished(keep, across(give, 2), 2)[0]
    keep_a, give_a = product((a, at))
    got_a = across(give_a, 1)
    b, keep_a, got_a, out, x_far = together(b_next, keep_a, got_a, out, x_far)
    b_parts.append(b)
    keep_b, give_b = product((b, at))
    x_near, x_far, give_b = together(x_near, x_far, give_b)
    keep, give = fold(2, keep_a, got_a, keep_b, across(give_b, 1))
    got = across(give, 2)
    out, _ = together(out, give)
    two = returned(out, 2)
    x_near, x_far = [x_near, across(x_near, 1)], [x_far, across(x_far, 1)]

    parts = [v for pair_of in zip(a_parts, b_parts) for v in pair_of]
    x_own[0], _ = together(x_own[0], give)
    weight_grad = weight_product(
        [x_own, x_near],
        [
            (0, ats[0], 0, 0),
            (1, ats[0], 0, 1),
            (2, ats[1], 1, 0),
            (3, ats[1], 1, 2 * x_count + 1),
        ],
        parts[:4],
        final=False,
    )
    keep, weight_grad = together(keep, weight_grad)
    out_a, out = finished(keep, got, 1, 1)
    above = returned(jnp.concatenate([out_a, nears[1]]), -1)
    below = returned(jnp.concatenate([nears[0], out]), 1)

    weight_grad, _ = together(weight_grad, out)
    weight_grad = weight_product(
        [x_near, x_far],
        [
            (0, ats[2], 1, 0),
            (1, ats[2], 1, 1),
            (2, ats[3], 0, 2 * x_count),
            (3, ats[3], 0, 1),
        ],
        parts[4:],
        weight_grad,
        final=True,
    )
    two, above, weight_grad = together(two, above, weight_grad)
    passed = call(
        functools.partial(passed_kernel, [0, 2, last]),
        [(rows, replicas * width)],
        base,
        zero,
        two,
        above,
    )[0]
    passed, below = together(passed, below)
    passed = call(
        last_kernel,
        [passed.shape],
        base,
        below,
        passed,
        in_specs=[VMEM] * 2 + [HBM],
        out_specs=[HBM],
        scratch_shapes=[pltpu.VMEM((rows, width), BF16), pltpu.SemaphoreType.DMA],
        input_output_aliases={2: 0},
    )[0]
    return passed[None, None], weight_grad[None]


def solution(mesh):
    return jax.shard_map(
        body,
        mesh=mesh,
        in_specs=(
            P("section", "dp", "tensor", None),
            P("section", "dp", "tensor", None),
            P("section", "dp", None, "tensor"),
            P("section", "dp", None, "tensor"),
            P("section", "dp", "tensor"),
        ),
        out_specs=(P("section", "dp", "tensor", None), P("section", "dp", "tensor")),
        check_vma=False,
    )
```

time: 193 us -> 83.3 us (0.43)
  waiting for transfers between devices: 141 us -> 34.2 us
  starting transfers between devices: 10.6 us -> 31.4 us
  Pallas kernels: 0 us -> 15.4 us
  between operations: 13.8 us -> 0.93 us
  local copies, waits for them, and re-layouts: 13.6 us -> 1.15 us
  matrix products: 10.7 us -> 0 us
  other arithmetic: 2.51 us -> 0.02 us
    all_gather x2 -> x0, waiting for transfers between devices: 64.3 us -> none  [the longest x1 44.7 us: body(): all_up_grads = lax.all_gather(up_grad, 'dp', axis=0, tiled=True)]
    all_to_all x2 -> x0, waiting for transfers between devices: 46.4 us -> none  [the longest x1 46.4 us: body(): lax.all_to_all(full_input, 'dp', split_axis=1, concat_axis=0, tiled=True)]
    ppermute x1 -> x26, waiting for transfers between devices: 0.01 us -> 34.2 us  [moved(): return lax.ppermute(value, AXES, pairs)]
    ppermute x1 -> x26, starting transfers between devices: 1.29 us -> 31.4 us  [moved(): return lax.ppermute(value, AXES, pairs)]
    reduce_scatter x1 -> x0, waiting for transfers between devices: 29.7 us -> none  [body(): lax.psum_scatter(jnp.einsum('rtf,df->trd', shaped, up_weight, preferred_e...]
    pallas_call x0 -> x25, Pallas kernels: none -> 15.4 us  [call(): pl.pallas_call(kernel, out_shape=[v if hasattr(v, 'dtype') else jax.Shape...]
    dot_general x2 -> x0, matrix products: 10.7 us -> none  [the longest x1 5.46 us: body(): lax.dot_general(input_columns, all_up_grads, (((0,), (0,)), ((), ())), pr...]
    all_to_all x2 -> x0, starting transfers between devices: 9.19 us -> none  [the longest x1 4.6 us: body(): lax.all_to_all(full_input, 'dp', split_axis=1, concat_axis=0, tiled=True)]
  transfers between devices with their start and end apart: 6 -> 26, of which waited for: 4 -> 11; matrix products, arithmetic and copies ran while one was open for 9% -> 0% of each run, Pallas kernels for 0% -> 16%
where the time goes in v2:
time: 83.3 us; the launch traced here: 83.1 us
  waiting for transfers between devices  34.2 us (41%)
  starting transfers between devices  31.4 us (38%)
  Pallas kernels  15.4 us (18%)
  local copies, waits for them, and re-layouts  1.15 us (1%)
  between operations  0.93 us (1%)
    ppermute x26, waiting for transfers between devices, moved(): return lax.ppermute(value, AXES, pairs)  34.2 us
    ppermute x26, starting transfers between devices, moved(): return lax.ppermute(value, AXES, pairs)  31.4 us
    pallas_call x25, Pallas kernels, call(): pl.pallas_call(kernel, out_shape=[v if hasattr(v, 'dtype') else jax.Shape...  15.4 us
  transfers between devices with their start and end apart: 26, of which 11 were waited for; matrix products, arithmetic and copies ran while one was open for 0% of the time, Pallas kernels for 16%

profile of v2, /device:TPU:0, one launch (start us, length us, event | category | flops | bytes accessed | tf_op | source)
XLA Modules:
  0.0 83.1 jit_solution(17141425446549917638)
XLA Ops:
  0.6 3.0 %collective-permute-start.2 = (bf16[64,4096]{1,0:T(8,128)(2,1)}, bf16[64,4096]{1,0:T(8,128)(2,1)S(1)}, u32[]{:S(2)}, u32[]{:S(2)}) collective-permute-start(bf16[64,4096]{1,0:T(8,128)(2,1)} %bitcast.16), channel_id=1, source_target_pairs={{0,16},{1,17},{2,18},{3,19},{4,20},{5,21},{6,22},{7,23},{8,24},{9,... | collective-permute-start | bytes 1572872 | tf_op jit(solution)/shard_map/ppermute | solution.py:31
  3.6 2.1 %shard_map.68.refs_0_.refs_4_ = bf16[52,32,128]{2,1,0:T(8,128)(2,1)} custom-call(bf16[256,896]{1,0:T(8,128)(2,1)} %bitcast.11, bf16[256,896]{1,0:T(8,128)(2,1)} %bitcast.13, bf16[64,4096]{1,0:T(8,128)(2,1)} %bitcast.8), custom_call_target="tpu_custom_call" | custom-call | tf_op jit(solution)/shard_map/pallas_call | solution.py:40
  5.8 1.6 %collective-permute-start = (bf16[52,32,128]{2,1,0:T(8,128)(2,1)}, bf16[52,32,128]{2,1,0:T(8,128)(2,1)S(1)}, u32[]{:S(2)}, u32[]{:S(2)}) collective-permute-start(bf16[52,32,128]{2,1,0:T(8,128)(2,1)} %shard_map.68.refs_0_.refs_4_), channel_id=1, source_target_pairs={{0,4},{1,5},{2,6},{3,7},{4,8},{5,9},{6,10},{7,11},{8,12},{9,13},{1... | collective-permute-start | bytes 1277960 | tf_op jit(solution)/shard_map/ppermute | solution.py:31
  7.4 2.2 %shard_map.69 = (bf16[16,32,128]{2,1,0:T(8,128)(2,1)}, bf16[52,32,128]{2,1,0:T(8,128)(2,1)}) custom-call(bf16[256,896]{1,0:T(8,128)(2,1)} %bitcast.12, bf16[256,896]{1,0:T(8,128)(2,1)} %bitcast.14, bf16[64,4096]{1,0:T(8,128)(2,1)} %bitcast.9), custom_call_target="tpu_custom_call" | custom-call | tf_op jit(solution)/shard_map/pallas_call | solution.py:40
  9.6 2.3 %collective-permute-start.1 = (bf16[52,32,128]{2,1,0:T(8,128)(2,1)}, bf16[52,32,128]{2,1,0:T(8,128)(2,1)S(1)}, u32[]{:S(2)}, u32[]{:S(2)}) collective-permute-start(bf16[52,32,128]{2,1,0:T(8,128)(2,1)} %get-tuple-element.59.refs_1_.refs_5_), channel_id=1, source_target_pairs={{0,12},{1,13},{2,14},{3,15},{4,0},{5,1},{6,2},{7,3},{8,4},{9,5},{1... | collective-permute-start | bytes 1277960 | tf_op jit(solution)/shard_map/ppermute | solution.py:31
  12.0 0.9 %copy-done = bf16[52,32,128]{2,1,0:T(8,128)(2,1)S(1)} copy-done((bf16[52,32,128]{2,1,0:T(8,128)(2,1)S(1)}, bf16[52,32,128]{2,1,0:T(8,128)(2,1)}, u32[]{:S(2)}) %copy-start) | copy-done | bytes 426008
  13.0 0.7 shard_map.71
  13.9 1.5 %collective-permute-start.5 = (bf16[16,32,128]{2,1,0:T(8,128)(2,1)S(1)}, bf16[16,32,128]{2,1,0:T(8,128)(2,1)S(1)}, u32[]{:S(2)}, u32[]{:S(2)}) collective-permute-start(bf16[16,32,128]{2,1,0:T(8,128)(2,1)S(1)} %copy-done.3), channel_id=1, source_target_pairs={{0,2},{1,3},{2,0},{3,1},{4,6},{5,7},{6,4},{7,5},{8,10},{9,11},{10,... | collective-permute-start | bytes 393224 | tf_op jit(solution)/shard_map/ppermute | solution.py:31
  15.5 4.3 %collective-permute-done.5.refs_1_ = bf16[16,32,128]{2,1,0:T(8,128)(2,1)S(1)} collective-permute-done((bf16[16,32,128]{2,1,0:T(8,128)(2,1)S(1)}, bf16[16,32,128]{2,1,0:T(8,128)(2,1)S(1)}, u32[]{:S(2)}, u32[]{:S(2)}) %collective-permute-start.5) | collective-permute-done | bytes 131104 | tf_op jit(solution)/shard_map/ppermute | solution.py:31
  20.0 1.6 %collective-permute-start.4 = (bf16[2,1,32,1024]{3,2,1,0:T(8,128)(2,1)S(1)}, bf16[2,1,32,1024]{3,2,1,0:T(8,128)(2,1)S(1)}, u32[]{:S(2)}, u32[]{:S(2)}) collective-permute-start(bf16[2,1,32,1024]{3,2,1,0:T(8,128)(2,1)S(1)} %get-tuple-element.63), channel_id=1, source_target_pairs={{0,2},{1,3},{2,0},{3,1},{4,6},{5,7},{6,4},{7,5},{8,10},{9,11},{10,... | collective-permute-start | bytes 393224 | tf_op jit(solution)/shard_map/ppermute | solution.py:31
  21.6 4.4 %collective-permute-done.4.got = bf16[2,1,32,1024]{3,2,1,0:T(8,128)(2,1)S(1)} collective-permute-done((bf16[2,1,32,1024]{3,2,1,0:T(8,128)(2,1)S(1)}, bf16[2,1,32,1024]{3,2,1,0:T(8,128)(2,1)S(1)}, u32[]{:S(2)}, u32[]{:S(2)}) %collective-permute-start.4) | collective-permute-done | bytes 131104 | tf_op jit(solution)/shard_map/ppermute | solution.py:31
  26.0 2.3 %collective-permute-done.1.refs_1_.refs_7_ = bf16[52,32,128]{2,1,0:T(8,128)(2,1)S(1)} collective-permute-done((bf16[52,32,128]{2,1,0:T(8,128)(2,1)}, bf16[52,32,128]{2,1,0:T(8,128)(2,1)S(1)}, u32[]{:S(2)}, u32[]{:S(2)}) %collective-permute-start.1) | collective-permute-done | bytes 426016 | tf_op jit(solution)/shard_map/ppermute | solution.py:31
  29.0 3.3 %collective-permute-start.8 = (bf16[36,32,128]{2,1,0:T(8,128)(2,1)S(1)}, bf16[36,32,128]{2,1,0:T(8,128)(2,1)S(1)}, u32[]{:S(2)}, u32[]{:S(2)}) collective-permute-start(bf16[36,32,128]{2,1,0:T(8,128)(2,1)S(1)} %slice.13), channel_id=1, source_target_pairs={{0,12},{1,13},{2,14},{3,15},{4,0},{5,1},{6,2},{7,3},{8,4},{9,5},{1... | collective-permute-start | bytes 884744 | tf_op jit(solution)/shard_map/ppermute | solution.py:31
  32.3 0.7 shard_map.75
  33.0 1.6 %collective-permute-start.11 = (bf16[32,32,128]{2,1,0:T(8,128)(2,1)S(1)}, bf16[32,32,128]{2,1,0:T(8,128)(2,1)S(1)}, u32[]{:S(2)}, u32[]{:S(2)}) collective-permute-start(bf16[32,32,128]{2,1,0:T(8,128)(2,1)S(1)} %shard_map.77.refs_0_), channel_id=1, source_target_pairs={{0,2},{1,3},{2,0},{3,1},{4,6},{5,7},{6,4},{7,5},{8,10},{9,11},{10,... | collective-permute-start | bytes 786440 | tf_op jit(solution)/shard_map/ppermute | solution.py:31
  35.3 5.4 %collective-permute-done.11.refs_1_ = bf16[32,32,128]{2,1,0:T(8,128)(2,1)S(1)} collective-permute-done((bf16[32,32,128]{2,1,0:T(8,128)(2,1)S(1)}, bf16[32,32,128]{2,1,0:T(8,128)(2,1)S(1)}, u32[]{:S(2)}, u32[]{:S(2)}) %collective-permute-start.11) | collective-permute-done | bytes 262176 | tf_op jit(solution)/shard_map/ppermute | solution.py:31
  40.9 3.1 %collective-permute-done.8.refs_1_.refs_5_ = bf16[36,32,128]{2,1,0:T(8,128)(2,1)S(1)} collective-permute-done((bf16[36,32,128]{2,1,0:T(8,128)(2,1)S(1)}, bf16[36,32,128]{2,1,0:T(8,128)(2,1)S(1)}, u32[]{:S(2)}, u32[]{:S(2)}) %collective-permute-start.8) | collective-permute-done | bytes 294944 | tf_op jit(solution)/shard_map/ppermute | solution.py:31
  44.0 0.7 shard_map.81
  45.2 1.5 %collective-permute-start.14 = (bf16[2,1,32,1024]{3,2,1,0:T(8,128)(2,1)S(1)}, bf16[2,1,32,1024]{3,2,1,0:T(8,128)(2,1)S(1)}, u32[]{:S(2)}, u32[]{:S(2)}) collective-permute-start(bf16[2,1,32,1024]{3,2,1,0:T(8,128)(2,1)S(1)} %get-tuple-element.77), channel_id=1, source_target_pairs={{0,2},{1,3},{2,0},{3,1},{4,6},{5,7},{6,4},{7,5},{8,10},{9,11},{10,... | collective-permute-start | bytes 393224 | tf_op jit(solution)/shard_map/ppermute | solution.py:31
  46.7 3.6 %collective-permute-start.12 = (bf16[28,32,128]{2,1,0:T(8,128)(2,1)S(1)}, bf16[28,32,128]{2,1,0:T(8,128)(2,1)S(1)}, u32[]{:S(2)}, u32[]{:S(2)}) collective-permute-start(bf16[28,32,128]{2,1,0:T(8,128)(2,1)S(1)} %slice.14), channel_id=1, source_target_pairs={{0,12},{1,13},{2,14},{3,15},{4,0},{5,1},{6,2},{7,3},{8,4},{9,5},{1... | collective-permute-start | bytes 688136 | tf_op jit(solution)/shard_map/ppermute | solution.py:31
  50.9 4.2 %collective-permute-done.13.refs_0_.refs_6_ = bf16[28,32,128]{2,1,0:T(8,128)(2,1)S(1)} collective-permute-done((bf16[28,32,128]{2,1,0:T(8,128)(2,1)S(1)}, bf16[28,32,128]{2,1,0:T(8,128)(2,1)S(1)}, u32[]{:S(2)}, u32[]{:S(2)}) %collective-permute-start.13) | collective-permute-done | bytes 229408 | tf_op jit(solution)/shard_map/ppermute | solution.py:31
  55.2 1.6 %collective-permute-start.17 = (bf16[2,1,32,1024]{3,2,1,0:T(8,128)(2,1)S(1)}, bf16[2,1,32,1024]{3,2,1,0:T(8,128)(2,1)S(1)}, u32[]{:S(2)}, u32[]{:S(2)}) collective-permute-start(bf16[2,1,32,1024]{3,2,1,0:T(8,128)(2,1)S(1)} %get-tuple-element.86), channel_id=1, source_target_pairs={{0,2},{1,3},{2,0},{3,1},{4,6},{5,7},{6,4},{7,5},{8,10},{9,11},{10,... | collective-permute-start | bytes 393224 | tf_op jit(solution)/shard_map/ppermute | solution.py:31
  57.6 2.6 %collective-permute-done.17.got = bf16[2,1,32,1024]{3,2,1,0:T(8,128)(2,1)S(1)} collective-permute-done((bf16[2,1,32,1024]{3,2,1,0:T(8,128)(2,1)S(1)}, bf16[2,1,32,1024]{3,2,1,0:T(8,128)(2,1)S(1)}, u32[]{:S(2)}, u32[]{:S(2)}) %collective-permute-start.17) | collective-permute-done | bytes 131104 | tf_op jit(solution)/shard_map/ppermute | solution.py:31
  61.6 1.6 %collective-permute-done.19.refs_3_ = bf16[1,2,32,1024]{3,2,1,0:T(8,128)(2,1)S(1)} collective-permute-done((bf16[1,2,32,1024]{3,2,1,0:T(8,128)(2,1)S(1)}, bf16[1,2,32,1024]{3,2,1,0:T(8,128)(2,1)S(1)}, u32[]{:S(2)}, u32[]{:S(2)}) %collective-permute-start.19) | collective-permute-done | bytes 131104 | tf_op jit(solution)/shard_map/ppermute | solution.py:31
  63.2 1.6 %collective-permute-start.22 = (bf16[2,1,32,1024]{3,2,1,0:T(8,128)(2,1)S(1)}, bf16[2,1,32,1024]{3,2,1,0:T(8,128)(2,1)S(1)}, u32[]{:S(2)}, u32[]{:S(2)}) collective-permute-start(bf16[2,1,32,1024]{3,2,1,0:T(8,128)(2,1)S(1)} %get-tuple-element.96), channel_id=1, source_target_pairs={{0,2},{1,3},{2,0},{3,1},{4,6},{5,7},{6,4},{7,5},{8,10},{9,11},{10,... | collective-permute-start | bytes 393224 | tf_op jit(solution)/shard_map/ppermute | solution.py:31
  65.5 2.0 %shard_map.88.refs_8_ = f32[1024,896]{1,0:T(8,128)S(1)} custom-call(bf16[32,32,128]{2,1,0:T(8,128)(2,1)S(1)} %shard_map.74.refs_0_, bf16[32,32,128]{2,1,0:T(8,128)(2,1)S(1)} %collective-permute-done.6.refs_1_, bf16[64,32,128]{2,1,0:T(8,128)(2,1)S(1)} %shard_map.78.refs_2_.refs_0_, bf16[64,32,128]{2,1,0:T(8,128)(2,1)S(1)} %collective-permute-done.21.refs_3_.refs_1_, ...), custom_call_target="tpu_custom_call" | custom-call | tf_op jit(solution)/shard_map/pallas_call | solution.py:40
  67.6 1.3 %collective-permute-done.22.got = bf16[2,1,32,1024]{3,2,1,0:T(8,128)(2,1)S(1)} collective-permute-done((bf16[2,1,32,1024]{3,2,1,0:T(8,128)(2,1)S(1)}, bf16[2,1,32,1024]{3,2,1,0:T(8,128)(2,1)S(1)}, u32[]{:S(2)}, u32[]{:S(2)}) %collective-permute-start.22) | collective-permute-done | bytes 131104 | tf_op jit(solution)/shard_map/ppermute | solution.py:31
  68.9 4.4 %collective-permute-start.23 = (bf16[64,1024]{1,0:T(8,128)(2,1)S(1)}, bf16[64,1024]{1,0:T(8,128)(2,1)S(1)}, u32[]{:S(2)}, u32[]{:S(2)}) collective-permute-start(bf16[64,1024]{1,0:T(8,128)(2,1)S(1)} %pad_maximum_fusion), channel_id=1, source_target_pairs={{0,16},{1,17},{2,18},{3,19},{4,20},{5,21},{6,22},{7,23},{8,24},{9,... | collective-permute-start | bytes 393224 | tf_op jit(solution)/shard_map/ppermute | solution.py:31
  73.4 3.1 %shard_map.90 = bf16[1024,896]{1,0:T(8,128)(2,1)} custom-call(bf16[64,32,128]{2,1,0:T(8,128)(2,1)S(1)} %shard_map.78.refs_2_.refs_0_, bf16[64,32,128]{2,1,0:T(8,128)(2,1)S(1)} %collective-permute-done.21.refs_3_.refs_1_, bf16[32,32,128]{2,1,0:T(8,128)(2,1)S(1)} %shard_map.85.refs_2_, bf16[32,32,128]{2,1,0:T(8,128)(2,1)S(1)} %collective-permute-done.24.refs_3_, ...), custom_call_target="tpu_custom_call" | custom-call | tf_op jit(solution)/shard_map/pallas_call | solution.py:40
  76.5 3.3 %collective-permute-done.20.refs_1_ = bf16[64,1024]{1,0:T(8,128)(2,1)S(1)} collective-permute-done((bf16[64,1024]{1,0:T(8,128)(2,1)S(1)}, bf16[64,1024]{1,0:T(8,128)(2,1)S(1)}, u32[]{:S(2)}, u32[]{:S(2)}) %collective-permute-start.20) | collective-permute-done | bytes 131104 | tf_op jit(solution)/shard_map/ppermute | solution.py:31
  79.8 0.9 %shard_map.91._ = bf16[64,4096]{1,0:T(8,128)(2,1)} custom-call(bf16[64,4096]{1,0:T(8,128)(2,1)S(1)} %collective-permute-done.2.base, bf16[64,1024]{1,0:T(8,128)(2,1)S(1)} %collective-permute-done.10.refs_0_, bf16[64,1024]{1,0:T(8,128)(2,1)S(1)} %collective-permute-done.20.refs_1_, bf16[64,1024]{1,0:T(8,128)(2,1)S(1)} %collective-permute-done.23.refs_2_), custom_call_target="tpu_custom_call" | custom-call | tf_op jit(solution)/shard_map/pallas_call | solution.py:40
  80.8 1.6 %collective-permute-done.25.piece = bf16[64,1024]{1,0:T(8,128)(2,1)S(1)} collective-permute-done((bf16[64,1024]{1,0:T(8,128)(2,1)S(1)}, bf16[64,1024]{1,0:T(8,128)(2,1)S(1)}, u32[]{:S(2)}, u32[]{:S(2)}) %collective-permute-start.25) | collective-permute-done | bytes 131104 | tf_op jit(solution)/shard_map/ppermute | solution.py:31
  (59 shorter events, 7.0 us)
Async XLA Ops:
  0.6 11.3 %copy-start.1 = (bf16[1,1024,896]{2,1,0:T(8,128)(2,1)S(1)}, bf16[1,1024,896]{2,1,0:T(8,128)(2,1)}, u32[]{:S(2)}) copy-start(bf16[1,1024,896]{2,1,0:T(8,128)(2,1)} %param.9) | copy-start | bytes 5505028
  0.6 27.6 %collective-permute-start.2 = (bf16[64,4096]{1,0:T(8,128)(2,1)}, bf16[64,4096]{1,0:T(8,128)(2,1)S(1)}, u32[]{:S(2)}, u32[]{:S(2)}) collective-permute-start(bf16[64,4096]{1,0:T(8,128)(2,1)} %bitcast.16), channel_id=1, source_target_pairs={{0,16},{1,17},{2,18},{3,19},{4,20},{5,21},{6,22},{7,23},{8,24},{9,... | collective-permute-start | bytes 1572872 | tf_op jit(solution)/shard_map/ppermute | solution.py:31
  5.8 20.2 %collective-permute-start = (bf16[52,32,128]{2,1,0:T(8,128)(2,1)}, bf16[52,32,128]{2,1,0:T(8,128)(2,1)S(1)}, u32[]{:S(2)}, u32[]{:S(2)}) collective-permute-start(bf16[52,32,128]{2,1,0:T(8,128)(2,1)} %shard_map.68.refs_0_.refs_4_), channel_id=1, source_target_pairs={{0,4},{1,5},{2,6},{3,7},{4,8},{5,9},{6,10},{7,11},{8,12},{9,13},{1... | collective-permute-start | bytes 1277960 | tf_op jit(solution)/shard_map/ppermute | solution.py:31
  9.6 18.7 %collective-permute-start.1 = (bf16[52,32,128]{2,1,0:T(8,128)(2,1)}, bf16[52,32,128]{2,1,0:T(8,128)(2,1)S(1)}, u32[]{:S(2)}, u32[]{:S(2)}) collective-permute-start(bf16[52,32,128]{2,1,0:T(8,128)(2,1)} %get-tuple-element.59.refs_1_.refs_5_), channel_id=1, source_target_pairs={{0,12},{1,13},{2,14},{3,15},{4,0},{5,1},{6,2},{7,3},{8,4},{9,5},{1... | collective-permute-start | bytes 1277960 | tf_op jit(solution)/shard_map/ppermute | solution.py:31
  11.9 1.0 %copy-start = (bf16[52,32,128]{2,1,0:T(8,128)(2,1)S(1)}, bf16[52,32,128]{2,1,0:T(8,128)(2,1)}, u32[]{:S(2)}) copy-start(bf16[52,32,128]{2,1,0:T(8,128)(2,1)} %shard_map.68.refs_0_.refs_4_) | copy-start | bytes 1277956
  11.9 1.1 %copy-start.2 = (bf16[52,32,128]{2,1,0:T(8,128)(2,1)S(1)}, bf16[52,32,128]{2,1,0:T(8,128)(2,1)}, u32[]{:S(2)}) copy-start(bf16[52,32,128]{2,1,0:T(8,128)(2,1)} %get-tuple-element.59.refs_1_.refs_5_) | copy-start | bytes 1277956
  13.0 0.9 %copy-start.3 = (bf16[16,32,128]{2,1,0:T(8,128)(2,1)S(1)}, bf16[16,32,128]{2,1,0:T(8,128)(2,1)}, u32[]{:S(2)}) copy-start(bf16[16,32,128]{2,1,0:T(8,128)(2,1)} %get-tuple-element.64.refs_0_) | copy-start | bytes 393220
  13.8 6.1 %collective-permute-start.3 = (bf16[2,2,32,1024]{3,2,1,0:T(8,128)(2,1)S(1)}, bf16[2,2,32,1024]{3,2,1,0:T(8,128)(2,1)S(1)}, u32[]{:S(2)}, u32[]{:S(2)}) collective-permute-start(bf16[2,2,32,1024]{3,2,1,0:T(8,128)(2,1)S(1)} %get-tuple-element.61), channel_id=1, source_target_pairs={{0,1},{1,0},{2,3},{3,2},{4,5},{5,4},{6,7},{7,6},{8,9},{9,8},{10,11... | collective-permute-start | bytes 786440 | tf_op jit(solution)/shard_map/ppermute | solution.py:31
  13.9 5.8 %collective-permute-start.5 = (bf16[16,32,128]{2,1,0:T(8,128)(2,1)S(1)}, bf16[16,32,128]{2,1,0:T(8,128)(2,1)S(1)}, u32[]{:S(2)}, u32[]{:S(2)}) collective-permute-start(bf16[16,32,128]{2,1,0:T(8,128)(2,1)S(1)} %copy-done.3), channel_id=1, source_target_pairs={{0,2},{1,3},{2,0},{3,1},{4,6},{5,7},{6,4},{7,5},{8,10},{9,11},{10,... | collective-permute-start | bytes 393224 | tf_op jit(solution)/shard_map/ppermute | solution.py:31
  19.8 6.2 %collective-permute-start.6 = (bf16[32,32,128]{2,1,0:T(8,128)(2,1)S(1)}, bf16[32,32,128]{2,1,0:T(8,128)(2,1)S(1)}, u32[]{:S(2)}, u32[]{:S(2)}) collective-permute-start(bf16[32,32,128]{2,1,0:T(8,128)(2,1)S(1)} %shard_map.74.refs_0_), channel_id=1, source_target_pairs={{0,1},{1,0},{2,3},{3,2},{4,5},{5,4},{6,7},{7,6},{8,9},{9,8},{10,11... | collective-permute-start | bytes 786440 | tf_op jit(solution)/shard_map/ppermute | solution.py:31
  20.0 5.9 %collective-permute-start.4 = (bf16[2,1,32,1024]{3,2,1,0:T(8,128)(2,1)S(1)}, bf16[2,1,32,1024]{3,2,1,0:T(8,128)(2,1)S(1)}, u32[]{:S(2)}, u32[]{:S(2)}) collective-permute-start(bf16[2,1,32,1024]{3,2,1,0:T(8,128)(2,1)S(1)} %get-tuple-element.63), channel_id=1, source_target_pairs={{0,2},{1,3},{2,0},{3,1},{4,6},{5,7},{6,4},{7,5},{8,10},{9,11},{10,... | collective-permute-start | bytes 393224 | tf_op jit(solution)/shard_map/ppermute | solution.py:31
  28.3 12.6 %collective-permute-start.7 = (bf16[36,32,128]{2,1,0:T(8,128)(2,1)S(1)}, bf16[36,32,128]{2,1,0:T(8,128)(2,1)S(1)}, u32[]{:S(2)}, u32[]{:S(2)}) collective-permute-start(bf16[36,32,128]{2,1,0:T(8,128)(2,1)S(1)} %slice.12), channel_id=1, source_target_pairs={{0,4},{1,5},{2,6},{3,7},{4,8},{5,9},{6,10},{7,11},{8,12},{9,13},{1... | collective-permute-start | bytes 884744 | tf_op jit(solution)/shard_map/ppermute | solution.py:31
  29.0 15.0 %collective-permute-start.8 = (bf16[36,32,128]{2,1,0:T(8,128)(2,1)S(1)}, bf16[36,32,128]{2,1,0:T(8,128)(2,1)S(1)}, u32[]{:S(2)}, u32[]{:S(2)}) collective-permute-start(bf16[36,32,128]{2,1,0:T(8,128)(2,1)S(1)} %slice.13), channel_id=1, source_target_pairs={{0,12},{1,13},{2,14},{3,15},{4,0},{5,1},{6,2},{7,3},{8,4},{9,5},{1... | collective-permute-start | bytes 884744 | tf_op jit(solution)/shard_map/ppermute | solution.py:31
  33.0 7.7 %collective-permute-start.11 = (bf16[32,32,128]{2,1,0:T(8,128)(2,1)S(1)}, bf16[32,32,128]{2,1,0:T(8,128)(2,1)S(1)}, u32[]{:S(2)}, u32[]{:S(2)}) collective-permute-start(bf16[32,32,128]{2,1,0:T(8,128)(2,1)S(1)} %shard_map.77.refs_0_), channel_id=1, source_target_pairs={{0,2},{1,3},{2,0},{3,1},{4,6},{5,7},{6,4},{7,5},{8,10},{9,11},{10,... | collective-permute-start | bytes 786440 | tf_op jit(solution)/shard_map/ppermute | solution.py:31
  34.6 6.2 %collective-permute-start.9 = (bf16[2,2,32,1024]{3,2,1,0:T(8,128)(2,1)S(1)}, bf16[2,2,32,1024]{3,2,1,0:T(8,128)(2,1)S(1)}, u32[]{:S(2)}, u32[]{:S(2)}) collective-permute-start(bf16[2,2,32,1024]{3,2,1,0:T(8,128)(2,1)S(1)} %get-tuple-element.69), channel_id=1, source_target_pairs={{0,1},{1,0},{2,3},{3,2},{4,5},{5,4},{6,7},{7,6},{8,9},{9,8},{10,11... | collective-permute-start | bytes 786440 | tf_op jit(solution)/shard_map/ppermute | solution.py:31
  34.6 6.3 %collective-permute-start.10 = (bf16[64,1024]{1,0:T(8,128)(2,1)S(1)}, bf16[64,1024]{1,0:T(8,128)(2,1)S(1)}, u32[]{:S(2)}, u32[]{:S(2)}) collective-permute-start(bf16[64,1024]{1,0:T(8,128)(2,1)S(1)} %shard_map.73), channel_id=1, source_target_pairs={{0,16},{1,17},{2,18},{3,19},{4,20},{5,21},{6,22},{7,23},{8,24},{9,... | collective-permute-start | bytes 393224 | tf_op jit(solution)/shard_map/ppermute | solution.py:31
  44.7 10.4 %collective-permute-start.16 = (bf16[2,2,32,1024]{3,2,1,0:T(8,128)(2,1)S(1)}, bf16[2,2,32,1024]{3,2,1,0:T(8,128)(2,1)S(1)}, u32[]{:S(2)}, u32[]{:S(2)}) collective-permute-start(bf16[2,2,32,1024]{3,2,1,0:T(8,128)(2,1)S(1)} %get-tuple-element.84), channel_id=1, source_target_pairs={{0,1},{1,0},{2,3},{3,2},{4,5},{5,4},{6,7},{7,6},{8,9},{9,8},{10,11... | collective-permute-start | bytes 786440 | tf_op jit(solution)/shard_map/ppermute | solution.py:31
  44.8 10.3 %collective-permute-start.13 = (bf16[28,32,128]{2,1,0:T(8,128)(2,1)S(1)}, bf16[28,32,128]{2,1,0:T(8,128)(2,1)S(1)}, u32[]{:S(2)}, u32[]{:S(2)}) collective-permute-start(bf16[28,32,128]{2,1,0:T(8,128)(2,1)S(1)} %slice.15), channel_id=1, source_target_pairs={{0,4},{1,5},{2,6},{3,7},{4,8},{5,9},{6,10},{7,11},{8,12},{9,13},{1... | collective-permute-start | bytes 688136 | tf_op jit(solution)/shard_map/ppermute | solution.py:31
  45.2 5.7 %collective-permute-start.14 = (bf16[2,1,32,1024]{3,2,1,0:T(8,128)(2,1)S(1)}, bf16[2,1,32,1024]{3,2,1,0:T(8,128)(2,1)S(1)}, u32[]{:S(2)}, u32[]{:S(2)}) collective-permute-start(bf16[2,1,32,1024]{3,2,1,0:T(8,128)(2,1)S(1)} %get-tuple-element.77), channel_id=1, source_target_pairs={{0,2},{1,3},{2,0},{3,1},{4,6},{5,7},{6,4},{7,5},{8,10},{9,11},{10,... | collective-permute-start | bytes 393224 | tf_op jit(solution)/shard_map/ppermute | solution.py:31
  46.7 13.5 %collective-permute-start.12 = (bf16[28,32,128]{2,1,0:T(8,128)(2,1)S(1)}, bf16[28,32,128]{2,1,0:T(8,128)(2,1)S(1)}, u32[]{:S(2)}, u32[]{:S(2)}) collective-permute-start(bf16[28,32,128]{2,1,0:T(8,128)(2,1)S(1)} %slice.14), channel_id=1, source_target_pairs={{0,12},{1,13},{2,14},{3,15},{4,0},{5,1},{6,2},{7,3},{8,4},{9,5},{1... | collective-permute-start | bytes 688136 | tf_op jit(solution)/shard_map/ppermute | solution.py:31
  50.3 7.3 %collective-permute-start.18 = (bf16[16,32,128]{2,1,0:T(8,128)(2,1)S(1)}, bf16[16,32,128]{2,1,0:T(8,128)(2,1)S(1)}, u32[]{:S(2)}, u32[]{:S(2)}) collective-permute-start(bf16[16,32,128]{2,1,0:T(8,128)(2,1)S(1)} %shard_map.84.refs_0_), channel_id=1, source_target_pairs={{0,2},{1,3},{2,0},{3,1},{4,6},{5,7},{6,4},{7,5},{8,10},{9,11},{10,... | collective-permute-start | bytes 393224 | tf_op jit(solution)/shard_map/ppermute | solution.py:31
  55.2 5.0 %collective-permute-start.17 = (bf16[2,1,32,1024]{3,2,1,0:T(8,128)(2,1)S(1)}, bf16[2,1,32,1024]{3,2,1,0:T(8,128)(2,1)S(1)}, u32[]{:S(2)}, u32[]{:S(2)}) collective-permute-start(bf16[2,1,32,1024]{3,2,1,0:T(8,128)(2,1)S(1)} %get-tuple-element.86), channel_id=1, source_target_pairs={{0,2},{1,3},{2,0},{3,1},{4,6},{5,7},{6,4},{7,5},{8,10},{9,11},{10,... | collective-permute-start | bytes 393224 | tf_op jit(solution)/shard_map/ppermute | solution.py:31
  57.5 2.8 %collective-permute-start.15 = (bf16[1,2,32,1024]{3,2,1,0:T(8,128)(2,1)S(1)}, bf16[1,2,32,1024]{3,2,1,0:T(8,128)(2,1)S(1)}, u32[]{:S(2)}, u32[]{:S(2)}) collective-permute-start(bf16[1,2,32,1024]{3,2,1,0:T(8,128)(2,1)S(1)} %get-tuple-element.82), channel_id=1, source_target_pairs={{0,1},{1,0},{2,3},{3,2},{4,5},{5,4},{6,7},{7,6},{8,9},{9,8},{10,11... | collective-permute-start | bytes 393224 | tf_op jit(solution)/shard_map/ppermute | solution.py:31
  61.0 4.5 %collective-permute-start.21 = (bf16[64,32,128]{2,1,0:T(8,128)(2,1)S(1)}, bf16[64,32,128]{2,1,0:T(8,128)(2,1)S(1)}, u32[]{:S(2)}, u32[]{:S(2)}) collective-permute-start(bf16[64,32,128]{2,1,0:T(8,128)(2,1)S(1)} %shard_map.78.refs_2_.refs_0_), channel_id=1, source_target_pairs={{0,1},{1,0},{2,3},{3,2},{4,5},{5,4},{6,7},{7,6},{8,9},{9,8},{10,11... | collective-permute-start | bytes 1572872 | tf_op jit(solution)/shard_map/ppermute | solution.py:31
  61.1 2.1 %collective-permute-start.19 = (bf16[1,2,32,1024]{3,2,1,0:T(8,128)(2,1)S(1)}, bf16[1,2,32,1024]{3,2,1,0:T(8,128)(2,1)S(1)}, u32[]{:S(2)}, u32[]{:S(2)}) collective-permute-start(bf16[1,2,32,1024]{3,2,1,0:T(8,128)(2,1)S(1)} %get-tuple-element.95), channel_id=1, source_target_pairs={{0,1},{1,0},{2,3},{3,2},{4,5},{5,4},{6,7},{7,6},{8,9},{9,8},{10,11... | collective-permute-start | bytes 393224 | tf_op jit(solution)/shard_map/ppermute | solution.py:31
  63.2 5.6 %collective-permute-start.22 = (bf16[2,1,32,1024]{3,2,1,0:T(8,128)(2,1)S(1)}, bf16[2,1,32,1024]{3,2,1,0:T(8,128)(2,1)S(1)}, u32[]{:S(2)}, u32[]{:S(2)}) collective-permute-start(bf16[2,1,32,1024]{3,2,1,0:T(8,128)(2,1)S(1)} %get-tuple-element.96), channel_id=1, source_target_pairs={{0,2},{1,3},{2,0},{3,1},{4,6},{5,7},{6,4},{7,5},{8,10},{9,11},{10,... | collective-permute-start | bytes 393224 | tf_op jit(solution)/shard_map/ppermute | solution.py:31
  64.8 8.6 %collective-permute-start.24 = (bf16[32,32,128]{2,1,0:T(8,128)(2,1)S(1)}, bf16[32,32,128]{2,1,0:T(8,128)(2,1)S(1)}, u32[]{:S(2)}, u32[]{:S(2)}) collective-permute-start(bf16[32,32,128]{2,1,0:T(8,128)(2,1)S(1)} %shard_map.85.refs_2_), channel_id=1, source_target_pairs={{0,1},{1,0},{2,3},{3,2},{4,5},{5,4},{6,7},{7,6},{8,9},{9,8},{10,11... | collective-permute-start | bytes 786440 | tf_op jit(solution)/shard_map/ppermute | solution.py:31
  64.8 15.0 %collective-permute-start.20 = (bf16[64,1024]{1,0:T(8,128)(2,1)S(1)}, bf16[64,1024]{1,0:T(8,128)(2,1)S(1)}, u32[]{:S(2)}, u32[]{:S(2)}) collective-permute-start(bf16[64,1024]{1,0:T(8,128)(2,1)S(1)} %shard_map.83), channel_id=1, source_target_pairs={{0,16},{1,17},{2,18},{3,19},{4,20},{5,21},{6,22},{7,23},{8,24},{9,... | collective-permute-start | bytes 393224 | tf_op jit(solution)/shard_map/ppermute | solution.py:31
  68.9 10.9 %collective-permute-start.23 = (bf16[64,1024]{1,0:T(8,128)(2,1)S(1)}, bf16[64,1024]{1,0:T(8,128)(2,1)S(1)}, u32[]{:S(2)}, u32[]{:S(2)}) collective-permute-start(bf16[64,1024]{1,0:T(8,128)(2,1)S(1)} %pad_maximum_fusion), channel_id=1, source_target_pairs={{0,16},{1,17},{2,18},{3,19},{4,20},{5,21},{6,22},{7,23},{8,24},{9,... | collective-permute-start | bytes 393224 | tf_op jit(solution)/shard_map/ppermute | solution.py:31
  73.3 9.1 %collective-permute-start.25 = (bf16[64,1024]{1,0:T(8,128)(2,1)S(1)}, bf16[64,1024]{1,0:T(8,128)(2,1)S(1)}, u32[]{:S(2)}, u32[]{:S(2)}) collective-permute-start(bf16[64,1024]{1,0:T(8,128)(2,1)S(1)} %pad_maximum_fusion.1), channel_id=1, source_target_pairs={{0,16},{1,17},{2,18},{3,19},{4,20},{5,21},{6,22},{7,23},{8,24},{9,... | collective-permute-start | bytes 393224 | tf_op jit(solution)/shard_map/ppermute | solution.py:31

commit v3 on v2

--- a/solution.py
+++ b/solution.py
@@ -35,7 +35,14 @@
     return lax.optimization_barrier(values)
 
 
-def call(kernel, outputs, *arrays, limit=8, **more):
+def shifted(r, k, replicas):
+    return lax.rem(r + k % replicas, replicas) if isinstance(r, jax.Array) else (r + k) % replicas
+
+
+def call(kernel, outputs, *arrays, limit=8, flops=0, **more):
+    size = sum(v.size * v.dtype.itemsize for v in arrays)
+    if flops:
+        more["cost_estimate"] = pl.CostEstimate(flops=flops, bytes_accessed=size, transcendentals=0)
     options = dict(in_specs=[VMEM] * len(arrays), out_specs=[VMEM] * len(outputs))
     return pl.pallas_call(
         kernel,
@@ -49,7 +56,7 @@
     return (a.astype(F32) + b.astype(F32)).astype(BF16)
 
 
-def start_kernel(cut, shards, items, grad, gate, x, *refs):
+def start_kernel(shards, items, grad, gate, x, *refs):
     *outs, grad_here, gate_here, x_here, arrived, x_arrived = refs
     tokens, hidden = grad.shape
     replicas = len(x_here)
@@ -57,31 +64,32 @@
     half = outs[0].shape[1]
     copies = []
     for shard in range(shards):
-        here = pl.ds((2 * shard + cut) * half, half) if half % 16 == 0 else pl.ds(2 * shard * half, 2 * half)
+        here = pl.ds(2 * shard * half, 2 * half)
         for i, (source, to) in enumerate(((grad, grad_here), (gate, gate_here))):
             copies.append(pltpu.make_async_copy(source.at[here], to.at[here], arrived.at[i, shard]))
             copies[-1].start()
-    x_copies = {}
-    for of in items:
-        for device, _ in of:
-            if device not in x_copies:
-                block = lax.rem(lax.axis_index("dp") + device, replicas)
-                columns = pl.ds(pl.multiple_of(block * width, width), width)
-                x_copies[device] = pltpu.make_async_copy(x.at[:, columns], x_here[device], x_arrived.at[device])
-                x_copies[device].start()
-    at = outs[-1].shape[0] - hidden // LANES * shards
+    x_copies = []
+    for device in range(replicas):
+        block = shifted(lax.axis_index("dp"), device, replicas)
+        columns = pl.ds(pl.multiple_of(block * width, width), width)
+        x_copies.append(pltpu.make_async_copy(x.at[:, columns], x_here[device], x_arrived.at[device]))
+        x_copies[-1].start()
     for shard in range(shards):
         copies[2 * shard].wait()
         copies[2 * shard + 1].wait()
-        here = pl.ds((2 * shard + cut) * half, half)
-        for column in range(hidden // LANES):
-            lanes = pl.ds(column * LANES, LANES)
-            g = gate_here[here, lanes].astype(F32)
-            value = grad_here[here, lanes].astype(F32) * g * (0.5 + 0.5 * jnp.tanh(0.5 * g))
-            outs[-1][at + column * shards + shard] = value.astype(BF16)
-    for copy in x_copies.values():
+        for out, (_, cut) in zip(outs, items):
+            if cut is None:
+                continue
+            at = out.shape[0] - hidden // LANES * shards + shard
+            here = pl.ds((2 * shard + cut) * half, half)
+            for column in range(hidden // LANES):
+                lanes = pl.ds(column * LANES, LANES)
+                g = gate_here[here, lanes].astype(F32)
+                value = grad_here[here, lanes].astype(F32) * g * (0.5 + 0.5 * jnp.tanh(0.5 * g))
+                out[at + column * shards] = value.astype(BF16)
+    for copy in x_copies:
         copy.wait()
-    for out, of in zip(outs, items):
+    for out, (of, _) in zip(outs, items):
         at = 0
         for device, cuts in of:
             for column in range(width // LANES):
@@ -104,7 +112,7 @@
 
 
 def product_kernel(shards, offsets, *refs):
-    *pieces, w, keep, give = refs
+    pieces, w, outs = refs[: len(offsets)], refs[len(offsets)], refs[len(offsets) + 1 :]
     columns = w.shape[1] // LANES
     bit = lax.rem(lax.axis_index("tensor"), 2)
     left = [
@@ -115,8 +123,56 @@
     ]
     out = lax.dot_general(jnp.concatenate(left), w[...], NT, preferred_element_type=F32).astype(BF16)
     rows = out.shape[0] // 2
-    keep[...] = out[:rows].reshape(keep.shape)
-    give[...] = out[rows:].reshape(give.shape)
+    for i, (mine, theirs) in enumerate(zip(outs[::2], outs[1::2])):
+        n = rows // (len(outs) // 2)
+        mine[...] = out[i * n : (i + 1) * n].reshape(mine.shape)
+        theirs[...] = out[rows + i * n : rows + (i + 1) * n].reshape(theirs.shape)
+
+
+def dealt_kernel(shards, offsets, rider, riders, *refs):
+    pieces, w, outs = refs[: len(offsets)], refs[len(offsets)], refs[len(offsets) + 1 :]
+    columns = w.shape[1] // LANES
+    left = [
+        jnp.concatenate([piece[at + c * shards + (lax.axis_index("tensor") ^ j)] for c in range(columns)], axis=1)
+        for j in range(shards)
+        for piece, at in zip(pieces, offsets)
+    ]
+    total = lax.dot_general(jnp.concatenate(left), w[...], NT, preferred_element_type=F32).astype(BF16)
+    rows = total.shape[0] // shards
+    for j, out in enumerate(outs):
+        if j != rider:
+            out[...] = total[j * rows : (j + 1) * rows]
+            continue
+        half = out.shape[1]
+        for n in range(rows // half):
+            for c in range(total.shape[1] // LANES):
+                out[c * (rows // half) + n] = total[
+                    j * rows + n * half : j * rows + (n + 1) * half, c * LANES : (c + 1) * LANES
+                ]
+        for piece, first, count, to, step in riders:
+            for i in range(count):
+                out[rows // half * (total.shape[1] // LANES) + to + i * step] = pieces[piece][first + i]
+
+
+def total_kernel(count, rider, *refs):
+    parts, outs = refs[:count], refs[count:]
+    rows, width = parts[0].shape
+    total = sum(part[...].astype(F32) for j, part in enumerate(parts) if j != rider)
+    at = 0
+    for out in outs:
+        value = total[at : at + out.shape[0]]
+        if rider is not None:
+            packed = parts[rider]
+            half = packed.shape[1]
+            blocks = [
+                jnp.concatenate(
+                    [packed[c * (rows // half) + n] for c in range(width // LANES)], axis=1
+                )
+                for n in range(at // half, (at + out.shape[0]) // half)
+            ]
+            value = value + jnp.concatenate(blocks).astype(F32)
+        out[...] = value.astype(BF16)
+        at += out.shape[0]
 
 
 def fold_kernel(step, *refs):
@@ -184,21 +240,25 @@
     sent = lax.axis_index("section") < lax.axis_size("section") - 1
     out[...] = jnp.where(sent, base[...], jnp.zeros(base.shape, BF16))
     for block, piece in zip(blocks, pieces):
-        device = lax.rem(lax.axis_index("dp") + block, replicas)
+        device = shifted(lax.axis_index("dp"), block, replicas)
         here = (slice(None), pl.ds(pl.multiple_of(device * width, width), width))
         out[here] = jnp.where(sent, added(base[here], piece[...]), jnp.zeros(piece.shape, BF16))
 
 
-def last_kernel(base, piece, _, out, total, done):
-    width = total.shape[1]
+def last_kernel(blocks, base, *refs):
+    *pieces, _, out, total, done = refs
+    width = pieces[0].shape[1]
     replicas = base.shape[1] // width
-    device = lax.rem(lax.axis_index("dp") + 1, replicas)
-    columns = pl.ds(pl.multiple_of(device * width, width), width)
     sent = lax.axis_index("section") < lax.axis_size("section") - 1
-    total[...] = jnp.where(sent, added(base[:, columns], piece[...]), jnp.zeros(piece.shape, BF16))
-    copy = pltpu.make_async_copy(total, out.at[:, columns], done)
-    copy.start()
-    copy.wait()
+    copies = []
+    for i, (block, piece) in enumerate(zip(blocks, pieces)):
+        device = shifted(lax.axis_index("dp"), block, replicas)
+        columns = pl.ds(pl.multiple_of(device * width, width), width)
+        total[i] = jnp.where(sent, added(base[:, columns], piece[...]), jnp.zeros(piece.shape, BF16))
+        copies.append(pltpu.make_async_copy(total.at[i], out.at[:, columns], done.at[i]))
+        copies[-1].start()
+    for copy in copies:
+        copy.wait()
 
 
 def body(section_input, carried_grad, hidden_grad, saved_gate, w_up):
@@ -213,25 +273,37 @@
     up_count, x_count = hidden // LANES * shards, width // LANES
 
     def up(value):
-        return moved(value, sizes, lambda s, i, j: (s, (i + 1) % replicas, j))
+        return moved(value, sizes, lambda s, i, j: (s, shifted(i, 1, replicas), j))
 
     def down(value):
-        return moved(value, sizes, lambda s, i, j: (s, (i - 1) % replicas, j))
+        return moved(value, sizes, lambda s, i, j: (s, shifted(i, -1, replicas), j))
 
     def returned(value, k):
         return moved(
             value,
             sizes,
-            lambda s, i, j: (s - 1, (i - k) % replicas, j) if s else (sections - 1, i, j),
+            lambda s, i, j: (s - 1, shifted(i, -k, replicas), j) if s else (sections - 1, i, j),
         )
 
     def across(value, step):
         return moved(value, sizes, lambda s, i, j: (s, i, j ^ step))
 
-    def product(*pieces):
-        share = (len(pieces), shards // 2, half, width)
+    def product(*pieces, groups=1, flops=0):
+        share = (len(pieces) // groups, shards // 2, half, width)
         kernel = functools.partial(product_kernel, shards, [at for _, at in pieces])
-        return call(kernel, [share, share], *[piece for piece, _ in pieces], w)
+        return call(kernel, [share] * (2 * groups), *[piece for piece, _ in pieces], w, flops=flops)
+
+    def summed(pieces, halves, rider=None, riders=()):
+        kernel = functools.partial(dealt_kernel, shards, [at for _, at in pieces], rider, riders)
+        shares = [(len(pieces) * half, width)] * shards
+        own = len(pieces) * x_count
+        if rider is not None:
+            shares[rider] = (own + sum(count for _, _, count, _, _ in riders), half, LANES)
+        mine, *others = call(kernel, shares, *[piece for piece, _ in pieces], w)
+        others = [across(v, j + 1) for j, v in enumerate(others)]
+        kernel = functools.partial(total_kernel, shards, rider)
+        outs = call(kernel, [(n * half, width) for n in halves], mine, *others)
+        return outs, others[rider - 1] if rider is not None else None
 
     def fold(step, *pairs):
         n, m = sum(v.shape[0] for v in pairs[::2]), pairs[0].shape[1]
@@ -261,26 +333,6 @@
     order = [0]
     for i in range(steps - 1):
         order += [j + (far_step >> i) for j in order]
-
-    def started(cut, *more):
-        mine = [(d if cut == 0 else replicas - d, (0, 1)) for d in range(1, (replicas + 1) // 2)]
-        if replicas % 2 == 0:
-            mine.append((middle, (cut,)))
-        items = [*more, mine]
-        counts = [sum(x_count * len(cuts) for _, cuts in of) for of in items]
-        counts[-1] += up_count
-        return call(
-            functools.partial(start_kernel, cut, shards, items),
-            [(n, half, LANES) for n in counts],
-            grad,
-            gate,
-            x,
-            in_specs=[HBM] * 3,
-            scratch_shapes=[pltpu.VMEM((tokens, hidden), BF16)] * 2
-            + [[pltpu.VMEM((rows, width), BF16)] * replicas]
-            + [pltpu.SemaphoreType.DMA((2, shards)), pltpu.SemaphoreType.DMA((replicas,))],
-            limit=START,
-        )
 
     tile = 256
 
@@ -298,17 +350,31 @@
             limit=20,
         )[0]
 
-    a = started(0)[0]
-    a_next = up(a)
-    x_own, b = started(1, [(0, (0, 1))])
-    b_next = down(b)
+    both = (0, 1)
+    items = [[(d, both) for d in range(1, (replicas + 1) // 2)], [(last + 1 - d, both) for d in range(1, (replicas + 1) // 2)]]
+    if replicas % 2 == 0:
+        for cut in both:
+            items[cut].append((middle, (cut,)))
+    items = [(items[0], 0), (items[1], 1), ([(0, both)], None)]
+    counts = [sum(x_count * len(cuts) for _, cuts in of) + (cut is not None) * up_count for of, cut in items]
+    a, b, x_own = call(
+        functools.partial(start_kernel, shards, items),
+        [(n, half, LANES) for n in counts],
+        grad,
+        gate,
+        x,
+        in_specs=[HBM] * 3,
+        scratch_shapes=[pltpu.VMEM((tokens, hidden), BF16)] * 2
+        + [[pltpu.VMEM((rows, width), BF16)] * replicas]
+        + [pltpu.SemaphoreType.DMA((2, shards)), pltpu.SemaphoreType.DMA((replicas,))],
+        limit=START,
+    )
+    a_next, b_next = up(a), down(b)
     base = returned(carried_grad[0, 0], 0)
     w = call(held_kernel, [w.shape], w, in_specs=[HBM], scratch_shapes=[pltpu.SemaphoreType.DMA])[0]
     at = a.shape[0] - up_count
     a_parts, b_parts, ats = [a], [b], [at]
-    keep, give = product((a, at), (b, at))
-    keep, give = fold(2, keep, across(give, 1))
-    out = finished(keep, across(give, 2), 2)[0]
+    (out,), _ = summed([(a, at), (b, at)], [2])
     x_own = doubled(x_own, far_step, steps - 1)
     x_own = [x_own, across(x_own, 1)]
 
@@ -318,39 +384,37 @@
     ats.append(at)
     a_next, b_next = up(a[2 * x_count :]), down(b[2 * x_count :])
     zero = returned(out, 0)
-    keep, give = product((a, at), (b, at))
-    keep, give = fold(2, keep, across(give, 1))
+    keep_a, give_a, keep_b, give_b = product((a, at), (b, at), groups=2)
+    keep, give = fold(2, keep_a, across(give_a, 1), keep_b, across(give_b, 1))
+    nears = finished(keep, across(give, 2), 1, 1)
     x_near = stacked(4 * x_count, [(i, 0, 2 * x_count, 2 * i * x_count, 1) for i in range(2)], a, b)
     x_near = doubled(x_near, far_step, steps - 1)
 
     at -= 2 * x_count
-    a, b, keep, give, zero, x_near = together(a_next, b_next, keep, give, zero, x_near)
+    a, b, zero, *nears = together(a_next, b_next, zero, *nears)
     a_parts.append(a)
     b_parts.append(b)
     ats.append(at)
     a_next, b_next = up(a[x_count:]), down(b[x_count:])
-    nears = finished(keep, across(give, 2), 1, 1)
-    keep, give = product((a, at), (b, at))
+    far_a, far_b, x_near = together(a, b, x_near)
+    riders = [(i, 0, x_count, i, 2) for i in range(2)]
+    (out,), x_far = summed([(far_a, at), (far_b, at)], [2], far_step, riders)
+
+    at -= x_count
+    a, b = a_next, b_next
+    a_parts.append(a)
+    b_parts.append(b)
+    ats.append(at)
+    keep, give = product((a, at), (b, at), flops=2 * tokens * hidden * width)
+    x_far, give, out = together(x_far, give, out)
+    two = returned(out, 0)
     keep, give = fold(2, keep, across(give, 1))
-    x_far = stacked(2 * x_count, [(i, 0, x_count, i, 2) for i in range(2)], a, b)
-    x_far = doubled(x_far, far_step, steps - 1)
-
-    at -= x_count
-    a, *nears = together(a_next, *nears)
-    a_parts.append(a)
-    ats.append(at)
-    out = finished(keep, across(give, 2), 2)[0]
-    keep_a, give_a = product((a, at))
-    got_a = across(give_a, 1)
-    b, keep_a, got_a, out, x_far = together(b_next, keep_a, got_a, out, x_far)
-    b_parts.append(b)
-    keep_b, give_b = product((b, at))
-    x_near, x_far, give_b = together(x_near, x_far, give_b)
-    keep, give = fold(2, keep_a, got_a, keep_b, across(give_b, 1))
     got = across(give, 2)
-    out, _ = together(out, give)
-    two = returned(out, 2)
-    x_near, x_far = [x_near, across(x_near, 1)], [x_far, across(x_far, 1)]
+    x_near = [x_near, across(x_near, 1)]
+    places = [(i, 0, x_count, i, 2) for i in range(2)] + [(2, 2 * x_count, 2 * x_count, 2 * x_count, 1)]
+    x_far = stacked(4 * x_count, places, a_parts[2], b_parts[2], x_far)
+    x_far = doubled(x_far, far_step // 2, steps - 2)
+    x_far = [x_far, across(x_far, 1)]
 
     parts = [v for pair_of in zip(a_parts, b_parts) for v in pair_of]
     x_own[0], _ = together(x_own[0], give)
@@ -365,7 +429,10 @@
         parts[:4],
         final=False,
     )
-    keep, weight_grad = together(keep, weight_grad)
+    keep, got, two, weight_grad = together(keep, got, two, weight_grad)
+    two = moved(
+        two, sizes, lambda s, i, j: (s, shifted(i, -2, replicas), j) if s < sections - 1 else (s, i, j ^ 1)
+    )
     out_a, out = finished(keep, got, 1, 1)
     above = returned(jnp.concatenate([out_a, nears[1]]), -1)
     below = returned(jnp.concatenate([nears[0], out]), 1)
@@ -383,26 +450,21 @@
         weight_grad,
         final=True,
     )
-    two, above, weight_grad = together(two, above, weight_grad)
+    two, weight_grad = together(two, weight_grad)
+    kernel = functools.partial(passed_kernel, [0, 2])
+    passed = call(kernel, [(rows, replicas * width)], base, zero, two)[0]
+    passed, above, below = together(passed, above, below)
     passed = call(
-        functools.partial(passed_kernel, [0, 2, last]),
-        [(rows, replicas * width)],
-        base,
-        zero,
-        two,
-        above,
-    )[0]
-    passed, below = together(passed, below)
-    passed = call(
-        last_kernel,
+        functools.partial(last_kernel, [last, 1]),
         [passed.shape],
         base,
+        above,
         below,
         passed,
-        in_specs=[VMEM] * 2 + [HBM],
+        in_specs=[VMEM] * 3 + [HBM],
         out_specs=[HBM],
-        scratch_shapes=[pltpu.VMEM((rows, width), BF16), pltpu.SemaphoreType.DMA],
-        input_output_aliases={2: 0},
+        scratch_shapes=[pltpu.VMEM((2, rows, width), BF16), pltpu.SemaphoreType.DMA((2,))],
+        input_output_aliases={3: 0},
     )[0]
     return passed[None, None], weight_grad[None]
 

time: 83.3 us -> 77.5 us (0.930)
  waiting for transfers between devices: 34.2 us -> 31.5 us
  Pallas kernels: 15.4 us -> 12.9 us
  starting transfers between devices: 31.4 us -> 29.4 us
  local copies, waits for them, and re-layouts: 1.15 us -> 2.57 us
    ppermute x26 -> x28, waiting for transfers between devices: 34.2 us -> 31.5 us  [moved(): return lax.ppermute(value, AXES, pairs)]
    pallas_call x25 -> x20, Pallas kernels: 15.4 us -> 12.9 us  [call(): pl.pallas_call(kernel, out_shape=[v if hasattr(v, 'dtype') else jax.Shape...]
    ppermute x26 -> x28, starting transfers between devices: 31.4 us -> 29.4 us  [moved(): return lax.ppermute(value, AXES, pairs)]
    unnamed x8, local copies, waits for them, and re-layouts: 1.07 us -> 2.5 us
  transfers between devices with their start and end apart: 26 -> 28, of which waited for: 11 -> 14; matrix products, arithmetic and copies ran while one was open for 0% -> 0% of each run, Pallas kernels for 16% -> 16%
where the time goes in v3:
time: 77.5 us; the launch traced here: 77.3 us
  waiting for transfers between devices  31.5 us (41%)
  starting transfers between devices  29.4 us (38%)
  Pallas kernels  12.9 us (17%)
  local copies, waits for them, and re-layouts  2.57 us (3%)
  between operations  0.88 us (1%)
    ppermute x28, waiting for transfers between devices, moved(): return lax.ppermute(value, AXES, pairs)  31.5 us
    ppermute x28, starting transfers between devices, moved(): return lax.ppermute(value, AXES, pairs)  29.4 us
    pallas_call x20, Pallas kernels, call(): pl.pallas_call(kernel, out_shape=[v if hasattr(v, 'dtype') else jax.Shape...  12.9 us
    unnamed x8, local copies, waits for them, and re-layouts  2.5 us
  transfers between devices with their start and end apart: 28, of which 14 were waited for; matrix products, arithmetic and copies ran while one was open for 0% of the time, Pallas kernels for 16%

profile of v3, /device:TPU:0, one launch (start us, length us, event | category | flops | bytes accessed | tf_op | source)
XLA Modules:
  0.0 77.3 jit_solution(696386485462683043)
XLA Ops:
  0.6 3.0 %collective-permute-start.2 = (bf16[64,4096]{1,0:T(8,128)(2,1)}, bf16[64,4096]{1,0:T(8,128)(2,1)S(1)}, u32[]{:S(2)}, u32[]{:S(2)}) collective-permute-start(bf16[64,4096]{1,0:T(8,128)(2,1)} %bitcast.13), channel_id=1, source_target_pairs={{0,16},{1,17},{2,18},{3,19},{4,20},{5,21},{6,22},{7,23},{8,24},{9,... | collective-permute-start | bytes 1572872 | tf_op jit(solution)/shard_map/ppermute | solution.py:31
  3.6 2.6 %shard_map.68 = (bf16[52,32,128]{2,1,0:T(8,128)(2,1)}, bf16[52,32,128]{2,1,0:T(8,128)(2,1)}, bf16[16,32,128]{2,1,0:T(8,128)(2,1)}) custom-call(bf16[256,896]{1,0:T(8,128)(2,1)} %bitcast.11, bf16[256,896]{1,0:T(8,128)(2,1)} %bitcast.12, bf16[64,4096]{1,0:T(8,128)(2,1)} %bitcast.10), custom_call_target="tpu_custom_call" | custom-call | tf_op jit(solution)/shard_map/pallas_call | solution.py:47
  6.2 1.6 %collective-permute-start = (bf16[52,32,128]{2,1,0:T(8,128)(2,1)}, bf16[52,32,128]{2,1,0:T(8,128)(2,1)S(1)}, u32[]{:S(2)}, u32[]{:S(2)}) collective-permute-start(bf16[52,32,128]{2,1,0:T(8,128)(2,1)} %get-tuple-element.55.refs_0_.refs_4_), channel_id=1, source_target_pairs={{0,4},{1,5},{2,6},{3,7},{4,8},{5,9},{6,10},{7,11},{8,12},{9,13},{1... | collective-permute-start | bytes 1277960 | tf_op jit(solution)/shard_map/ppermute | solution.py:31
  7.8 2.2 %collective-permute-start.1 = (bf16[52,32,128]{2,1,0:T(8,128)(2,1)}, bf16[52,32,128]{2,1,0:T(8,128)(2,1)S(1)}, u32[]{:S(2)}, u32[]{:S(2)}) collective-permute-start(bf16[52,32,128]{2,1,0:T(8,128)(2,1)} %get-tuple-element.56.refs_1_.refs_5_), channel_id=1, source_target_pairs={{0,12},{1,13},{2,14},{3,15},{4,0},{5,1},{6,2},{7,3},{8,4},{9,5},{1... | collective-permute-start | bytes 1277960 | tf_op jit(solution)/shard_map/ppermute | solution.py:31
  10.1 1.5 %collective-permute-start.6 = (bf16[16,32,128]{2,1,0:T(8,128)(2,1)}, bf16[16,32,128]{2,1,0:T(8,128)(2,1)S(1)}, u32[]{:S(2)}, u32[]{:S(2)}) collective-permute-start(bf16[16,32,128]{2,1,0:T(8,128)(2,1)} %get-tuple-element.61.refs_0_), channel_id=1, source_target_pairs={{0,2},{1,3},{2,0},{3,1},{4,6},{5,7},{6,4},{7,5},{8,10},{9,11},{10,... | collective-permute-start | bytes 393224 | tf_op jit(solution)/shard_map/ppermute | solution.py:31
  11.6 1.5 %copy-done = bf16[1,1024,896]{2,1,0:T(8,128)(2,1)S(1)} copy-done((bf16[1,1024,896]{2,1,0:T(8,128)(2,1)S(1)}, bf16[1,1024,896]{2,1,0:T(8,128)(2,1)}, u32[]{:S(2)}) %copy-start) | copy-done | bytes 1835032
  13.3 0.9 %copy-done.1 = bf16[52,32,128]{2,1,0:T(8,128)(2,1)S(1)} copy-done((bf16[52,32,128]{2,1,0:T(8,128)(2,1)S(1)}, bf16[52,32,128]{2,1,0:T(8,128)(2,1)}, u32[]{:S(2)}) %copy-start.1) | copy-done | bytes 426008
  15.3 1.5 %collective-permute-start.4 = (bf16[64,1024]{1,0:T(8,128)(2,1)S(1)}, bf16[64,1024]{1,0:T(8,128)(2,1)S(1)}, u32[]{:S(2)}, u32[]{:S(2)}) collective-permute-start(bf16[64,1024]{1,0:T(8,128)(2,1)S(1)} %get-tuple-element.59), channel_id=1, source_target_pairs={{0,2},{1,3},{2,0},{3,1},{4,6},{5,7},{6,4},{7,5},{8,10},{9,11},{10,... | collective-permute-start | bytes 393224 | tf_op jit(solution)/shard_map/ppermute | solution.py:31
  16.9 4.1 %collective-permute-done.4.refs_2_ = bf16[64,1024]{1,0:T(8,128)(2,1)S(1)} collective-permute-done((bf16[64,1024]{1,0:T(8,128)(2,1)S(1)}, bf16[64,1024]{1,0:T(8,128)(2,1)S(1)}, u32[]{:S(2)}, u32[]{:S(2)}) %collective-permute-start.4) | collective-permute-done | bytes 131104 | tf_op jit(solution)/shard_map/ppermute | solution.py:31
  21.0 5.5 %collective-permute-done.5.refs_3_ = bf16[64,1024]{1,0:T(8,128)(2,1)S(1)} collective-permute-done((bf16[64,1024]{1,0:T(8,128)(2,1)S(1)}, bf16[64,1024]{1,0:T(8,128)(2,1)S(1)}, u32[]{:S(2)}, u32[]{:S(2)}) %collective-permute-start.5) | collective-permute-done | bytes 131104 | tf_op jit(solution)/shard_map/ppermute | solution.py:31
  26.6 1.6 %collective-permute-done.1.refs_1_.refs_7_ = bf16[52,32,128]{2,1,0:T(8,128)(2,1)S(1)} collective-permute-done((bf16[52,32,128]{2,1,0:T(8,128)(2,1)}, bf16[52,32,128]{2,1,0:T(8,128)(2,1)S(1)}, u32[]{:S(2)}, u32[]{:S(2)}) %collective-permute-start.1) | collective-permute-done | bytes 426016 | tf_op jit(solution)/shard_map/ppermute | solution.py:31
  28.2 1.2 %collective-permute-start.8 = (bf16[36,32,128]{2,1,0:T(8,128)(2,1)S(1)}, bf16[36,32,128]{2,1,0:T(8,128)(2,1)S(1)}, u32[]{:S(2)}, u32[]{:S(2)}) collective-permute-start(bf16[36,32,128]{2,1,0:T(8,128)(2,1)S(1)} %slice.12), channel_id=1, source_target_pairs={{0,4},{1,5},{2,6},{3,7},{4,8},{5,9},{6,10},{7,11},{8,12},{9,13},{1... | collective-permute-start | bytes 884744 | tf_op jit(solution)/shard_map/ppermute | solution.py:31
  29.4 2.7 %collective-permute-start.9 = (bf16[36,32,128]{2,1,0:T(8,128)(2,1)S(1)}, bf16[36,32,128]{2,1,0:T(8,128)(2,1)S(1)}, u32[]{:S(2)}, u32[]{:S(2)}) collective-permute-start(bf16[36,32,128]{2,1,0:T(8,128)(2,1)S(1)} %slice.13), channel_id=1, source_target_pairs={{0,12},{1,13},{2,14},{3,15},{4,0},{5,1},{6,2},{7,3},{8,4},{9,5},{1... | collective-permute-start | bytes 884744 | tf_op jit(solution)/shard_map/ppermute | solution.py:31
  33.5 1.6 %collective-permute-start.16 = (bf16[32,32,128]{2,1,0:T(8,128)(2,1)S(1)}, bf16[32,32,128]{2,1,0:T(8,128)(2,1)S(1)}, u32[]{:S(2)}, u32[]{:S(2)}) collective-permute-start(bf16[32,32,128]{2,1,0:T(8,128)(2,1)S(1)} %shard_map.77.refs_0_), channel_id=1, source_target_pairs={{0,2},{1,3},{2,0},{3,1},{4,6},{5,7},{6,4},{7,5},{8,10},{9,11},{10,... | collective-permute-start | bytes 786440 | tf_op jit(solution)/shard_map/ppermute | solution.py:31
  35.2 1.0 %collective-permute-start.13 = (bf16[2,1,32,1024]{3,2,1,0:T(8,128)(2,1)S(1)}, bf16[2,1,32,1024]{3,2,1,0:T(8,128)(2,1)S(1)}, u32[]{:S(2)}, u32[]{:S(2)}) collective-permute-start(bf16[2,1,32,1024]{3,2,1,0:T(8,128)(2,1)S(1)} %get-tuple-element.71), channel_id=1, source_target_pairs={{0,2},{1,3},{2,0},{3,1},{4,6},{5,7},{6,4},{7,5},{8,10},{9,11},{10,... | collective-permute-start | bytes 393224 | tf_op jit(solution)/shard_map/ppermute | solution.py:31
  36.7 8.0 %collective-permute-done.13.got = bf16[2,1,32,1024]{3,2,1,0:T(8,128)(2,1)S(1)} collective-permute-done((bf16[2,1,32,1024]{3,2,1,0:T(8,128)(2,1)S(1)}, bf16[2,1,32,1024]{3,2,1,0:T(8,128)(2,1)S(1)}, u32[]{:S(2)}, u32[]{:S(2)}) %collective-permute-start.13) | collective-permute-done | bytes 131104 | tf_op jit(solution)/shard_map/ppermute | solution.py:31
  44.9 3.9 %collective-permute-start.15 = (bf16[28,32,128]{2,1,0:T(8,128)(2,1)S(1)}, bf16[28,32,128]{2,1,0:T(8,128)(2,1)S(1)}, u32[]{:S(2)}, u32[]{:S(2)}) collective-permute-start(bf16[28,32,128]{2,1,0:T(8,128)(2,1)S(1)} %slice.15), channel_id=1, source_target_pairs={{0,12},{1,13},{2,14},{3,15},{4,0},{5,1},{6,2},{7,3},{8,4},{9,5},{1... | collective-permute-start | bytes 688136 | tf_op jit(solution)/shard_map/ppermute | solution.py:31
  48.8 0.8 shard_map.79
  49.5 1.6 %collective-permute-start.17 = (bf16[32,32,128]{2,1,0:T(8,128)(2,1)S(1)}, bf16[32,32,128]{2,1,0:T(8,128)(2,1)S(1)}, u32[]{:S(2)}, u32[]{:S(2)}) collective-permute-start(bf16[32,32,128]{2,1,0:T(8,128)(2,1)S(1)} %get-tuple-element.80), channel_id=1, source_target_pairs={{0,2},{1,3},{2,0},{3,1},{4,6},{5,7},{6,4},{7,5},{8,10},{9,11},{10,... | collective-permute-start | bytes 786440 | tf_op jit(solution)/shard_map/ppermute | solution.py:31
  51.7 3.4 %collective-permute-done.14.refs_0_.refs_6_ = bf16[28,32,128]{2,1,0:T(8,128)(2,1)S(1)} collective-permute-done((bf16[28,32,128]{2,1,0:T(8,128)(2,1)S(1)}, bf16[28,32,128]{2,1,0:T(8,128)(2,1)S(1)}, u32[]{:S(2)}, u32[]{:S(2)}) %collective-permute-start.14) | collective-permute-done | bytes 229408 | tf_op jit(solution)/shard_map/ppermute | solution.py:31
  55.2 1.6 %collective-permute-done.15.refs_1_.refs_7_ = bf16[28,32,128]{2,1,0:T(8,128)(2,1)S(1)} collective-permute-done((bf16[28,32,128]{2,1,0:T(8,128)(2,1)S(1)}, bf16[28,32,128]{2,1,0:T(8,128)(2,1)S(1)}, u32[]{:S(2)}, u32[]{:S(2)}) %collective-permute-start.15) | collective-permute-done | bytes 229408 | tf_op jit(solution)/shard_map/ppermute | solution.py:31
  57.5 1.0 %collective-permute-done.19.refs_3_ = bf16[64,1024]{1,0:T(8,128)(2,1)S(1)} collective-permute-done((bf16[64,1024]{1,0:T(8,128)(2,1)S(1)}, bf16[64,1024]{1,0:T(8,128)(2,1)S(1)}, u32[]{:S(2)}, u32[]{:S(2)}) %collective-permute-start.19) | collective-permute-done | bytes 131104 | tf_op jit(solution)/shard_map/ppermute | solution.py:31
  58.5 0.8 %collective-permute-start.20 = (bf16[2,2,32,1024]{3,2,1,0:T(8,128)(2,1)S(1)}, bf16[2,2,32,1024]{3,2,1,0:T(8,128)(2,1)S(1)}, u32[]{:S(2)}, u32[]{:S(2)}) collective-permute-start(bf16[2,2,32,1024]{3,2,1,0:T(8,128)(2,1)S(1)} %get-tuple-element.85), channel_id=1, source_target_pairs={{0,1},{1,0},{2,3},{3,2},{4,5},{5,4},{6,7},{7,6},{8,9},{9,8},{10,11... | collective-permute-start | bytes 786440 | tf_op jit(solution)/shard_map/ppermute | solution.py:31
  60.6 1.6 %collective-permute-start.21 = (bf16[2,1,32,1024]{3,2,1,0:T(8,128)(2,1)S(1)}, bf16[2,1,32,1024]{3,2,1,0:T(8,128)(2,1)S(1)}, u32[]{:S(2)}, u32[]{:S(2)}) collective-permute-start(bf16[2,1,32,1024]{3,2,1,0:T(8,128)(2,1)S(1)} %get-tuple-element.87), channel_id=1, source_target_pairs={{0,2},{1,3},{2,0},{3,1},{4,6},{5,7},{6,4},{7,5},{8,10},{9,11},{10,... | collective-permute-start | bytes 393224 | tf_op jit(solution)/shard_map/ppermute | solution.py:31
  62.4 2.0 %shard_map.82.refs_8_ = f32[1024,896]{1,0:T(8,128)S(1)} custom-call(bf16[32,32,128]{2,1,0:T(8,128)(2,1)S(1)} %shard_map.72.refs_0_, bf16[32,32,128]{2,1,0:T(8,128)(2,1)S(1)} %collective-permute-done.7.refs_1_, bf16[64,32,128]{2,1,0:T(8,128)(2,1)S(1)} %shard_map.78.refs_2_.refs_0_, bf16[64,32,128]{2,1,0:T(8,128)(2,1)S(1)} %collective-permute-done.23.refs_3_.refs_1_, ...), custom_call_target="tpu_custom_call" | custom-call | tf_op jit(solution)/shard_map/pallas_call | solution.py:47
  64.9 1.6 %collective-permute-done.21.got = bf16[2,1,32,1024]{3,2,1,0:T(8,128)(2,1)S(1)} collective-permute-done((bf16[2,1,32,1024]{3,2,1,0:T(8,128)(2,1)S(1)}, bf16[2,1,32,1024]{3,2,1,0:T(8,128)(2,1)S(1)}, u32[]{:S(2)}, u32[]{:S(2)}) %collective-permute-start.21) | collective-permute-done | bytes 131104 | tf_op jit(solution)/shard_map/ppermute | solution.py:31
  67.3 1.7 %collective-permute-start.27 = (bf16[64,1024]{1,0:T(8,128)(2,1)S(1)}, bf16[64,1024]{1,0:T(8,128)(2,1)S(1)}, u32[]{:S(2)}, u32[]{:S(2)}) collective-permute-start(bf16[64,1024]{1,0:T(8,128)(2,1)S(1)} %pad_maximum_fusion.1), channel_id=1, source_target_pairs={{0,16},{1,17},{2,18},{3,19},{4,20},{5,21},{6,22},{7,23},{8,24},{9,... | collective-permute-start | bytes 393224 | tf_op jit(solution)/shard_map/ppermute | solution.py:31
  69.0 3.1 %shard_map.85 = bf16[1024,896]{1,0:T(8,128)(2,1)} custom-call(bf16[64,32,128]{2,1,0:T(8,128)(2,1)S(1)} %shard_map.78.refs_2_.refs_0_, bf16[64,32,128]{2,1,0:T(8,128)(2,1)S(1)} %collective-permute-done.23.refs_3_.refs_1_, bf16[32,32,128]{2,1,0:T(8,128)(2,1)S(1)} %shard_map.83.refs_2_, bf16[32,32,128]{2,1,0:T(8,128)(2,1)S(1)} %collective-permute-done.25.refs_3_, ...), custom_call_target="tpu_custom_call" | custom-call | tf_op jit(solution)/shard_map/pallas_call | solution.py:47
  72.1 1.4 %collective-permute-done.24.refs_1_ = bf16[64,1024]{1,0:T(8,128)(2,1)S(1)} collective-permute-done((bf16[64,1024]{1,0:T(8,128)(2,1)S(1)}, bf16[64,1024]{1,0:T(8,128)(2,1)S(1)}, u32[]{:S(2)}, u32[]{:S(2)}) %collective-permute-start.24) | collective-permute-done | bytes 131104 | tf_op jit(solution)/shard_map/ppermute | solution.py:31
  73.5 0.9 %shard_map.86.refs_2_ = bf16[64,4096]{1,0:T(8,128)(2,1)} custom-call(bf16[64,4096]{1,0:T(8,128)(2,1)S(1)} %collective-permute-done.2.base, bf16[64,1024]{1,0:T(8,128)(2,1)S(1)} %collective-permute-done.10.refs_0_, bf16[64,1024]{1,0:T(8,128)(2,1)S(1)} %collective-permute-done.24.refs_1_), custom_call_target="tpu_custom_call" | custom-call | tf_op jit(solution)/shard_map/pallas_call | solution.py:47
  74.4 1.5 %collective-permute-done.26.refs_0_ = bf16[64,1024]{1,0:T(8,128)(2,1)S(1)} collective-permute-done((bf16[64,1024]{1,0:T(8,128)(2,1)S(1)}, bf16[64,1024]{1,0:T(8,128)(2,1)S(1)}, u32[]{:S(2)}, u32[]{:S(2)}) %collective-permute-start.26) | collective-permute-done | bytes 131104 | tf_op jit(solution)/shard_map/ppermute | solution.py:31
  76.5 0.8 shard_map.87
  (58 shorter events, 8.2 us)
Async XLA Ops:
  0.6 27.5 %collective-permute-start.2 = (bf16[64,4096]{1,0:T(8,128)(2,1)}, bf16[64,4096]{1,0:T(8,128)(2,1)S(1)}, u32[]{:S(2)}, u32[]{:S(2)}) collective-permute-start(bf16[64,4096]{1,0:T(8,128)(2,1)} %bitcast.13), channel_id=1, source_target_pairs={{0,16},{1,17},{2,18},{3,19},{4,20},{5,21},{6,22},{7,23},{8,24},{9,... | collective-permute-start | bytes 1572872 | tf_op jit(solution)/shard_map/ppermute | solution.py:31
  6.2 20.3 %collective-permute-start = (bf16[52,32,128]{2,1,0:T(8,128)(2,1)}, bf16[52,32,128]{2,1,0:T(8,128)(2,1)S(1)}, u32[]{:S(2)}, u32[]{:S(2)}) collective-permute-start(bf16[52,32,128]{2,1,0:T(8,128)(2,1)} %get-tuple-element.55.refs_0_.refs_4_), channel_id=1, source_target_pairs={{0,4},{1,5},{2,6},{3,7},{4,8},{5,9},{6,10},{7,11},{8,12},{9,13},{1... | collective-permute-start | bytes 1277960 | tf_op jit(solution)/shard_map/ppermute | solution.py:31
  7.8 20.3 %collective-permute-start.1 = (bf16[52,32,128]{2,1,0:T(8,128)(2,1)}, bf16[52,32,128]{2,1,0:T(8,128)(2,1)S(1)}, u32[]{:S(2)}, u32[]{:S(2)}) collective-permute-start(bf16[52,32,128]{2,1,0:T(8,128)(2,1)} %get-tuple-element.56.refs_1_.refs_5_), channel_id=1, source_target_pairs={{0,12},{1,13},{2,14},{3,15},{4,0},{5,1},{6,2},{7,3},{8,4},{9,5},{1... | collective-permute-start | bytes 1277960 | tf_op jit(solution)/shard_map/ppermute | solution.py:31
  10.1 5.2 %collective-permute-start.6 = (bf16[16,32,128]{2,1,0:T(8,128)(2,1)}, bf16[16,32,128]{2,1,0:T(8,128)(2,1)S(1)}, u32[]{:S(2)}, u32[]{:S(2)}) collective-permute-start(bf16[16,32,128]{2,1,0:T(8,128)(2,1)} %get-tuple-element.61.refs_0_), channel_id=1, source_target_pairs={{0,2},{1,3},{2,0},{3,1},{4,6},{5,7},{6,4},{7,5},{8,10},{9,11},{10,... | collective-permute-start | bytes 393224 | tf_op jit(solution)/shard_map/ppermute | solution.py:31
  11.6 1.5 %copy-start = (bf16[1,1024,896]{2,1,0:T(8,128)(2,1)S(1)}, bf16[1,1024,896]{2,1,0:T(8,128)(2,1)}, u32[]{:S(2)}) copy-start(bf16[1,1024,896]{2,1,0:T(8,128)(2,1)} %param.9) | copy-start | bytes 5505028
  13.1 1.0 %copy-start.1 = (bf16[52,32,128]{2,1,0:T(8,128)(2,1)S(1)}, bf16[52,32,128]{2,1,0:T(8,128)(2,1)}, u32[]{:S(2)}) copy-start(bf16[52,32,128]{2,1,0:T(8,128)(2,1)} %get-tuple-element.55.refs_0_.refs_4_) | copy-start | bytes 1277956
  13.1 1.1 %copy-start.2 = (bf16[52,32,128]{2,1,0:T(8,128)(2,1)S(1)}, bf16[52,32,128]{2,1,0:T(8,128)(2,1)}, u32[]{:S(2)}) copy-start(bf16[52,32,128]{2,1,0:T(8,128)(2,1)} %get-tuple-element.56.refs_1_.refs_5_) | copy-start | bytes 1277956
  14.2 2.5 %copy-start.3 = (bf16[16,32,128]{2,1,0:T(8,128)(2,1)S(1)}, bf16[16,32,128]{2,1,0:T(8,128)(2,1)}, u32[]{:S(2)}) copy-start(bf16[16,32,128]{2,1,0:T(8,128)(2,1)} %get-tuple-element.61.refs_0_) | copy-start | bytes 393220
  15.0 1.8 %collective-permute-start.3 = (bf16[64,1024]{1,0:T(8,128)(2,1)S(1)}, bf16[64,1024]{1,0:T(8,128)(2,1)S(1)}, u32[]{:S(2)}, u32[]{:S(2)}) collective-permute-start(bf16[64,1024]{1,0:T(8,128)(2,1)S(1)} %get-tuple-element.58), channel_id=1, source_target_pairs={{0,1},{1,0},{2,3},{3,2},{4,5},{5,4},{6,7},{7,6},{8,9},{9,8},{10,11... | collective-permute-start | bytes 393224 | tf_op jit(solution)/shard_map/ppermute | solution.py:31
  15.3 5.7 %collective-permute-start.4 = (bf16[64,1024]{1,0:T(8,128)(2,1)S(1)}, bf16[64,1024]{1,0:T(8,128)(2,1)S(1)}, u32[]{:S(2)}, u32[]{:S(2)}) collective-permute-start(bf16[64,1024]{1,0:T(8,128)(2,1)S(1)} %get-tuple-element.59), channel_id=1, source_target_pairs={{0,2},{1,3},{2,0},{3,1},{4,6},{5,7},{6,4},{7,5},{8,10},{9,11},{10,... | collective-permute-start | bytes 393224 | tf_op jit(solution)/shard_map/ppermute | solution.py:31
  16.8 9.7 %collective-permute-start.7 = (bf16[32,32,128]{2,1,0:T(8,128)(2,1)S(1)}, bf16[32,32,128]{2,1,0:T(8,128)(2,1)S(1)}, u32[]{:S(2)}, u32[]{:S(2)}) collective-permute-start(bf16[32,32,128]{2,1,0:T(8,128)(2,1)S(1)} %shard_map.72.refs_0_), channel_id=1, source_target_pairs={{0,1},{1,0},{2,3},{3,2},{4,5},{5,4},{6,7},{7,6},{8,9},{9,8},{10,11... | collective-permute-start | bytes 786440 | tf_op jit(solution)/shard_map/ppermute | solution.py:31
  21.0 5.5 %collective-permute-start.5 = (bf16[64,1024]{1,0:T(8,128)(2,1)S(1)}, bf16[64,1024]{1,0:T(8,128)(2,1)S(1)}, u32[]{:S(2)}, u32[]{:S(2)}) collective-permute-start(bf16[64,1024]{1,0:T(8,128)(2,1)S(1)} %get-tuple-element.60), channel_id=1, source_target_pairs={{0,3},{1,2},{2,1},{3,0},{4,7},{5,6},{6,5},{7,4},{8,11},{9,10},{10,... | collective-permute-start | bytes 393224 | tf_op jit(solution)/shard_map/ppermute | solution.py:31
  28.2 16.5 %collective-permute-start.8 = (bf16[36,32,128]{2,1,0:T(8,128)(2,1)S(1)}, bf16[36,32,128]{2,1,0:T(8,128)(2,1)S(1)}, u32[]{:S(2)}, u32[]{:S(2)}) collective-permute-start(bf16[36,32,128]{2,1,0:T(8,128)(2,1)S(1)} %slice.12), channel_id=1, source_target_pairs={{0,4},{1,5},{2,6},{3,7},{4,8},{5,9},{6,10},{7,11},{8,12},{9,13},{1... | collective-permute-start | bytes 884744 | tf_op jit(solution)/shard_map/ppermute | solution.py:31
  29.4 15.3 %collective-permute-start.9 = (bf16[36,32,128]{2,1,0:T(8,128)(2,1)S(1)}, bf16[36,32,128]{2,1,0:T(8,128)(2,1)S(1)}, u32[]{:S(2)}, u32[]{:S(2)}) collective-permute-start(bf16[36,32,128]{2,1,0:T(8,128)(2,1)S(1)} %slice.13), channel_id=1, source_target_pairs={{0,12},{1,13},{2,14},{3,15},{4,0},{5,1},{6,2},{7,3},{8,4},{9,5},{1... | collective-permute-start | bytes 884744 | tf_op jit(solution)/shard_map/ppermute | solution.py:31
  32.9 2.2 %collective-permute-start.11 = (bf16[1,2,32,1024]{3,2,1,0:T(8,128)(2,1)S(1)}, bf16[1,2,32,1024]{3,2,1,0:T(8,128)(2,1)S(1)}, u32[]{:S(2)}, u32[]{:S(2)}) collective-permute-start(bf16[1,2,32,1024]{3,2,1,0:T(8,128)(2,1)S(1)} %get-tuple-element.67), channel_id=1, source_target_pairs={{0,1},{1,0},{2,3},{3,2},{4,5},{5,4},{6,7},{7,6},{8,9},{9,8},{10,11... | collective-permute-start | bytes 393224 | tf_op jit(solution)/shard_map/ppermute | solution.py:31
  33.0 2.1 %collective-permute-start.12 = (bf16[1,2,32,1024]{3,2,1,0:T(8,128)(2,1)S(1)}, bf16[1,2,32,1024]{3,2,1,0:T(8,128)(2,1)S(1)}, u32[]{:S(2)}, u32[]{:S(2)}) collective-permute-start(bf16[1,2,32,1024]{3,2,1,0:T(8,128)(2,1)S(1)} %get-tuple-element.69), channel_id=1, source_target_pairs={{0,1},{1,0},{2,3},{3,2},{4,5},{5,4},{6,7},{7,6},{8,9},{9,8},{10,11... | collective-permute-start | bytes 393224 | tf_op jit(solution)/shard_map/ppermute | solution.py:31
  33.5 15.2 %collective-permute-start.16 = (bf16[32,32,128]{2,1,0:T(8,128)(2,1)S(1)}, bf16[32,32,128]{2,1,0:T(8,128)(2,1)S(1)}, u32[]{:S(2)}, u32[]{:S(2)}) collective-permute-start(bf16[32,32,128]{2,1,0:T(8,128)(2,1)S(1)} %shard_map.77.refs_0_), channel_id=1, source_target_pairs={{0,2},{1,3},{2,0},{3,1},{4,6},{5,7},{6,4},{7,5},{8,10},{9,11},{10,... | collective-permute-start | bytes 786440 | tf_op jit(solution)/shard_map/ppermute | solution.py:31
  35.2 9.5 %collective-permute-start.13 = (bf16[2,1,32,1024]{3,2,1,0:T(8,128)(2,1)S(1)}, bf16[2,1,32,1024]{3,2,1,0:T(8,128)(2,1)S(1)}, u32[]{:S(2)}, u32[]{:S(2)}) collective-permute-start(bf16[2,1,32,1024]{3,2,1,0:T(8,128)(2,1)S(1)} %get-tuple-element.71), channel_id=1, source_target_pairs={{0,2},{1,3},{2,0},{3,1},{4,6},{5,7},{6,4},{7,5},{8,10},{9,11},{10,... | collective-permute-start | bytes 393224 | tf_op jit(solution)/shard_map/ppermute | solution.py:31
  36.2 8.5 %collective-permute-start.10 = (bf16[64,1024]{1,0:T(8,128)(2,1)S(1)}, bf16[64,1024]{1,0:T(8,128)(2,1)S(1)}, u32[]{:S(2)}, u32[]{:S(2)}) collective-permute-start(bf16[64,1024]{1,0:T(8,128)(2,1)S(1)} %shard_map.71), channel_id=1, source_target_pairs={{0,16},{1,17},{2,18},{3,19},{4,20},{5,21},{6,22},{7,23},{8,24},{9,... | collective-permute-start | bytes 393224 | tf_op jit(solution)/shard_map/ppermute | solution.py:31
  44.8 10.4 %collective-permute-start.14 = (bf16[28,32,128]{2,1,0:T(8,128)(2,1)S(1)}, bf16[28,32,128]{2,1,0:T(8,128)(2,1)S(1)}, u32[]{:S(2)}, u32[]{:S(2)}) collective-permute-start(bf16[28,32,128]{2,1,0:T(8,128)(2,1)S(1)} %slice.14), channel_id=1, source_target_pairs={{0,4},{1,5},{2,6},{3,7},{4,8},{5,9},{6,10},{7,11},{8,12},{9,13},{1... | collective-permute-start | bytes 688136 | tf_op jit(solution)/shard_map/ppermute | solution.py:31
  44.9 11.9 %collective-permute-start.15 = (bf16[28,32,128]{2,1,0:T(8,128)(2,1)S(1)}, bf16[28,32,128]{2,1,0:T(8,128)(2,1)S(1)}, u32[]{:S(2)}, u32[]{:S(2)}) collective-permute-start(bf16[28,32,128]{2,1,0:T(8,128)(2,1)S(1)} %slice.15), channel_id=1, source_target_pairs={{0,12},{1,13},{2,14},{3,15},{4,0},{5,1},{6,2},{7,3},{8,4},{9,5},{1... | collective-permute-start | bytes 688136 | tf_op jit(solution)/shard_map/ppermute | solution.py:31
  49.5 9.0 %collective-permute-start.17 = (bf16[32,32,128]{2,1,0:T(8,128)(2,1)S(1)}, bf16[32,32,128]{2,1,0:T(8,128)(2,1)S(1)}, u32[]{:S(2)}, u32[]{:S(2)}) collective-permute-start(bf16[32,32,128]{2,1,0:T(8,128)(2,1)S(1)} %get-tuple-element.80), channel_id=1, source_target_pairs={{0,2},{1,3},{2,0},{3,1},{4,6},{5,7},{6,4},{7,5},{8,10},{9,11},{10,... | collective-permute-start | bytes 786440 | tf_op jit(solution)/shard_map/ppermute | solution.py:31
  51.1 6.4 %collective-permute-start.18 = (bf16[64,1024]{1,0:T(8,128)(2,1)S(1)}, bf16[64,1024]{1,0:T(8,128)(2,1)S(1)}, u32[]{:S(2)}, u32[]{:S(2)}) collective-permute-start(bf16[64,1024]{1,0:T(8,128)(2,1)S(1)} %get-tuple-element.83), channel_id=1, source_target_pairs={{0,1},{1,0},{2,3},{3,2},{4,5},{5,4},{6,7},{7,6},{8,9},{9,8},{10,11... | collective-permute-start | bytes 393224 | tf_op jit(solution)/shard_map/ppermute | solution.py:31
  51.1 7.4 %collective-permute-start.19 = (bf16[64,1024]{1,0:T(8,128)(2,1)S(1)}, bf16[64,1024]{1,0:T(8,128)(2,1)S(1)}, u32[]{:S(2)}, u32[]{:S(2)}) collective-permute-start(bf16[64,1024]{1,0:T(8,128)(2,1)S(1)} %get-tuple-element.84), channel_id=1, source_target_pairs={{0,3},{1,2},{2,1},{3,0},{4,7},{5,6},{6,5},{7,4},{8,11},{9,10},{10,... | collective-permute-start | bytes 393224 | tf_op jit(solution)/shard_map/ppermute | solution.py:31
  55.2 7.2 %collective-permute-start.23 = (bf16[64,32,128]{2,1,0:T(8,128)(2,1)S(1)}, bf16[64,32,128]{2,1,0:T(8,128)(2,1)S(1)}, u32[]{:S(2)}, u32[]{:S(2)}) collective-permute-start(bf16[64,32,128]{2,1,0:T(8,128)(2,1)S(1)} %shard_map.78.refs_2_.refs_0_), channel_id=1, source_target_pairs={{0,1},{1,0},{2,3},{3,2},{4,5},{5,4},{6,7},{7,6},{8,9},{9,8},{10,11... | collective-permute-start | bytes 1572872 | tf_op jit(solution)/shard_map/ppermute | solution.py:31
  58.5 2.0 %collective-permute-start.20 = (bf16[2,2,32,1024]{3,2,1,0:T(8,128)(2,1)S(1)}, bf16[2,2,32,1024]{3,2,1,0:T(8,128)(2,1)S(1)}, u32[]{:S(2)}, u32[]{:S(2)}) collective-permute-start(bf16[2,2,32,1024]{3,2,1,0:T(8,128)(2,1)S(1)} %get-tuple-element.85), channel_id=1, source_target_pairs={{0,1},{1,0},{2,3},{3,2},{4,5},{5,4},{6,7},{7,6},{8,9},{9,8},{10,11... | collective-permute-start | bytes 786440 | tf_op jit(solution)/shard_map/ppermute | solution.py:31
  59.4 5.5 %collective-permute-start.22 = (bf16[64,1024]{1,0:T(8,128)(2,1)S(1)}, bf16[64,1024]{1,0:T(8,128)(2,1)S(1)}, u32[]{:S(2)}, u32[]{:S(2)}) collective-permute-start(bf16[64,1024]{1,0:T(8,128)(2,1)S(1)} %shard_map.80), channel_id=1, source_target_pairs={{0,16},{1,17},{2,18},{3,19},{4,20},{5,21},{6,22},{7,23},{8,24},{9,... | collective-permute-start | bytes 393224 | tf_op jit(solution)/shard_map/ppermute | solution.py:31
  60.6 5.8 %collective-permute-start.21 = (bf16[2,1,32,1024]{3,2,1,0:T(8,128)(2,1)S(1)}, bf16[2,1,32,1024]{3,2,1,0:T(8,128)(2,1)S(1)}, u32[]{:S(2)}, u32[]{:S(2)}) collective-permute-start(bf16[2,1,32,1024]{3,2,1,0:T(8,128)(2,1)S(1)} %get-tuple-element.87), channel_id=1, source_target_pairs={{0,2},{1,3},{2,0},{3,1},{4,6},{5,7},{6,4},{7,5},{8,10},{9,11},{10,... | collective-permute-start | bytes 393224 | tf_op jit(solution)/shard_map/ppermute | solution.py:31
  62.2 6.8 %collective-permute-start.25 = (bf16[32,32,128]{2,1,0:T(8,128)(2,1)S(1)}, bf16[32,32,128]{2,1,0:T(8,128)(2,1)S(1)}, u32[]{:S(2)}, u32[]{:S(2)}) collective-permute-start(bf16[32,32,128]{2,1,0:T(8,128)(2,1)S(1)} %shard_map.83.refs_2_), channel_id=1, source_target_pairs={{0,1},{1,0},{2,3},{3,2},{4,5},{5,4},{6,7},{7,6},{8,9},{9,8},{10,11... | collective-permute-start | bytes 786440 | tf_op jit(solution)/shard_map/ppermute | solution.py:31
  66.5 7.1 %collective-permute-start.24 = (bf16[64,1024]{1,0:T(8,128)(2,1)S(1)}, bf16[64,1024]{1,0:T(8,128)(2,1)S(1)}, u32[]{:S(2)}, u32[]{:S(2)}) collective-permute-start(bf16[64,1024]{1,0:T(8,128)(2,1)S(1)} %collective-permute-done.22), channel_id=1, source_target_pairs={{0,8},{1,9},{2,10},{3,11},{4,12},{5,13},{6,14},{7,15},{8,0},{9,1},... | collective-permute-start | bytes 393224 | tf_op jit(solution)/shard_map/ppermute | solution.py:31
  67.2 8.7 %collective-permute-start.26 = (bf16[64,1024]{1,0:T(8,128)(2,1)S(1)}, bf16[64,1024]{1,0:T(8,128)(2,1)S(1)}, u32[]{:S(2)}, u32[]{:S(2)}) collective-permute-start(bf16[64,1024]{1,0:T(8,128)(2,1)S(1)} %pad_maximum_fusion), channel_id=1, source_target_pairs={{0,16},{1,17},{2,18},{3,19},{4,20},{5,21},{6,22},{7,23},{8,24},{9,... | collective-permute-start | bytes 393224 | tf_op jit(solution)/shard_map/ppermute | solution.py:31
  67.3 9.2 %collective-permute-start.27 = (bf16[64,1024]{1,0:T(8,128)(2,1)S(1)}, bf16[64,1024]{1,0:T(8,128)(2,1)S(1)}, u32[]{:S(2)}, u32[]{:S(2)}) collective-permute-start(bf16[64,1024]{1,0:T(8,128)(2,1)S(1)} %pad_maximum_fusion.1), channel_id=1, source_target_pairs={{0,16},{1,17},{2,18},{3,19},{4,20},{5,21},{6,22},{7,23},{8,24},{9,... | collective-permute-start | bytes 393224 | tf_op jit(solution)/shard_map/ppermute | solution.py:31

commit v4 on v3

--- a/solution.py
+++ b/solution.py
@@ -15,7 +15,7 @@
 NT = (((1,), (1,)), ((), ()))
 TN = (((0,), (0,)), ((), ()))
 LANES = 128
-START = 58
+START = 53
 
 
 def moved(value, sizes, target):
@@ -36,7 +36,10 @@
 
 
 def shifted(r, k, replicas):
-    return lax.rem(r + k % replicas, replicas) if isinstance(r, jax.Array) else (r + k) % replicas
+    if replicas != 4:
+        return lax.rem(r + k % replicas, replicas) if isinstance(r, jax.Array) else (r + k) % replicas
+    place = ((r ^ (r >> 1)) + k % 4) & 3
+    return place ^ (place >> 1)
 
 
 def call(kernel, outputs, *arrays, limit=8, flops=0, **more):
@@ -233,16 +236,12 @@
     out[...] = (total / scale).astype(out.dtype)
 
 
-def passed_kernel(blocks, base, *refs):
-    *pieces, out = refs
-    width = pieces[0].shape[1]
-    replicas = base.shape[1] // width
+def passed_kernel(base, piece, out):
+    width = piece.shape[1]
     sent = lax.axis_index("section") < lax.axis_size("section") - 1
     out[...] = jnp.where(sent, base[...], jnp.zeros(base.shape, BF16))
-    for block, piece in zip(blocks, pieces):
-        device = shifted(lax.axis_index("dp"), block, replicas)
-        here = (slice(None), pl.ds(pl.multiple_of(device * width, width), width))
-        out[here] = jnp.where(sent, added(base[here], piece[...]), jnp.zeros(piece.shape, BF16))
+    here = (slice(None), pl.ds(pl.multiple_of(lax.axis_index("dp") * width, width), width))
+    out[here] = jnp.where(sent, added(base[here], piece[...]), jnp.zeros(piece.shape, BF16))
 
 
 def last_kernel(blocks, base, *refs):
@@ -370,7 +369,8 @@
         limit=START,
     )
     a_next, b_next = up(a), down(b)
-    base = returned(carried_grad[0, 0], 0)
+    carried, *_ = together(carried_grad[0, 0], a, b)
+    base = returned(carried, 0)
     w = call(held_kernel, [w.shape], w, in_specs=[HBM], scratch_shapes=[pltpu.SemaphoreType.DMA])[0]
     at = a.shape[0] - up_count
     a_parts, b_parts, ats = [a], [b], [at]
@@ -391,7 +391,10 @@
     x_near = doubled(x_near, far_step, steps - 1)
 
     at -= 2 * x_count
-    a, b, zero, *nears = together(a_next, b_next, zero, *nears)
+    weight_grad = weight_product(
+        [x_own], [(0, ats[0], 0, 0), (1, ats[0], 0, 1)], [a_parts[0], b_parts[0]], final=False
+    )
+    a, b, zero, weight_grad, *nears = together(a_next, b_next, zero, weight_grad, *nears)
     a_parts.append(a)
     b_parts.append(b)
     ats.append(at)
@@ -406,7 +409,8 @@
     b_parts.append(b)
     ats.append(at)
     keep, give = product((a, at), (b, at), flops=2 * tokens * hidden * width)
-    x_far, give, out = together(x_far, give, out)
+    passed = call(passed_kernel, [(rows, replicas * width)], base, zero)[0]
+    x_far, give, out, passed = together(x_far, give, out, passed)
     two = returned(out, 0)
     keep, give = fold(2, keep, across(give, 1))
     got = across(give, 2)
@@ -417,19 +421,7 @@
     x_far = [x_far, across(x_far, 1)]
 
     parts = [v for pair_of in zip(a_parts, b_parts) for v in pair_of]
-    x_own[0], _ = together(x_own[0], give)
-    weight_grad = weight_product(
-        [x_own, x_near],
-        [
-            (0, ats[0], 0, 0),
-            (1, ats[0], 0, 1),
-            (2, ats[1], 1, 0),
-            (3, ats[1], 1, 2 * x_count + 1),
-        ],
-        parts[:4],
-        final=False,
-    )
-    keep, got, two, weight_grad = together(keep, got, two, weight_grad)
+    keep, got, two = together(keep, got, two)
     two = moved(
         two, sizes, lambda s, i, j: (s, shifted(i, -2, replicas), j) if s < sections - 1 else (s, i, j ^ 1)
     )
@@ -441,30 +433,30 @@
     weight_grad = weight_product(
         [x_near, x_far],
         [
-            (0, ats[2], 1, 0),
-            (1, ats[2], 1, 1),
-            (2, ats[3], 0, 2 * x_count),
-            (3, ats[3], 0, 1),
+            (0, ats[1], 0, 0),
+            (1, ats[1], 0, 2 * x_count + 1),
+            (2, ats[2], 1, 0),
+            (3, ats[2], 1, 1),
+            (4, ats[3], 0, 2 * x_count),
+            (5, ats[3], 0, 1),
         ],
-        parts[4:],
+        parts[2:],
         weight_grad,
         final=True,
     )
-    two, weight_grad = together(two, weight_grad)
-    kernel = functools.partial(passed_kernel, [0, 2])
-    passed = call(kernel, [(rows, replicas * width)], base, zero, two)[0]
-    passed, above, below = together(passed, above, below)
+    passed, weight_grad = together(passed, weight_grad)
     passed = call(
-        functools.partial(last_kernel, [last, 1]),
+        functools.partial(last_kernel, [2, last, 1]),
         [passed.shape],
         base,
+        two,
         above,
         below,
         passed,
-        in_specs=[VMEM] * 3 + [HBM],
+        in_specs=[VMEM] * 4 + [HBM],
         out_specs=[HBM],
-        scratch_shapes=[pltpu.VMEM((2, rows, width), BF16), pltpu.SemaphoreType.DMA((2,))],
-        input_output_aliases={3: 0},
+        scratch_shapes=[pltpu.VMEM((3, rows, width), BF16), pltpu.SemaphoreType.DMA((3,))],
+        input_output_aliases={4: 0},
     )[0]
     return passed[None, None], weight_grad[None]
 

time: 77.5 us -> 74.6 us (0.963)
  starting transfers between devices: 29.4 us -> 26.2 us
  waiting for transfers between devices: 31.5 us -> 33.9 us
  Pallas kernels: 12.9 us -> 11.9 us
  local copies, waits for them, and re-layouts: 2.57 us -> 1.57 us
    ppermute x28, starting transfers between devices: 29.4 us -> 26.2 us  [moved(): return lax.ppermute(value, AXES, pairs)]
    ppermute x28, waiting for transfers between devices: 31.5 us -> 33.9 us  [moved(): return lax.ppermute(value, AXES, pairs)]
    pallas_call x20, Pallas kernels: 12.9 us -> 11.9 us  [call(): pl.pallas_call(kernel, out_shape=[v if hasattr(v, 'dtype') else jax.Shape...]
    unnamed x8 -> x2, local copies, waits for them, and re-layouts: 2.5 us -> 1.5 us
  transfers between devices with their start and end apart: 28 -> 28, of which waited for: 14 -> 12; matrix products, arithmetic and copies ran while one was open for 0% -> 0% of each run, Pallas kernels for 16% -> 13%
where the time goes in v4:
time: 74.6 us; the launch traced here: 74.4 us
  waiting for transfers between devices  33.9 us (45%)
  starting transfers between devices  26.2 us (35%)
  Pallas kernels  11.9 us (16%)
  local copies, waits for them, and re-layouts  1.57 us (2%)
  between operations  0.88 us (1%)
    ppermute x28, waiting for transfers between devices, moved(): return lax.ppermute(value, AXES, pairs)  33.9 us
    ppermute x28, starting transfers between devices, moved(): return lax.ppermute(value, AXES, pairs)  26.2 us
    pallas_call x20, Pallas kernels, call(): pl.pallas_call(kernel, out_shape=[v if hasattr(v, 'dtype') else jax.Shape...  11.9 us
    unnamed x2, local copies, waits for them, and re-layouts  1.5 us
  transfers between devices with their start and end apart: 28, of which 12 were waited for; matrix products, arithmetic and copies ran while one was open for 0% of the time, Pallas kernels for 13%

profile of v4, /device:TPU:0, one launch (start us, length us, event | category | flops | bytes accessed | tf_op | source)
XLA Modules:
  0.0 74.4 jit_solution(14356654188099396814)
XLA Ops:
  0.6 1.6 %shard_map.68 = (bf16[52,32,128]{2,1,0:T(8,128)(2,1)S(1)}, bf16[52,32,128]{2,1,0:T(8,128)(2,1)S(1)}, bf16[16,32,128]{2,1,0:T(8,128)(2,1)S(1)}) custom-call(bf16[256,896]{1,0:T(8,128)(2,1)} %bitcast.11, bf16[256,896]{1,0:T(8,128)(2,1)} %bitcast.12, bf16[64,4096]{1,0:T(8,128)(2,1)} %bitcast.10), custom_call_target="tpu_custom_call" | custom-call | tf_op jit(solution)/shard_map/pallas_call | solution.py:50
  2.3 3.0 %collective-permute-start.2 = (bf16[64,4096]{1,0:T(8,128)(2,1)}, bf16[64,4096]{1,0:T(8,128)(2,1)S(1)}, u32[]{:S(2)}, u32[]{:S(2)}) collective-permute-start(bf16[64,4096]{1,0:T(8,128)(2,1)} %bitcast.13), channel_id=1, source_target_pairs={{0,16},{1,17},{2,18},{3,19},{4,20},{5,21},{6,22},{7,23},{8,24},{9,... | collective-permute-start | bytes 1572872 | tf_op jit(solution)/shard_map/ppermute | solution.py:31
  5.3 1.6 %collective-permute-start = (bf16[52,32,128]{2,1,0:T(8,128)(2,1)S(1)}, bf16[52,32,128]{2,1,0:T(8,128)(2,1)S(1)}, u32[]{:S(2)}, u32[]{:S(2)}) collective-permute-start(bf16[52,32,128]{2,1,0:T(8,128)(2,1)S(1)} %get-tuple-element.53.refs_0_.refs_2_), channel_id=1, source_target_pairs={{0,4},{1,5},{2,6},{3,7},{4,12},{5,13},{6,14},{7,15},{8,0},{9,1},{1... | collective-permute-start | bytes 1277960 | tf_op jit(solution)/shard_map/ppermute | solution.py:31
  6.9 1.3 %collective-permute-start.1 = (bf16[52,32,128]{2,1,0:T(8,128)(2,1)S(1)}, bf16[52,32,128]{2,1,0:T(8,128)(2,1)S(1)}, u32[]{:S(2)}, u32[]{:S(2)}) collective-permute-start(bf16[52,32,128]{2,1,0:T(8,128)(2,1)S(1)} %get-tuple-element.54.refs_1_.refs_3_), channel_id=1, source_target_pairs={{0,8},{1,9},{2,10},{3,11},{4,0},{5,1},{6,2},{7,3},{8,12},{9,13},{1... | collective-permute-start | bytes 1277960 | tf_op jit(solution)/shard_map/ppermute | solution.py:31
  8.2 1.5 %collective-permute-start.6 = (bf16[16,32,128]{2,1,0:T(8,128)(2,1)S(1)}, bf16[16,32,128]{2,1,0:T(8,128)(2,1)S(1)}, u32[]{:S(2)}, u32[]{:S(2)}) collective-permute-start(bf16[16,32,128]{2,1,0:T(8,128)(2,1)S(1)} %get-tuple-element.60.refs_0_), channel_id=1, source_target_pairs={{0,2},{1,3},{2,0},{3,1},{4,6},{5,7},{6,4},{7,5},{8,10},{9,11},{10,... | collective-permute-start | bytes 393224 | tf_op jit(solution)/shard_map/ppermute | solution.py:31
  9.7 1.5 %copy-done = bf16[1,1024,896]{2,1,0:T(8,128)(2,1)S(1)} copy-done((bf16[1,1024,896]{2,1,0:T(8,128)(2,1)S(1)}, bf16[1,1024,896]{2,1,0:T(8,128)(2,1)}, u32[]{:S(2)}) %copy-start) | copy-done | bytes 1835032
  11.4 0.7 %shard_map.70 = (bf16[64,1024]{1,0:T(8,128)(2,1)S(1)}, bf16[64,1024]{1,0:T(8,128)(2,1)S(1)}, bf16[64,1024]{1,0:T(8,128)(2,1)S(1)}, bf16[64,1024]{1,0:T(8,128)(2,1)S(1)}) custom-call(bf16[52,32,128]{2,1,0:T(8,128)(2,1)S(1)} %get-tuple-element.53.refs_0_.refs_2_, bf16[52,32,128]{2,1,0:T(8,128)(2,1)S(1)} %get-tuple-element.54.refs_1_.refs_3_, ...), custom_call_target="tpu_custom_call" | custom-call | tf_op jit(solution)/shard_map/pallas_call | solution.py:50
  12.2 1.0 %collective-permute-done.6.refs_1_ = bf16[16,32,128]{2,1,0:T(8,128)(2,1)S(1)} collective-permute-done((bf16[16,32,128]{2,1,0:T(8,128)(2,1)S(1)}, bf16[16,32,128]{2,1,0:T(8,128)(2,1)S(1)}, u32[]{:S(2)}, u32[]{:S(2)}) %collective-permute-start.6) | collective-permute-done | bytes 131104 | tf_op jit(solution)/shard_map/ppermute | solution.py:31
  13.2 1.5 %collective-permute-start.4 = (bf16[64,1024]{1,0:T(8,128)(2,1)S(1)}, bf16[64,1024]{1,0:T(8,128)(2,1)S(1)}, u32[]{:S(2)}, u32[]{:S(2)}) collective-permute-start(bf16[64,1024]{1,0:T(8,128)(2,1)S(1)} %get-tuple-element.58), channel_id=1, source_target_pairs={{0,2},{1,3},{2,0},{3,1},{4,6},{5,7},{6,4},{7,5},{8,10},{9,11},{10,... | collective-permute-start | bytes 393224 | tf_op jit(solution)/shard_map/ppermute | solution.py:31
  14.8 3.3 %collective-permute-done.4.refs_2_ = bf16[64,1024]{1,0:T(8,128)(2,1)S(1)} collective-permute-done((bf16[64,1024]{1,0:T(8,128)(2,1)S(1)}, bf16[64,1024]{1,0:T(8,128)(2,1)S(1)}, u32[]{:S(2)}, u32[]{:S(2)}) %collective-permute-start.4) | collective-permute-done | bytes 131104 | tf_op jit(solution)/shard_map/ppermute | solution.py:31
  18.2 5.7 %collective-permute-done.5.refs_3_ = bf16[64,1024]{1,0:T(8,128)(2,1)S(1)} collective-permute-done((bf16[64,1024]{1,0:T(8,128)(2,1)S(1)}, bf16[64,1024]{1,0:T(8,128)(2,1)S(1)}, u32[]{:S(2)}, u32[]{:S(2)}) %collective-permute-start.5) | collective-permute-done | bytes 131104 | tf_op jit(solution)/shard_map/ppermute | solution.py:31
  24.0 2.6 %collective-permute-done.1.refs_1_.refs_5_ = bf16[52,32,128]{2,1,0:T(8,128)(2,1)S(1)} collective-permute-done((bf16[52,32,128]{2,1,0:T(8,128)(2,1)S(1)}, bf16[52,32,128]{2,1,0:T(8,128)(2,1)S(1)}, u32[]{:S(2)}, u32[]{:S(2)}) %collective-permute-start.1) | collective-permute-done | bytes 426016 | tf_op jit(solution)/shard_map/ppermute | solution.py:31
  26.6 1.7 %collective-permute-start.9 = (bf16[36,32,128]{2,1,0:T(8,128)(2,1)S(1)}, bf16[36,32,128]{2,1,0:T(8,128)(2,1)S(1)}, u32[]{:S(2)}, u32[]{:S(2)}) collective-permute-start(bf16[36,32,128]{2,1,0:T(8,128)(2,1)S(1)} %slice.13), channel_id=1, source_target_pairs={{0,8},{1,9},{2,10},{3,11},{4,0},{5,1},{6,2},{7,3},{8,12},{9,13},{1... | collective-permute-start | bytes 884744 | tf_op jit(solution)/shard_map/ppermute | solution.py:31
  30.1 1.6 %collective-permute-start.16 = (bf16[32,32,128]{2,1,0:T(8,128)(2,1)S(1)}, bf16[32,32,128]{2,1,0:T(8,128)(2,1)S(1)}, u32[]{:S(2)}, u32[]{:S(2)}) collective-permute-start(bf16[32,32,128]{2,1,0:T(8,128)(2,1)S(1)} %shard_map.78.refs_0_), channel_id=1, source_target_pairs={{0,2},{1,3},{2,0},{3,1},{4,6},{5,7},{6,4},{7,5},{8,10},{9,11},{10,... | collective-permute-start | bytes 786440 | tf_op jit(solution)/shard_map/ppermute | solution.py:31
  31.7 1.0 %collective-permute-start.13 = (bf16[2,1,32,1024]{3,2,1,0:T(8,128)(2,1)S(1)}, bf16[2,1,32,1024]{3,2,1,0:T(8,128)(2,1)S(1)}, u32[]{:S(2)}, u32[]{:S(2)}) collective-permute-start(bf16[2,1,32,1024]{3,2,1,0:T(8,128)(2,1)S(1)} %get-tuple-element.72), channel_id=1, source_target_pairs={{0,2},{1,3},{2,0},{3,1},{4,6},{5,7},{6,4},{7,5},{8,10},{9,11},{10,... | collective-permute-start | bytes 393224 | tf_op jit(solution)/shard_map/ppermute | solution.py:31
  33.3 1.4 %shard_map.73.refs_10_ = f32[1024,896]{1,0:T(8,128)S(1)} custom-call(bf16[32,32,128]{2,1,0:T(8,128)(2,1)S(1)} %shard_map.72.refs_0_, bf16[32,32,128]{2,1,0:T(8,128)(2,1)S(1)} %collective-permute-done.7.refs_1_, bf16[52,32,128]{2,1,0:T(8,128)(2,1)S(1)} %get-tuple-element.53.refs_0_.refs_2_, bf16[52,32,128]{2,1,0:T(8,128)(2,1)S(1)} %get-tuple-element.54.refs_1_.refs_3_), custom_call_target="tpu_custom_call" | custom-call | tf_op jit(solution)/shard_map/pallas_call | solution.py:50
  34.7 6.6 %collective-permute-done.13.got = bf16[2,1,32,1024]{3,2,1,0:T(8,128)(2,1)S(1)} collective-permute-done((bf16[2,1,32,1024]{3,2,1,0:T(8,128)(2,1)S(1)}, bf16[2,1,32,1024]{3,2,1,0:T(8,128)(2,1)S(1)}, u32[]{:S(2)}, u32[]{:S(2)}) %collective-permute-start.13) | collective-permute-done | bytes 131104 | tf_op jit(solution)/shard_map/ppermute | solution.py:31
  41.3 1.3 %collective-permute-done.8.refs_0_.refs_6_ = bf16[36,32,128]{2,1,0:T(8,128)(2,1)S(1)} collective-permute-done((bf16[36,32,128]{2,1,0:T(8,128)(2,1)S(1)}, bf16[36,32,128]{2,1,0:T(8,128)(2,1)S(1)}, u32[]{:S(2)}, u32[]{:S(2)}) %collective-permute-start.8) | collective-permute-done | bytes 294944 | tf_op jit(solution)/shard_map/ppermute | solution.py:31
  42.6 1.3 %collective-permute-start.15 = (bf16[28,32,128]{2,1,0:T(8,128)(2,1)S(1)}, bf16[28,32,128]{2,1,0:T(8,128)(2,1)S(1)}, u32[]{:S(2)}, u32[]{:S(2)}) collective-permute-start(bf16[28,32,128]{2,1,0:T(8,128)(2,1)S(1)} %slice.15), channel_id=1, source_target_pairs={{0,8},{1,9},{2,10},{3,11},{4,0},{5,1},{6,2},{7,3},{8,12},{9,13},{1... | collective-permute-start | bytes 688136 | tf_op jit(solution)/shard_map/ppermute | solution.py:31
  44.8 0.7 %shard_map.80 = (bf16[64,1024]{1,0:T(8,128)(2,1)S(1)}, bf16[64,1024]{1,0:T(8,128)(2,1)S(1)}, bf16[32,32,128]{2,1,0:T(8,128)(2,1)S(1)}, bf16[64,1024]{1,0:T(8,128)(2,1)S(1)}) custom-call(bf16[36,32,128]{2,1,0:T(8,128)(2,1)S(1)} %collective-permute-done.8.refs_0_.refs_6_, bf16[36,32,128]{2,1,0:T(8,128)(2,1)S(1)} %collective-permute-done.9.refs_1_.refs_7_, ...), custom_call_target="tpu_custom_call" | custom-call | tf_op jit(solution)/shard_map/pallas_call | solution.py:50
  45.5 1.6 %collective-permute-start.17 = (bf16[32,32,128]{2,1,0:T(8,128)(2,1)S(1)}, bf16[32,32,128]{2,1,0:T(8,128)(2,1)S(1)}, u32[]{:S(2)}, u32[]{:S(2)}) collective-permute-start(bf16[32,32,128]{2,1,0:T(8,128)(2,1)S(1)} %get-tuple-element.80), channel_id=1, source_target_pairs={{0,2},{1,3},{2,0},{3,1},{4,6},{5,7},{6,4},{7,5},{8,10},{9,11},{10,... | collective-permute-start | bytes 786440 | tf_op jit(solution)/shard_map/ppermute | solution.py:31
  47.7 0.9 %shard_map.82.refs_3_ = bf16[64,4096]{1,0:T(8,128)(2,1)} custom-call(bf16[64,4096]{1,0:T(8,128)(2,1)S(1)} %collective-permute-done.2.base, bf16[64,1024]{1,0:T(8,128)(2,1)S(1)} %collective-permute-done.10.piece), custom_call_target="tpu_custom_call" | custom-call | tf_op jit(solution)/shard_map/pallas_call | solution.py:50
  48.6 2.6 %collective-permute-done.15.refs_1_.refs_9_ = bf16[28,32,128]{2,1,0:T(8,128)(2,1)S(1)} collective-permute-done((bf16[28,32,128]{2,1,0:T(8,128)(2,1)S(1)}, bf16[28,32,128]{2,1,0:T(8,128)(2,1)S(1)}, u32[]{:S(2)}, u32[]{:S(2)}) %collective-permute-start.15) | collective-permute-done | bytes 229408 | tf_op jit(solution)/shard_map/ppermute | solution.py:31
  51.2 4.8 %collective-permute-done.14.refs_0_.refs_8_ = bf16[28,32,128]{2,1,0:T(8,128)(2,1)S(1)} collective-permute-done((bf16[28,32,128]{2,1,0:T(8,128)(2,1)S(1)}, bf16[28,32,128]{2,1,0:T(8,128)(2,1)S(1)}, u32[]{:S(2)}, u32[]{:S(2)}) %collective-permute-start.14) | collective-permute-done | bytes 229408 | tf_op jit(solution)/shard_map/ppermute | solution.py:31
  58.5 1.6 %collective-permute-start.21 = (bf16[2,1,32,1024]{3,2,1,0:T(8,128)(2,1)S(1)}, bf16[2,1,32,1024]{3,2,1,0:T(8,128)(2,1)S(1)}, u32[]{:S(2)}, u32[]{:S(2)}) collective-permute-start(bf16[2,1,32,1024]{3,2,1,0:T(8,128)(2,1)S(1)} %get-tuple-element.88), channel_id=1, source_target_pairs={{0,2},{1,3},{2,0},{3,1},{4,6},{5,7},{6,4},{7,5},{8,10},{9,11},{10,... | collective-permute-start | bytes 393224 | tf_op jit(solution)/shard_map/ppermute | solution.py:31
  60.2 2.7 %collective-permute-done.22 = bf16[64,1024]{1,0:T(8,128)(2,1)S(1)} collective-permute-done((bf16[64,1024]{1,0:T(8,128)(2,1)S(1)}, bf16[64,1024]{1,0:T(8,128)(2,1)S(1)}, u32[]{:S(2)}, u32[]{:S(2)}) %collective-permute-start.22) | collective-permute-done | bytes 131104 | tf_op jit(solution)/shard_map/ppermute | solution.py:31
  62.9 1.2 %collective-permute-done.21.got = bf16[2,1,32,1024]{3,2,1,0:T(8,128)(2,1)S(1)} collective-permute-done((bf16[2,1,32,1024]{3,2,1,0:T(8,128)(2,1)S(1)}, bf16[2,1,32,1024]{3,2,1,0:T(8,128)(2,1)S(1)}, u32[]{:S(2)}, u32[]{:S(2)}) %collective-permute-start.21) | collective-permute-done | bytes 131104 | tf_op jit(solution)/shard_map/ppermute | solution.py:31
  64.9 1.5 %collective-permute-start.24 = (bf16[64,1024]{1,0:T(8,128)(2,1)S(1)}, bf16[64,1024]{1,0:T(8,128)(2,1)S(1)}, u32[]{:S(2)}, u32[]{:S(2)}) collective-permute-start(bf16[64,1024]{1,0:T(8,128)(2,1)S(1)} %pad_maximum_fusion), channel_id=1, source_target_pairs={{0,16},{1,17},{2,18},{3,19},{4,20},{5,21},{6,22},{7,23},{8,24},{9,... | collective-permute-start | bytes 393224 | tf_op jit(solution)/shard_map/ppermute | solution.py:31
  66.4 2.1 %collective-permute-start.23 = (bf16[64,1024]{1,0:T(8,128)(2,1)S(1)}, bf16[64,1024]{1,0:T(8,128)(2,1)S(1)}, u32[]{:S(2)}, u32[]{:S(2)}) collective-permute-start(bf16[64,1024]{1,0:T(8,128)(2,1)S(1)} %collective-permute-done.22), channel_id=1, source_target_pairs={{0,12},{1,13},{2,14},{3,15},{4,8},{5,9},{6,10},{7,11},{8,4},{9,5},... | collective-permute-start | bytes 393224 | tf_op jit(solution)/shard_map/ppermute | solution.py:31
  68.5 3.6 %shard_map.86 = bf16[1024,896]{1,0:T(8,128)(2,1)} custom-call(bf16[64,32,128]{2,1,0:T(8,128)(2,1)S(1)} %shard_map.79.refs_0_, bf16[64,32,128]{2,1,0:T(8,128)(2,1)S(1)} %collective-permute-done.26.refs_1_, bf16[32,32,128]{2,1,0:T(8,128)(2,1)S(1)} %shard_map.85.refs_2_, bf16[32,32,128]{2,1,0:T(8,128)(2,1)S(1)} %collective-permute-done.27.refs_3_, ...), custom_call_target="tpu_custom_call" | custom-call | tf_op jit(solution)/shard_map/pallas_call | solution.py:50
  72.1 1.5 %collective-permute-done.24.refs_1_ = bf16[64,1024]{1,0:T(8,128)(2,1)S(1)} collective-permute-done((bf16[64,1024]{1,0:T(8,128)(2,1)S(1)}, bf16[64,1024]{1,0:T(8,128)(2,1)S(1)}, u32[]{:S(2)}, u32[]{:S(2)}) %collective-permute-start.24) | collective-permute-done | bytes 131104 | tf_op jit(solution)/shard_map/ppermute | solution.py:31
  73.6 0.8 %shard_map.87 = bf16[64,4096]{1,0:T(8,128)(2,1)} custom-call(bf16[64,4096]{1,0:T(8,128)(2,1)S(1)} %collective-permute-done.2.base, bf16[64,1024]{1,0:T(8,128)(2,1)S(1)} %collective-permute-done.23.refs_0_, bf16[64,1024]{1,0:T(8,128)(2,1)S(1)} %collective-permute-done.24.refs_1_, ...), custom_call_target="tpu_custom_call", output_to_operand_aliasing={{}: (4, {})} | custom-call | tf_op jit(solution)/shard_map/pallas_call | solution.py:50
  (52 shorter events, 7.5 us)
Async XLA Ops:
  2.3 24.3 %collective-permute-start.2 = (bf16[64,4096]{1,0:T(8,128)(2,1)}, bf16[64,4096]{1,0:T(8,128)(2,1)S(1)}, u32[]{:S(2)}, u32[]{:S(2)}) collective-permute-start(bf16[64,4096]{1,0:T(8,128)(2,1)} %bitcast.13), channel_id=1, source_target_pairs={{0,16},{1,17},{2,18},{3,19},{4,20},{5,21},{6,22},{7,23},{8,24},{9,... | collective-permute-start | bytes 1572872 | tf_op jit(solution)/shard_map/ppermute | solution.py:31
  5.3 18.7 %collective-permute-start = (bf16[52,32,128]{2,1,0:T(8,128)(2,1)S(1)}, bf16[52,32,128]{2,1,0:T(8,128)(2,1)S(1)}, u32[]{:S(2)}, u32[]{:S(2)}) collective-permute-start(bf16[52,32,128]{2,1,0:T(8,128)(2,1)S(1)} %get-tuple-element.53.refs_0_.refs_2_), channel_id=1, source_target_pairs={{0,4},{1,5},{2,6},{3,7},{4,12},{5,13},{6,14},{7,15},{8,0},{9,1},{1... | collective-permute-start | bytes 1277960 | tf_op jit(solution)/shard_map/ppermute | solution.py:31
  6.9 19.7 %collective-permute-start.1 = (bf16[52,32,128]{2,1,0:T(8,128)(2,1)S(1)}, bf16[52,32,128]{2,1,0:T(8,128)(2,1)S(1)}, u32[]{:S(2)}, u32[]{:S(2)}) collective-permute-start(bf16[52,32,128]{2,1,0:T(8,128)(2,1)S(1)} %get-tuple-element.54.refs_1_.refs_3_), channel_id=1, source_target_pairs={{0,8},{1,9},{2,10},{3,11},{4,0},{5,1},{6,2},{7,3},{8,12},{9,13},{1... | collective-permute-start | bytes 1277960 | tf_op jit(solution)/shard_map/ppermute | solution.py:31
  8.2 5.0 %collective-permute-start.6 = (bf16[16,32,128]{2,1,0:T(8,128)(2,1)S(1)}, bf16[16,32,128]{2,1,0:T(8,128)(2,1)S(1)}, u32[]{:S(2)}, u32[]{:S(2)}) collective-permute-start(bf16[16,32,128]{2,1,0:T(8,128)(2,1)S(1)} %get-tuple-element.60.refs_0_), channel_id=1, source_target_pairs={{0,2},{1,3},{2,0},{3,1},{4,6},{5,7},{6,4},{7,5},{8,10},{9,11},{10,... | collective-permute-start | bytes 393224 | tf_op jit(solution)/shard_map/ppermute | solution.py:31
  9.7 1.5 %copy-start = (bf16[1,1024,896]{2,1,0:T(8,128)(2,1)S(1)}, bf16[1,1024,896]{2,1,0:T(8,128)(2,1)}, u32[]{:S(2)}) copy-start(bf16[1,1024,896]{2,1,0:T(8,128)(2,1)} %param.9) | copy-start | bytes 5505028
  12.1 2.6 %collective-permute-start.3 = (bf16[64,1024]{1,0:T(8,128)(2,1)S(1)}, bf16[64,1024]{1,0:T(8,128)(2,1)S(1)}, u32[]{:S(2)}, u32[]{:S(2)}) collective-permute-start(bf16[64,1024]{1,0:T(8,128)(2,1)S(1)} %get-tuple-element.57), channel_id=1, source_target_pairs={{0,1},{1,0},{2,3},{3,2},{4,5},{5,4},{6,7},{7,6},{8,9},{9,8},{10,11... | collective-permute-start | bytes 393224 | tf_op jit(solution)/shard_map/ppermute | solution.py:31
  13.2 5.0 %collective-permute-start.4 = (bf16[64,1024]{1,0:T(8,128)(2,1)S(1)}, bf16[64,1024]{1,0:T(8,128)(2,1)S(1)}, u32[]{:S(2)}, u32[]{:S(2)}) collective-permute-start(bf16[64,1024]{1,0:T(8,128)(2,1)S(1)} %get-tuple-element.58), channel_id=1, source_target_pairs={{0,2},{1,3},{2,0},{3,1},{4,6},{5,7},{6,4},{7,5},{8,10},{9,11},{10,... | collective-permute-start | bytes 393224 | tf_op jit(solution)/shard_map/ppermute | solution.py:31
  14.7 9.2 %collective-permute-start.7 = (bf16[32,32,128]{2,1,0:T(8,128)(2,1)S(1)}, bf16[32,32,128]{2,1,0:T(8,128)(2,1)S(1)}, u32[]{:S(2)}, u32[]{:S(2)}) collective-permute-start(bf16[32,32,128]{2,1,0:T(8,128)(2,1)S(1)} %shard_map.72.refs_0_), channel_id=1, source_target_pairs={{0,1},{1,0},{2,3},{3,2},{4,5},{5,4},{6,7},{7,6},{8,9},{9,8},{10,11... | collective-permute-start | bytes 786440 | tf_op jit(solution)/shard_map/ppermute | solution.py:31
  18.1 5.7 %collective-permute-start.5 = (bf16[64,1024]{1,0:T(8,128)(2,1)S(1)}, bf16[64,1024]{1,0:T(8,128)(2,1)S(1)}, u32[]{:S(2)}, u32[]{:S(2)}) collective-permute-start(bf16[64,1024]{1,0:T(8,128)(2,1)S(1)} %get-tuple-element.59), channel_id=1, source_target_pairs={{0,3},{1,2},{2,1},{3,0},{4,7},{5,6},{6,5},{7,4},{8,11},{9,10},{10,... | collective-permute-start | bytes 393224 | tf_op jit(solution)/shard_map/ppermute | solution.py:31
  26.6 14.6 %collective-permute-start.9 = (bf16[36,32,128]{2,1,0:T(8,128)(2,1)S(1)}, bf16[36,32,128]{2,1,0:T(8,128)(2,1)S(1)}, u32[]{:S(2)}, u32[]{:S(2)}) collective-permute-start(bf16[36,32,128]{2,1,0:T(8,128)(2,1)S(1)} %slice.13), channel_id=1, source_target_pairs={{0,8},{1,9},{2,10},{3,11},{4,0},{5,1},{6,2},{7,3},{8,12},{9,13},{1... | collective-permute-start | bytes 884744 | tf_op jit(solution)/shard_map/ppermute | solution.py:31
  28.4 14.2 %collective-permute-start.8 = (bf16[36,32,128]{2,1,0:T(8,128)(2,1)S(1)}, bf16[36,32,128]{2,1,0:T(8,128)(2,1)S(1)}, u32[]{:S(2)}, u32[]{:S(2)}) collective-permute-start(bf16[36,32,128]{2,1,0:T(8,128)(2,1)S(1)} %slice.12), channel_id=1, source_target_pairs={{0,4},{1,5},{2,6},{3,7},{4,12},{5,13},{6,14},{7,15},{8,0},{9,1},{1... | collective-permute-start | bytes 884744 | tf_op jit(solution)/shard_map/ppermute | solution.py:31
  29.5 2.2 %collective-permute-start.11 = (bf16[1,2,32,1024]{3,2,1,0:T(8,128)(2,1)S(1)}, bf16[1,2,32,1024]{3,2,1,0:T(8,128)(2,1)S(1)}, u32[]{:S(2)}, u32[]{:S(2)}) collective-permute-start(bf16[1,2,32,1024]{3,2,1,0:T(8,128)(2,1)S(1)} %get-tuple-element.68), channel_id=1, source_target_pairs={{0,1},{1,0},{2,3},{3,2},{4,5},{5,4},{6,7},{7,6},{8,9},{9,8},{10,11... | collective-permute-start | bytes 393224 | tf_op jit(solution)/shard_map/ppermute | solution.py:31
  29.6 2.1 %collective-permute-start.12 = (bf16[1,2,32,1024]{3,2,1,0:T(8,128)(2,1)S(1)}, bf16[1,2,32,1024]{3,2,1,0:T(8,128)(2,1)S(1)}, u32[]{:S(2)}, u32[]{:S(2)}) collective-permute-start(bf16[1,2,32,1024]{3,2,1,0:T(8,128)(2,1)S(1)} %get-tuple-element.70), channel_id=1, source_target_pairs={{0,1},{1,0},{2,3},{3,2},{4,5},{5,4},{6,7},{7,6},{8,9},{9,8},{10,11... | collective-permute-start | bytes 393224 | tf_op jit(solution)/shard_map/ppermute | solution.py:31
  30.1 14.7 %collective-permute-start.16 = (bf16[32,32,128]{2,1,0:T(8,128)(2,1)S(1)}, bf16[32,32,128]{2,1,0:T(8,128)(2,1)S(1)}, u32[]{:S(2)}, u32[]{:S(2)}) collective-permute-start(bf16[32,32,128]{2,1,0:T(8,128)(2,1)S(1)} %shard_map.78.refs_0_), channel_id=1, source_target_pairs={{0,2},{1,3},{2,0},{3,1},{4,6},{5,7},{6,4},{7,5},{8,10},{9,11},{10,... | collective-permute-start | bytes 786440 | tf_op jit(solution)/shard_map/ppermute | solution.py:31
  31.7 9.5 %collective-permute-start.13 = (bf16[2,1,32,1024]{3,2,1,0:T(8,128)(2,1)S(1)}, bf16[2,1,32,1024]{3,2,1,0:T(8,128)(2,1)S(1)}, u32[]{:S(2)}, u32[]{:S(2)}) collective-permute-start(bf16[2,1,32,1024]{3,2,1,0:T(8,128)(2,1)S(1)} %get-tuple-element.72), channel_id=1, source_target_pairs={{0,2},{1,3},{2,0},{3,1},{4,6},{5,7},{6,4},{7,5},{8,10},{9,11},{10,... | collective-permute-start | bytes 393224 | tf_op jit(solution)/shard_map/ppermute | solution.py:31
  32.7 8.6 %collective-permute-start.10 = (bf16[64,1024]{1,0:T(8,128)(2,1)S(1)}, bf16[64,1024]{1,0:T(8,128)(2,1)S(1)}, u32[]{:S(2)}, u32[]{:S(2)}) collective-permute-start(bf16[64,1024]{1,0:T(8,128)(2,1)S(1)} %shard_map.71), channel_id=1, source_target_pairs={{0,16},{1,17},{2,18},{3,19},{4,20},{5,21},{6,22},{7,23},{8,24},{9,... | collective-permute-start | bytes 393224 | tf_op jit(solution)/shard_map/ppermute | solution.py:31
  42.6 8.6 %collective-permute-start.15 = (bf16[28,32,128]{2,1,0:T(8,128)(2,1)S(1)}, bf16[28,32,128]{2,1,0:T(8,128)(2,1)S(1)}, u32[]{:S(2)}, u32[]{:S(2)}) collective-permute-start(bf16[28,32,128]{2,1,0:T(8,128)(2,1)S(1)} %slice.15), channel_id=1, source_target_pairs={{0,8},{1,9},{2,10},{3,11},{4,0},{5,1},{6,2},{7,3},{8,12},{9,13},{1... | collective-permute-start | bytes 688136 | tf_op jit(solution)/shard_map/ppermute | solution.py:31
  44.0 12.0 %collective-permute-start.14 = (bf16[28,32,128]{2,1,0:T(8,128)(2,1)S(1)}, bf16[28,32,128]{2,1,0:T(8,128)(2,1)S(1)}, u32[]{:S(2)}, u32[]{:S(2)}) collective-permute-start(bf16[28,32,128]{2,1,0:T(8,128)(2,1)S(1)} %slice.14), channel_id=1, source_target_pairs={{0,4},{1,5},{2,6},{3,7},{4,12},{5,13},{6,14},{7,15},{8,0},{9,1},{1... | collective-permute-start | bytes 688136 | tf_op jit(solution)/shard_map/ppermute | solution.py:31
  45.5 11.2 %collective-permute-start.17 = (bf16[32,32,128]{2,1,0:T(8,128)(2,1)S(1)}, bf16[32,32,128]{2,1,0:T(8,128)(2,1)S(1)}, u32[]{:S(2)}, u32[]{:S(2)}) collective-permute-start(bf16[32,32,128]{2,1,0:T(8,128)(2,1)S(1)} %get-tuple-element.80), channel_id=1, source_target_pairs={{0,2},{1,3},{2,0},{3,1},{4,6},{5,7},{6,4},{7,5},{8,10},{9,11},{10,... | collective-permute-start | bytes 786440 | tf_op jit(solution)/shard_map/ppermute | solution.py:31
  47.1 9.6 %collective-permute-start.18 = (bf16[64,1024]{1,0:T(8,128)(2,1)S(1)}, bf16[64,1024]{1,0:T(8,128)(2,1)S(1)}, u32[]{:S(2)}, u32[]{:S(2)}) collective-permute-start(bf16[64,1024]{1,0:T(8,128)(2,1)S(1)} %get-tuple-element.83), channel_id=1, source_target_pairs={{0,1},{1,0},{2,3},{3,2},{4,5},{5,4},{6,7},{7,6},{8,9},{9,8},{10,11... | collective-permute-start | bytes 393224 | tf_op jit(solution)/shard_map/ppermute | solution.py:31
  47.1 9.6 %collective-permute-start.19 = (bf16[64,1024]{1,0:T(8,128)(2,1)S(1)}, bf16[64,1024]{1,0:T(8,128)(2,1)S(1)}, u32[]{:S(2)}, u32[]{:S(2)}) collective-permute-start(bf16[64,1024]{1,0:T(8,128)(2,1)S(1)} %get-tuple-element.84), channel_id=1, source_target_pairs={{0,3},{1,2},{2,1},{3,0},{4,7},{5,6},{6,5},{7,4},{8,11},{9,10},{10,... | collective-permute-start | bytes 393224 | tf_op jit(solution)/shard_map/ppermute | solution.py:31
  56.9 1.6 %collective-permute-start.20 = (bf16[2,2,32,1024]{3,2,1,0:T(8,128)(2,1)S(1)}, bf16[2,2,32,1024]{3,2,1,0:T(8,128)(2,1)S(1)}, u32[]{:S(2)}, u32[]{:S(2)}) collective-permute-start(bf16[2,2,32,1024]{3,2,1,0:T(8,128)(2,1)S(1)} %get-tuple-element.86), channel_id=1, source_target_pairs={{0,1},{1,0},{2,3},{3,2},{4,5},{5,4},{6,7},{7,6},{8,9},{9,8},{10,11... | collective-permute-start | bytes 786440 | tf_op jit(solution)/shard_map/ppermute | solution.py:31
  56.9 11.6 %collective-permute-start.26 = (bf16[64,32,128]{2,1,0:T(8,128)(2,1)S(1)}, bf16[64,32,128]{2,1,0:T(8,128)(2,1)S(1)}, u32[]{:S(2)}, u32[]{:S(2)}) collective-permute-start(bf16[64,32,128]{2,1,0:T(8,128)(2,1)S(1)} %shard_map.79.refs_0_), channel_id=1, source_target_pairs={{0,1},{1,0},{2,3},{3,2},{4,5},{5,4},{6,7},{7,6},{8,9},{9,8},{10,11... | collective-permute-start | bytes 1572872 | tf_op jit(solution)/shard_map/ppermute | solution.py:31
  57.4 5.5 %collective-permute-start.22 = (bf16[64,1024]{1,0:T(8,128)(2,1)S(1)}, bf16[64,1024]{1,0:T(8,128)(2,1)S(1)}, u32[]{:S(2)}, u32[]{:S(2)}) collective-permute-start(bf16[64,1024]{1,0:T(8,128)(2,1)S(1)} %shard_map.81), channel_id=1, source_target_pairs={{0,16},{1,17},{2,18},{3,19},{4,20},{5,21},{6,22},{7,23},{8,24},{9,... | collective-permute-start | bytes 393224 | tf_op jit(solution)/shard_map/ppermute | solution.py:31
  58.5 5.6 %collective-permute-start.21 = (bf16[2,1,32,1024]{3,2,1,0:T(8,128)(2,1)S(1)}, bf16[2,1,32,1024]{3,2,1,0:T(8,128)(2,1)S(1)}, u32[]{:S(2)}, u32[]{:S(2)}) collective-permute-start(bf16[2,1,32,1024]{3,2,1,0:T(8,128)(2,1)S(1)} %get-tuple-element.88), channel_id=1, source_target_pairs={{0,2},{1,3},{2,0},{3,1},{4,6},{5,7},{6,4},{7,5},{8,10},{9,11},{10,... | collective-permute-start | bytes 393224 | tf_op jit(solution)/shard_map/ppermute | solution.py:31
  60.1 8.4 %collective-permute-start.27 = (bf16[32,32,128]{2,1,0:T(8,128)(2,1)S(1)}, bf16[32,32,128]{2,1,0:T(8,128)(2,1)S(1)}, u32[]{:S(2)}, u32[]{:S(2)}) collective-permute-start(bf16[32,32,128]{2,1,0:T(8,128)(2,1)S(1)} %shard_map.85.refs_2_), channel_id=1, source_target_pairs={{0,1},{1,0},{2,3},{3,2},{4,5},{5,4},{6,7},{7,6},{8,9},{9,8},{10,11... | collective-permute-start | bytes 786440 | tf_op jit(solution)/shard_map/ppermute | solution.py:31
  64.2 8.0 %collective-permute-start.25 = (bf16[64,1024]{1,0:T(8,128)(2,1)S(1)}, bf16[64,1024]{1,0:T(8,128)(2,1)S(1)}, u32[]{:S(2)}, u32[]{:S(2)}) collective-permute-start(bf16[64,1024]{1,0:T(8,128)(2,1)S(1)} %pad_maximum_fusion.1), channel_id=1, source_target_pairs={{0,16},{1,17},{2,18},{3,19},{4,20},{5,21},{6,22},{7,23},{8,24},{9,... | collective-permute-start | bytes 393224 | tf_op jit(solution)/shard_map/ppermute | solution.py:31
  64.9 8.7 %collective-permute-start.24 = (bf16[64,1024]{1,0:T(8,128)(2,1)S(1)}, bf16[64,1024]{1,0:T(8,128)(2,1)S(1)}, u32[]{:S(2)}, u32[]{:S(2)}) collective-permute-start(bf16[64,1024]{1,0:T(8,128)(2,1)S(1)} %pad_maximum_fusion), channel_id=1, source_target_pairs={{0,16},{1,17},{2,18},{3,19},{4,20},{5,21},{6,22},{7,23},{8,24},{9,... | collective-permute-start | bytes 393224 | tf_op jit(solution)/shard_map/ppermute | solution.py:31
  66.4 7.3 %collective-permute-start.23 = (bf16[64,1024]{1,0:T(8,128)(2,1)S(1)}, bf16[64,1024]{1,0:T(8,128)(2,1)S(1)}, u32[]{:S(2)}, u32[]{:S(2)}) collective-permute-start(bf16[64,1024]{1,0:T(8,128)(2,1)S(1)} %collective-permute-done.22), channel_id=1, source_target_pairs={{0,12},{1,13},{2,14},{3,15},{4,8},{5,9},{6,10},{7,11},{8,4},{9,5},... | collective-permute-start | bytes 393224 | tf_op jit(solution)/shard_map/ppermute | solution.py:31

commit v5 on v4

--- a/solution.py
+++ b/solution.py
@@ -200,22 +200,28 @@
         at += n
 
 
-def weight_kernel(order, pairs, scale, xs, *refs):
-    inputs, rest = refs[: 2 * xs], refs[2 * xs :]
+def crossed_kernel(mine, got, first, second, above, below):
+    half = first.shape[0]
+    total = added(mine[...], got[...]).reshape(-1, first.shape[1])
+    above[:half], above[half:] = total[:half], second[...]
+    below[:half], below[half:] = first[...], total[half:]
+
+
+def weight_kernel(groups, pairs, scale, count, *refs):
+    inputs, rest = refs[:count], refs[count:]
     *rest, out, right = rest
-    count = 1 + max(p[0] for p in pairs)
-    parts, so_far = rest[:count], rest[count:]
+    many = 1 + max(p[0] for p in pairs)
+    parts, so_far = rest[:many], rest[many:]
     half = parts[0].shape[1]
     hidden = out.shape[1]
-    shards = 2 * len(order)
-    blocks = [(i, j, other) for other in (0, 1) for i, j in enumerate(order)]
+    shards = len(groups[0])
 
     @pl.when(pl.program_id(0) == 0)
     def _():
         row = 0
         for part, at, _, _ in pairs:
-            for _, j, other in blocks:
-                shard = lax.axis_index("tensor") ^ j ^ other
+            for j in range(shards):
+                shard = lax.axis_index("tensor") ^ j
                 for c in range(hidden // LANES):
                     right[pl.ds(row, half), pl.ds(c * LANES, LANES)] = parts[part][at + c * shards + shard]
                 row += half
@@ -223,13 +229,11 @@
     tile = out.shape[0]
     first = pl.program_id(0) * (tile // LANES)
     left = []
-    for _, _, x, at in pairs:
-        for i, _, other in blocks:
-            block = inputs[2 * x + other]
-            start = i * (block.shape[0] // len(order)) + at
-            left.append(
-                jnp.concatenate([block[start + 2 * (first + c)] for c in range(tile // LANES)], axis=1)
-            )
+    for _, _, group, at in pairs:
+        for j in range(shards):
+            block, start = groups[group][j]
+            columns = [inputs[block][start + at + 2 * (first + c)] for c in range(tile // LANES)]
+            left.append(jnp.concatenate(columns, axis=1))
     total = lax.dot_general(jnp.concatenate(left), right[...], TN, preferred_element_type=F32)
     for already in so_far:
         total += already[pl.ds(pl.multiple_of(pl.program_id(0) * tile, tile), tile)]
@@ -336,7 +340,18 @@
     tile = 256
 
     def weight_product(xs, pairs, parts, *so_far, final):
-        kernel = functools.partial(weight_kernel, order, pairs, replicas if final else 1, len(xs))
+        groups, at = [], 0
+        for x in xs:
+            group = [None] * shards
+            for i, j in enumerate(order):
+                for other in (0, 1):
+                    if len(x) == 2:
+                        group[j ^ other] = (at + other, i * (x[0].shape[0] // len(order)))
+                    else:
+                        group[j ^ other] = (at + (j ^ other), 0)
+            groups.append(group)
+            at += len(x)
+        kernel = functools.partial(weight_kernel, groups, pairs, replicas if final else 1, at)
         return call(
             kernel,
             [jax.ShapeDtypeStruct((width, hidden), BF16 if final else F32)],
@@ -388,7 +403,12 @@
     keep, give = fold(2, keep_a, across(give_a, 1), keep_b, across(give_b, 1))
     nears = finished(keep, across(give, 2), 1, 1)
     x_near = stacked(4 * x_count, [(i, 0, 2 * x_count, 2 * i * x_count, 1) for i in range(2)], a, b)
-    x_near = doubled(x_near, far_step, steps - 1)
+    x_near, step = {0: x_near}, far_step
+    while step > 1:
+        x_near |= {j + step: across(v, step) for j, v in x_near.items()}
+        step //= 2
+    blocks = sorted(x_near)
+    x_near = [x_near[j] for j in blocks]
 
     at -= 2 * x_count
     weight_grad = weight_product(
@@ -399,7 +419,7 @@
     b_parts.append(b)
     ats.append(at)
     a_next, b_next = up(a[x_count:]), down(b[x_count:])
-    far_a, far_b, x_near = together(a, b, x_near)
+    far_a, far_b, *x_near = together(a, b, *x_near)
     riders = [(i, 0, x_count, i, 2) for i in range(2)]
     (out,), x_far = summed([(far_a, at), (far_b, at)], [2], far_step, riders)
 
@@ -414,7 +434,7 @@
     two = returned(out, 0)
     keep, give = fold(2, keep, across(give, 1))
     got = across(give, 2)
-    x_near = [x_near, across(x_near, 1)]
+    x_near = [v for pair in ((v, across(v, 1)) for v in x_near) for v in pair]
     places = [(i, 0, x_count, i, 2) for i in range(2)] + [(2, 2 * x_count, 2 * x_count, 2 * x_count, 1)]
     x_far = stacked(4 * x_count, places, a_parts[2], b_parts[2], x_far)
     x_far = doubled(x_far, far_step // 2, steps - 2)
@@ -422,12 +442,17 @@
 
     parts = [v for pair_of in zip(a_parts, b_parts) for v in pair_of]
     keep, got, two = together(keep, got, two)
+    step = 4
+    while step < shards:
+        keep, give = fold(step, keep, got)
+        got = across(give, step)
+        step *= 2
+    above, below = call(crossed_kernel, [(rows, width)] * 2, keep, got, *nears)
+    out = above
+    above, below = returned(above, -1), returned(below, 1)
     two = moved(
         two, sizes, lambda s, i, j: (s, shifted(i, -2, replicas), j) if s < sections - 1 else (s, i, j ^ 1)
     )
-    out_a, out = finished(keep, got, 1, 1)
-    above = returned(jnp.concatenate([out_a, nears[1]]), -1)
-    below = returned(jnp.concatenate([nears[0], out]), 1)
 
     weight_grad, _ = together(weight_grad, out)
     weight_grad = weight_product(
@@ -445,6 +470,7 @@
         final=True,
     )
     passed, weight_grad = together(passed, weight_grad)
+    passed, above, below = together(passed, above, below)
     passed = call(
         functools.partial(last_kernel, [2, last, 1]),
         [passed.shape],

time: 74.6 us -> 74 us (level)
  waiting for transfers between devices: 33.9 us -> 31.4 us
  starting transfers between devices: 26.2 us -> 28.2 us
    ppermute x28 -> x29, waiting for transfers between devices: 33.9 us -> 31.4 us  [moved(): return lax.ppermute(value, AXES, pairs)]
    ppermute x28 -> x29, starting transfers between devices: 26.2 us -> 28.2 us  [moved(): return lax.ppermute(value, AXES, pairs)]
    pallas_call x20 -> x19, Pallas kernels: 11.9 us -> 11.8 us  [call(): pl.pallas_call(kernel, out_shape=[v if hasattr(v, 'dtype') else jax.Shape...]
  transfers between devices with their start and end apart: 28 -> 29, of which waited for: 12 -> 12; matrix products, arithmetic and copies ran while one was open for 0% -> 0% of each run, Pallas kernels for 13% -> 13%
where the time goes in v5:
time: 74 us; the launch traced here: 73.8 us
  waiting for transfers between devices  31.4 us (42%)
  starting transfers between devices  28.2 us (38%)
  Pallas kernels  11.8 us (16%)
  local copies, waits for them, and re-layouts  1.57 us (2%)
  between operations  0.84 us (1%)
    ppermute x29, waiting for transfers between devices, moved(): return lax.ppermute(value, AXES, pairs)  31.4 us
    ppermute x29, starting transfers between devices, moved(): return lax.ppermute(value, AXES, pairs)  28.2 us
    pallas_call x19, Pallas kernels, call(): pl.pallas_call(kernel, out_shape=[v if hasattr(v, 'dtype') else jax.Shape...  11.8 us
    unnamed x2, local copies, waits for them, and re-layouts  1.5 us
  transfers between devices with their start and end apart: 29, of which 12 were waited for; matrix products, arithmetic and copies ran while one was open for 0% of the time, Pallas kernels for 13%

profile of v5, /device:TPU:0, one launch (start us, length us, event | category | flops | bytes accessed | tf_op | source)
XLA Modules:
  0.0 73.8 jit_solution(1783446120163366767)
XLA Ops:
  0.6 1.6 %shard_map.68 = (bf16[52,32,128]{2,1,0:T(8,128)(2,1)S(1)}, bf16[52,32,128]{2,1,0:T(8,128)(2,1)S(1)}, bf16[16,32,128]{2,1,0:T(8,128)(2,1)S(1)}) custom-call(bf16[256,896]{1,0:T(8,128)(2,1)} %bitcast.11, bf16[256,896]{1,0:T(8,128)(2,1)} %bitcast.12, bf16[64,4096]{1,0:T(8,128)(2,1)} %bitcast.10), custom_call_target="tpu_custom_call" | custom-call | tf_op jit(solution)/shard_map/pallas_call | solution.py:50
  2.3 3.0 %collective-permute-start.2 = (bf16[64,4096]{1,0:T(8,128)(2,1)}, bf16[64,4096]{1,0:T(8,128)(2,1)S(1)}, u32[]{:S(2)}, u32[]{:S(2)}) collective-permute-start(bf16[64,4096]{1,0:T(8,128)(2,1)} %bitcast.13), channel_id=1, source_target_pairs={{0,16},{1,17},{2,18},{3,19},{4,20},{5,21},{6,22},{7,23},{8,24},{9,... | collective-permute-start | bytes 1572872 | tf_op jit(solution)/shard_map/ppermute | solution.py:31
  5.3 1.6 %collective-permute-start = (bf16[52,32,128]{2,1,0:T(8,128)(2,1)S(1)}, bf16[52,32,128]{2,1,0:T(8,128)(2,1)S(1)}, u32[]{:S(2)}, u32[]{:S(2)}) collective-permute-start(bf16[52,32,128]{2,1,0:T(8,128)(2,1)S(1)} %get-tuple-element.57.refs_0_.refs_2_), channel_id=1, source_target_pairs={{0,4},{1,5},{2,6},{3,7},{4,12},{5,13},{6,14},{7,15},{8,0},{9,1},{1... | collective-permute-start | bytes 1277960 | tf_op jit(solution)/shard_map/ppermute | solution.py:31
  6.9 1.3 %collective-permute-start.1 = (bf16[52,32,128]{2,1,0:T(8,128)(2,1)S(1)}, bf16[52,32,128]{2,1,0:T(8,128)(2,1)S(1)}, u32[]{:S(2)}, u32[]{:S(2)}) collective-permute-start(bf16[52,32,128]{2,1,0:T(8,128)(2,1)S(1)} %get-tuple-element.58.refs_1_.refs_3_), channel_id=1, source_target_pairs={{0,8},{1,9},{2,10},{3,11},{4,0},{5,1},{6,2},{7,3},{8,12},{9,13},{1... | collective-permute-start | bytes 1277960 | tf_op jit(solution)/shard_map/ppermute | solution.py:31
  8.2 1.5 %collective-permute-start.6 = (bf16[16,32,128]{2,1,0:T(8,128)(2,1)S(1)}, bf16[16,32,128]{2,1,0:T(8,128)(2,1)S(1)}, u32[]{:S(2)}, u32[]{:S(2)}) collective-permute-start(bf16[16,32,128]{2,1,0:T(8,128)(2,1)S(1)} %get-tuple-element.64.refs_0_), channel_id=1, source_target_pairs={{0,2},{1,3},{2,0},{3,1},{4,6},{5,7},{6,4},{7,5},{8,10},{9,11},{10,... | collective-permute-start | bytes 393224 | tf_op jit(solution)/shard_map/ppermute | solution.py:31
  9.7 1.5 %copy-done = bf16[1,1024,896]{2,1,0:T(8,128)(2,1)S(1)} copy-done((bf16[1,1024,896]{2,1,0:T(8,128)(2,1)S(1)}, bf16[1,1024,896]{2,1,0:T(8,128)(2,1)}, u32[]{:S(2)}) %copy-start) | copy-done | bytes 1835032
  11.4 0.7 %shard_map.70 = (bf16[64,1024]{1,0:T(8,128)(2,1)S(1)}, bf16[64,1024]{1,0:T(8,128)(2,1)S(1)}, bf16[64,1024]{1,0:T(8,128)(2,1)S(1)}, bf16[64,1024]{1,0:T(8,128)(2,1)S(1)}) custom-call(bf16[52,32,128]{2,1,0:T(8,128)(2,1)S(1)} %get-tuple-element.57.refs_0_.refs_2_, bf16[52,32,128]{2,1,0:T(8,128)(2,1)S(1)} %get-tuple-element.58.refs_1_.refs_3_, ...), custom_call_target="tpu_custom_call" | custom-call | tf_op jit(solution)/shard_map/pallas_call | solution.py:50
  12.2 1.0 %collective-permute-done.6.refs_1_ = bf16[16,32,128]{2,1,0:T(8,128)(2,1)S(1)} collective-permute-done((bf16[16,32,128]{2,1,0:T(8,128)(2,1)S(1)}, bf16[16,32,128]{2,1,0:T(8,128)(2,1)S(1)}, u32[]{:S(2)}, u32[]{:S(2)}) %collective-permute-start.6) | collective-permute-done | bytes 131104 | tf_op jit(solution)/shard_map/ppermute | solution.py:31
  13.2 1.5 %collective-permute-start.4 = (bf16[64,1024]{1,0:T(8,128)(2,1)S(1)}, bf16[64,1024]{1,0:T(8,128)(2,1)S(1)}, u32[]{:S(2)}, u32[]{:S(2)}) collective-permute-start(bf16[64,1024]{1,0:T(8,128)(2,1)S(1)} %get-tuple-element.62), channel_id=1, source_target_pairs={{0,2},{1,3},{2,0},{3,1},{4,6},{5,7},{6,4},{7,5},{8,10},{9,11},{10,... | collective-permute-start | bytes 393224 | tf_op jit(solution)/shard_map/ppermute | solution.py:31
  14.8 3.3 %collective-permute-done.4.refs_2_ = bf16[64,1024]{1,0:T(8,128)(2,1)S(1)} collective-permute-done((bf16[64,1024]{1,0:T(8,128)(2,1)S(1)}, bf16[64,1024]{1,0:T(8,128)(2,1)S(1)}, u32[]{:S(2)}, u32[]{:S(2)}) %collective-permute-start.4) | collective-permute-done | bytes 131104 | tf_op jit(solution)/shard_map/ppermute | solution.py:31
  18.2 5.7 %collective-permute-done.5.refs_3_ = bf16[64,1024]{1,0:T(8,128)(2,1)S(1)} collective-permute-done((bf16[64,1024]{1,0:T(8,128)(2,1)S(1)}, bf16[64,1024]{1,0:T(8,128)(2,1)S(1)}, u32[]{:S(2)}, u32[]{:S(2)}) %collective-permute-start.5) | collective-permute-done | bytes 131104 | tf_op jit(solution)/shard_map/ppermute | solution.py:31
  24.0 2.6 %collective-permute-done.1.refs_1_.refs_7_ = bf16[52,32,128]{2,1,0:T(8,128)(2,1)S(1)} collective-permute-done((bf16[52,32,128]{2,1,0:T(8,128)(2,1)S(1)}, bf16[52,32,128]{2,1,0:T(8,128)(2,1)S(1)}, u32[]{:S(2)}, u32[]{:S(2)}) %collective-permute-start.1) | collective-permute-done | bytes 426016 | tf_op jit(solution)/shard_map/ppermute | solution.py:31
  26.6 1.7 %collective-permute-start.8 = (bf16[36,32,128]{2,1,0:T(8,128)(2,1)S(1)}, bf16[36,32,128]{2,1,0:T(8,128)(2,1)S(1)}, u32[]{:S(2)}, u32[]{:S(2)}) collective-permute-start(bf16[36,32,128]{2,1,0:T(8,128)(2,1)S(1)} %slice.12), channel_id=1, source_target_pairs={{0,4},{1,5},{2,6},{3,7},{4,12},{5,13},{6,14},{7,15},{8,0},{9,1},{1... | collective-permute-start | bytes 884744 | tf_op jit(solution)/shard_map/ppermute | solution.py:31
  28.4 1.3 %collective-permute-start.9 = (bf16[36,32,128]{2,1,0:T(8,128)(2,1)S(1)}, bf16[36,32,128]{2,1,0:T(8,128)(2,1)S(1)}, u32[]{:S(2)}, u32[]{:S(2)}) collective-permute-start(bf16[36,32,128]{2,1,0:T(8,128)(2,1)S(1)} %slice.13), channel_id=1, source_target_pairs={{0,8},{1,9},{2,10},{3,11},{4,0},{5,1},{6,2},{7,3},{8,12},{9,13},{1... | collective-permute-start | bytes 884744 | tf_op jit(solution)/shard_map/ppermute | solution.py:31
  31.0 1.6 %collective-permute-start.16 = (bf16[32,32,128]{2,1,0:T(8,128)(2,1)S(1)}, bf16[32,32,128]{2,1,0:T(8,128)(2,1)S(1)}, u32[]{:S(2)}, u32[]{:S(2)}) collective-permute-start(bf16[32,32,128]{2,1,0:T(8,128)(2,1)S(1)} %shard_map.78.refs_0_), channel_id=1, source_target_pairs={{0,2},{1,3},{2,0},{3,1},{4,6},{5,7},{6,4},{7,5},{8,10},{9,11},{10,... | collective-permute-start | bytes 786440 | tf_op jit(solution)/shard_map/ppermute | solution.py:31
  32.7 1.0 %collective-permute-start.13 = (bf16[2,1,32,1024]{3,2,1,0:T(8,128)(2,1)S(1)}, bf16[2,1,32,1024]{3,2,1,0:T(8,128)(2,1)S(1)}, u32[]{:S(2)}, u32[]{:S(2)}) collective-permute-start(bf16[2,1,32,1024]{3,2,1,0:T(8,128)(2,1)S(1)} %get-tuple-element.76), channel_id=1, source_target_pairs={{0,2},{1,3},{2,0},{3,1},{4,6},{5,7},{6,4},{7,5},{8,10},{9,11},{10,... | collective-permute-start | bytes 393224 | tf_op jit(solution)/shard_map/ppermute | solution.py:31
  34.2 1.4 %shard_map.73.refs_12_ = f32[1024,896]{1,0:T(8,128)S(1)} custom-call(bf16[32,32,128]{2,1,0:T(8,128)(2,1)S(1)} %shard_map.72.refs_0_, bf16[32,32,128]{2,1,0:T(8,128)(2,1)S(1)} %collective-permute-done.7.refs_1_, bf16[52,32,128]{2,1,0:T(8,128)(2,1)S(1)} %get-tuple-element.57.refs_0_.refs_2_, bf16[52,32,128]{2,1,0:T(8,128)(2,1)S(1)} %get-tuple-element.58.refs_1_.refs_3_), custom_call_target="tpu_custom_call" | custom-call | tf_op jit(solution)/shard_map/pallas_call | solution.py:50
  35.6 6.6 %collective-permute-done.13.got = bf16[2,1,32,1024]{3,2,1,0:T(8,128)(2,1)S(1)} collective-permute-done((bf16[2,1,32,1024]{3,2,1,0:T(8,128)(2,1)S(1)}, bf16[2,1,32,1024]{3,2,1,0:T(8,128)(2,1)S(1)}, u32[]{:S(2)}, u32[]{:S(2)}) %collective-permute-start.13) | collective-permute-done | bytes 131104 | tf_op jit(solution)/shard_map/ppermute | solution.py:31
  42.9 0.7 %collective-permute-start.14 = (bf16[28,32,128]{2,1,0:T(8,128)(2,1)S(1)}, bf16[28,32,128]{2,1,0:T(8,128)(2,1)S(1)}, u32[]{:S(2)}, u32[]{:S(2)}) collective-permute-start(bf16[28,32,128]{2,1,0:T(8,128)(2,1)S(1)} %slice.14), channel_id=1, source_target_pairs={{0,4},{1,5},{2,6},{3,7},{4,12},{5,13},{6,14},{7,15},{8,0},{9,1},{1... | collective-permute-start | bytes 688136 | tf_op jit(solution)/shard_map/ppermute | solution.py:31
  43.7 2.3 %collective-permute-start.15 = (bf16[28,32,128]{2,1,0:T(8,128)(2,1)S(1)}, bf16[28,32,128]{2,1,0:T(8,128)(2,1)S(1)}, u32[]{:S(2)}, u32[]{:S(2)}) collective-permute-start(bf16[28,32,128]{2,1,0:T(8,128)(2,1)S(1)} %slice.15), channel_id=1, source_target_pairs={{0,8},{1,9},{2,10},{3,11},{4,0},{5,1},{6,2},{7,3},{8,12},{9,13},{1... | collective-permute-start | bytes 688136 | tf_op jit(solution)/shard_map/ppermute | solution.py:31
  46.7 1.6 %collective-permute-start.17 = (bf16[32,32,128]{2,1,0:T(8,128)(2,1)S(1)}, bf16[32,32,128]{2,1,0:T(8,128)(2,1)S(1)}, u32[]{:S(2)}, u32[]{:S(2)}) collective-permute-start(bf16[32,32,128]{2,1,0:T(8,128)(2,1)S(1)} %get-tuple-element.84), channel_id=1, source_target_pairs={{0,2},{1,3},{2,0},{3,1},{4,6},{5,7},{6,4},{7,5},{8,10},{9,11},{10,... | collective-permute-start | bytes 786440 | tf_op jit(solution)/shard_map/ppermute | solution.py:31
  48.9 0.9 %shard_map.81.refs_3_ = bf16[64,4096]{1,0:T(8,128)(2,1)} custom-call(bf16[64,4096]{1,0:T(8,128)(2,1)S(1)} %collective-permute-done.2.base, bf16[64,1024]{1,0:T(8,128)(2,1)S(1)} %collective-permute-done.10.piece), custom_call_target="tpu_custom_call" | custom-call | tf_op jit(solution)/shard_map/pallas_call | solution.py:50
  49.8 1.9 %collective-permute-done.14.refs_0_.refs_10_ = bf16[28,32,128]{2,1,0:T(8,128)(2,1)S(1)} collective-permute-done((bf16[28,32,128]{2,1,0:T(8,128)(2,1)S(1)}, bf16[28,32,128]{2,1,0:T(8,128)(2,1)S(1)}, u32[]{:S(2)}, u32[]{:S(2)}) %collective-permute-start.14) | collective-permute-done | bytes 229408 | tf_op jit(solution)/shard_map/ppermute | solution.py:31
  51.6 3.8 %collective-permute-done.15.refs_1_.refs_11_ = bf16[28,32,128]{2,1,0:T(8,128)(2,1)S(1)} collective-permute-done((bf16[28,32,128]{2,1,0:T(8,128)(2,1)S(1)}, bf16[28,32,128]{2,1,0:T(8,128)(2,1)S(1)}, u32[]{:S(2)}, u32[]{:S(2)}) %collective-permute-start.15) | collective-permute-done | bytes 229408 | tf_op jit(solution)/shard_map/ppermute | solution.py:31
  58.0 1.6 %collective-permute-start.21 = (bf16[2,1,32,1024]{3,2,1,0:T(8,128)(2,1)S(1)}, bf16[2,1,32,1024]{3,2,1,0:T(8,128)(2,1)S(1)}, u32[]{:S(2)}, u32[]{:S(2)}) collective-permute-start(bf16[2,1,32,1024]{3,2,1,0:T(8,128)(2,1)S(1)} %get-tuple-element.92), channel_id=1, source_target_pairs={{0,2},{1,3},{2,0},{3,1},{4,6},{5,7},{6,4},{7,5},{8,10},{9,11},{10,... | collective-permute-start | bytes 393224 | tf_op jit(solution)/shard_map/ppermute | solution.py:31
  60.1 2.2 %collective-permute-done.22 = bf16[64,1024]{1,0:T(8,128)(2,1)S(1)} collective-permute-done((bf16[64,1024]{1,0:T(8,128)(2,1)S(1)}, bf16[64,1024]{1,0:T(8,128)(2,1)S(1)}, u32[]{:S(2)}, u32[]{:S(2)}) %collective-permute-start.22) | collective-permute-done | bytes 131104 | tf_op jit(solution)/shard_map/ppermute | solution.py:31
  62.3 1.2 %collective-permute-done.21.got = bf16[2,1,32,1024]{3,2,1,0:T(8,128)(2,1)S(1)} collective-permute-done((bf16[2,1,32,1024]{3,2,1,0:T(8,128)(2,1)S(1)}, bf16[2,1,32,1024]{3,2,1,0:T(8,128)(2,1)S(1)}, u32[]{:S(2)}, u32[]{:S(2)}) %collective-permute-start.21) | collective-permute-done | bytes 131104 | tf_op jit(solution)/shard_map/ppermute | solution.py:31
  64.3 1.8 %collective-permute-start.28 = (bf16[64,1024]{1,0:T(8,128)(2,1)S(1)}, bf16[64,1024]{1,0:T(8,128)(2,1)S(1)}, u32[]{:S(2)}, u32[]{:S(2)}) collective-permute-start(bf16[64,1024]{1,0:T(8,128)(2,1)S(1)} %get-tuple-element.107), channel_id=1, source_target_pairs={{0,16},{1,17},{2,18},{3,19},{4,20},{5,21},{6,22},{7,23},{8,24},{9,... | collective-permute-start | bytes 393224 | tf_op jit(solution)/shard_map/ppermute | solution.py:31
  66.2 1.4 %collective-permute-start.23 = (bf16[64,1024]{1,0:T(8,128)(2,1)S(1)}, bf16[64,1024]{1,0:T(8,128)(2,1)S(1)}, u32[]{:S(2)}, u32[]{:S(2)}) collective-permute-start(bf16[64,1024]{1,0:T(8,128)(2,1)S(1)} %collective-permute-done.22), channel_id=1, source_target_pairs={{0,12},{1,13},{2,14},{3,15},{4,8},{5,9},{6,10},{7,11},{8,4},{9,5},... | collective-permute-start | bytes 393224 | tf_op jit(solution)/shard_map/ppermute | solution.py:31
  67.5 3.6 %shard_map.85 = bf16[1024,896]{1,0:T(8,128)(2,1)} custom-call(bf16[32,32,128]{2,1,0:T(8,128)(2,1)S(1)} %shard_map.78.refs_0_, bf16[32,32,128]{2,1,0:T(8,128)(2,1)S(1)} %collective-permute-done.24.refs_1_, bf16[32,32,128]{2,1,0:T(8,128)(2,1)S(1)} %collective-permute-done.16.refs_2_, bf16[32,32,128]{2,1,0:T(8,128)(2,1)S(1)} %collective-permute-done.25.refs_3_, ...), custom_call_target="tpu_custom_call" | custom-call | tf_op jit(solution)/shard_map/pallas_call | solution.py:50
  71.2 1.8 %collective-permute-done.27.refs_1_ = bf16[64,1024]{1,0:T(8,128)(2,1)S(1)} collective-permute-done((bf16[64,1024]{1,0:T(8,128)(2,1)S(1)}, bf16[64,1024]{1,0:T(8,128)(2,1)S(1)}, u32[]{:S(2)}, u32[]{:S(2)}) %collective-permute-start.27) | collective-permute-done | bytes 131104 | tf_op jit(solution)/shard_map/ppermute | solution.py:31
  73.0 0.8 %shard_map.86 = bf16[64,4096]{1,0:T(8,128)(2,1)} custom-call(bf16[64,4096]{1,0:T(8,128)(2,1)S(1)} %collective-permute-done.2.base, bf16[64,1024]{1,0:T(8,128)(2,1)S(1)} %collective-permute-done.23.refs_0_, bf16[64,1024]{1,0:T(8,128)(2,1)S(1)} %collective-permute-done.27.refs_1_, ...), custom_call_target="tpu_custom_call", output_to_operand_aliasing={{}: (4, {})} | custom-call | tf_op jit(solution)/shard_map/pallas_call | solution.py:50
  (51 shorter events, 8.3 us)
Async XLA Ops:
  2.3 24.3 %collective-permute-start.2 = (bf16[64,4096]{1,0:T(8,128)(2,1)}, bf16[64,4096]{1,0:T(8,128)(2,1)S(1)}, u32[]{:S(2)}, u32[]{:S(2)}) collective-permute-start(bf16[64,4096]{1,0:T(8,128)(2,1)} %bitcast.13), channel_id=1, source_target_pairs={{0,16},{1,17},{2,18},{3,19},{4,20},{5,21},{6,22},{7,23},{8,24},{9,... | collective-permute-start | bytes 1572872 | tf_op jit(solution)/shard_map/ppermute | solution.py:31
  5.3 18.7 %collective-permute-start = (bf16[52,32,128]{2,1,0:T(8,128)(2,1)S(1)}, bf16[52,32,128]{2,1,0:T(8,128)(2,1)S(1)}, u32[]{:S(2)}, u32[]{:S(2)}) collective-permute-start(bf16[52,32,128]{2,1,0:T(8,128)(2,1)S(1)} %get-tuple-element.57.refs_0_.refs_2_), channel_id=1, source_target_pairs={{0,4},{1,5},{2,6},{3,7},{4,12},{5,13},{6,14},{7,15},{8,0},{9,1},{1... | collective-permute-start | bytes 1277960 | tf_op jit(solution)/shard_map/ppermute | solution.py:31
  6.9 19.7 %collective-permute-start.1 = (bf16[52,32,128]{2,1,0:T(8,128)(2,1)S(1)}, bf16[52,32,128]{2,1,0:T(8,128)(2,1)S(1)}, u32[]{:S(2)}, u32[]{:S(2)}) collective-permute-start(bf16[52,32,128]{2,1,0:T(8,128)(2,1)S(1)} %get-tuple-element.58.refs_1_.refs_3_), channel_id=1, source_target_pairs={{0,8},{1,9},{2,10},{3,11},{4,0},{5,1},{6,2},{7,3},{8,12},{9,13},{1... | collective-permute-start | bytes 1277960 | tf_op jit(solution)/shard_map/ppermute | solution.py:31
  8.2 5.0 %collective-permute-start.6 = (bf16[16,32,128]{2,1,0:T(8,128)(2,1)S(1)}, bf16[16,32,128]{2,1,0:T(8,128)(2,1)S(1)}, u32[]{:S(2)}, u32[]{:S(2)}) collective-permute-start(bf16[16,32,128]{2,1,0:T(8,128)(2,1)S(1)} %get-tuple-element.64.refs_0_), channel_id=1, source_target_pairs={{0,2},{1,3},{2,0},{3,1},{4,6},{5,7},{6,4},{7,5},{8,10},{9,11},{10,... | collective-permute-start | bytes 393224 | tf_op jit(solution)/shard_map/ppermute | solution.py:31
  9.7 1.5 %copy-start = (bf16[1,1024,896]{2,1,0:T(8,128)(2,1)S(1)}, bf16[1,1024,896]{2,1,0:T(8,128)(2,1)}, u32[]{:S(2)}) copy-start(bf16[1,1024,896]{2,1,0:T(8,128)(2,1)} %param.9) | copy-start | bytes 5505028
  12.1 2.6 %collective-permute-start.3 = (bf16[64,1024]{1,0:T(8,128)(2,1)S(1)}, bf16[64,1024]{1,0:T(8,128)(2,1)S(1)}, u32[]{:S(2)}, u32[]{:S(2)}) collective-permute-start(bf16[64,1024]{1,0:T(8,128)(2,1)S(1)} %get-tuple-element.61), channel_id=1, source_target_pairs={{0,1},{1,0},{2,3},{3,2},{4,5},{5,4},{6,7},{7,6},{8,9},{9,8},{10,11... | collective-permute-start | bytes 393224 | tf_op jit(solution)/shard_map/ppermute | solution.py:31
  13.2 5.0 %collective-permute-start.4 = (bf16[64,1024]{1,0:T(8,128)(2,1)S(1)}, bf16[64,1024]{1,0:T(8,128)(2,1)S(1)}, u32[]{:S(2)}, u32[]{:S(2)}) collective-permute-start(bf16[64,1024]{1,0:T(8,128)(2,1)S(1)} %get-tuple-element.62), channel_id=1, source_target_pairs={{0,2},{1,3},{2,0},{3,1},{4,6},{5,7},{6,4},{7,5},{8,10},{9,11},{10,... | collective-permute-start | bytes 393224 | tf_op jit(solution)/shard_map/ppermute | solution.py:31
  14.7 9.2 %collective-permute-start.7 = (bf16[32,32,128]{2,1,0:T(8,128)(2,1)S(1)}, bf16[32,32,128]{2,1,0:T(8,128)(2,1)S(1)}, u32[]{:S(2)}, u32[]{:S(2)}) collective-permute-start(bf16[32,32,128]{2,1,0:T(8,128)(2,1)S(1)} %shard_map.72.refs_0_), channel_id=1, source_target_pairs={{0,1},{1,0},{2,3},{3,2},{4,5},{5,4},{6,7},{7,6},{8,9},{9,8},{10,11... | collective-permute-start | bytes 786440 | tf_op jit(solution)/shard_map/ppermute | solution.py:31
  18.1 5.7 %collective-permute-start.5 = (bf16[64,1024]{1,0:T(8,128)(2,1)S(1)}, bf16[64,1024]{1,0:T(8,128)(2,1)S(1)}, u32[]{:S(2)}, u32[]{:S(2)}) collective-permute-start(bf16[64,1024]{1,0:T(8,128)(2,1)S(1)} %get-tuple-element.63), channel_id=1, source_target_pairs={{0,3},{1,2},{2,1},{3,0},{4,7},{5,6},{6,5},{7,4},{8,11},{9,10},{10,... | collective-permute-start | bytes 393224 | tf_op jit(solution)/shard_map/ppermute | solution.py:31
  26.6 16.2 %collective-permute-start.8 = (bf16[36,32,128]{2,1,0:T(8,128)(2,1)S(1)}, bf16[36,32,128]{2,1,0:T(8,128)(2,1)S(1)}, u32[]{:S(2)}, u32[]{:S(2)}) collective-permute-start(bf16[36,32,128]{2,1,0:T(8,128)(2,1)S(1)} %slice.12), channel_id=1, source_target_pairs={{0,4},{1,5},{2,6},{3,7},{4,12},{5,13},{6,14},{7,15},{8,0},{9,1},{1... | collective-permute-start | bytes 884744 | tf_op jit(solution)/shard_map/ppermute | solution.py:31
  28.4 14.5 %collective-permute-start.9 = (bf16[36,32,128]{2,1,0:T(8,128)(2,1)S(1)}, bf16[36,32,128]{2,1,0:T(8,128)(2,1)S(1)}, u32[]{:S(2)}, u32[]{:S(2)}) collective-permute-start(bf16[36,32,128]{2,1,0:T(8,128)(2,1)S(1)} %slice.13), channel_id=1, source_target_pairs={{0,8},{1,9},{2,10},{3,11},{4,0},{5,1},{6,2},{7,3},{8,12},{9,13},{1... | collective-permute-start | bytes 884744 | tf_op jit(solution)/shard_map/ppermute | solution.py:31
  30.4 2.2 %collective-permute-start.11 = (bf16[1,2,32,1024]{3,2,1,0:T(8,128)(2,1)S(1)}, bf16[1,2,32,1024]{3,2,1,0:T(8,128)(2,1)S(1)}, u32[]{:S(2)}, u32[]{:S(2)}) collective-permute-start(bf16[1,2,32,1024]{3,2,1,0:T(8,128)(2,1)S(1)} %get-tuple-element.72), channel_id=1, source_target_pairs={{0,1},{1,0},{2,3},{3,2},{4,5},{5,4},{6,7},{7,6},{8,9},{9,8},{10,11... | collective-permute-start | bytes 393224 | tf_op jit(solution)/shard_map/ppermute | solution.py:31
  30.5 2.1 %collective-permute-start.12 = (bf16[1,2,32,1024]{3,2,1,0:T(8,128)(2,1)S(1)}, bf16[1,2,32,1024]{3,2,1,0:T(8,128)(2,1)S(1)}, u32[]{:S(2)}, u32[]{:S(2)}) collective-permute-start(bf16[1,2,32,1024]{3,2,1,0:T(8,128)(2,1)S(1)} %get-tuple-element.74), channel_id=1, source_target_pairs={{0,1},{1,0},{2,3},{3,2},{4,5},{5,4},{6,7},{7,6},{8,9},{9,8},{10,11... | collective-permute-start | bytes 393224 | tf_op jit(solution)/shard_map/ppermute | solution.py:31
  31.0 14.9 %collective-permute-start.16 = (bf16[32,32,128]{2,1,0:T(8,128)(2,1)S(1)}, bf16[32,32,128]{2,1,0:T(8,128)(2,1)S(1)}, u32[]{:S(2)}, u32[]{:S(2)}) collective-permute-start(bf16[32,32,128]{2,1,0:T(8,128)(2,1)S(1)} %shard_map.78.refs_0_), channel_id=1, source_target_pairs={{0,2},{1,3},{2,0},{3,1},{4,6},{5,7},{6,4},{7,5},{8,10},{9,11},{10,... | collective-permute-start | bytes 786440 | tf_op jit(solution)/shard_map/ppermute | solution.py:31
  32.7 9.5 %collective-permute-start.13 = (bf16[2,1,32,1024]{3,2,1,0:T(8,128)(2,1)S(1)}, bf16[2,1,32,1024]{3,2,1,0:T(8,128)(2,1)S(1)}, u32[]{:S(2)}, u32[]{:S(2)}) collective-permute-start(bf16[2,1,32,1024]{3,2,1,0:T(8,128)(2,1)S(1)} %get-tuple-element.76), channel_id=1, source_target_pairs={{0,2},{1,3},{2,0},{3,1},{4,6},{5,7},{6,4},{7,5},{8,10},{9,11},{10,... | collective-permute-start | bytes 393224 | tf_op jit(solution)/shard_map/ppermute | solution.py:31
  33.7 8.5 %collective-permute-start.10 = (bf16[64,1024]{1,0:T(8,128)(2,1)S(1)}, bf16[64,1024]{1,0:T(8,128)(2,1)S(1)}, u32[]{:S(2)}, u32[]{:S(2)}) collective-permute-start(bf16[64,1024]{1,0:T(8,128)(2,1)S(1)} %shard_map.71), channel_id=1, source_target_pairs={{0,16},{1,17},{2,18},{3,19},{4,20},{5,21},{6,22},{7,23},{8,24},{9,... | collective-permute-start | bytes 393224 | tf_op jit(solution)/shard_map/ppermute | solution.py:31
  42.9 8.8 %collective-permute-start.14 = (bf16[28,32,128]{2,1,0:T(8,128)(2,1)S(1)}, bf16[28,32,128]{2,1,0:T(8,128)(2,1)S(1)}, u32[]{:S(2)}, u32[]{:S(2)}) collective-permute-start(bf16[28,32,128]{2,1,0:T(8,128)(2,1)S(1)} %slice.14), channel_id=1, source_target_pairs={{0,4},{1,5},{2,6},{3,7},{4,12},{5,13},{6,14},{7,15},{8,0},{9,1},{1... | collective-permute-start | bytes 688136 | tf_op jit(solution)/shard_map/ppermute | solution.py:31
  43.7 11.8 %collective-permute-start.15 = (bf16[28,32,128]{2,1,0:T(8,128)(2,1)S(1)}, bf16[28,32,128]{2,1,0:T(8,128)(2,1)S(1)}, u32[]{:S(2)}, u32[]{:S(2)}) collective-permute-start(bf16[28,32,128]{2,1,0:T(8,128)(2,1)S(1)} %slice.15), channel_id=1, source_target_pairs={{0,8},{1,9},{2,10},{3,11},{4,0},{5,1},{6,2},{7,3},{8,12},{9,13},{1... | collective-permute-start | bytes 688136 | tf_op jit(solution)/shard_map/ppermute | solution.py:31
  46.7 9.5 %collective-permute-start.17 = (bf16[32,32,128]{2,1,0:T(8,128)(2,1)S(1)}, bf16[32,32,128]{2,1,0:T(8,128)(2,1)S(1)}, u32[]{:S(2)}, u32[]{:S(2)}) collective-permute-start(bf16[32,32,128]{2,1,0:T(8,128)(2,1)S(1)} %get-tuple-element.84), channel_id=1, source_target_pairs={{0,2},{1,3},{2,0},{3,1},{4,6},{5,7},{6,4},{7,5},{8,10},{9,11},{10,... | collective-permute-start | bytes 786440 | tf_op jit(solution)/shard_map/ppermute | solution.py:31
  48.3 7.9 %collective-permute-start.18 = (bf16[64,1024]{1,0:T(8,128)(2,1)S(1)}, bf16[64,1024]{1,0:T(8,128)(2,1)S(1)}, u32[]{:S(2)}, u32[]{:S(2)}) collective-permute-start(bf16[64,1024]{1,0:T(8,128)(2,1)S(1)} %get-tuple-element.87), channel_id=1, source_target_pairs={{0,1},{1,0},{2,3},{3,2},{4,5},{5,4},{6,7},{7,6},{8,9},{9,8},{10,11... | collective-permute-start | bytes 393224 | tf_op jit(solution)/shard_map/ppermute | solution.py:31
  48.3 7.9 %collective-permute-start.19 = (bf16[64,1024]{1,0:T(8,128)(2,1)S(1)}, bf16[64,1024]{1,0:T(8,128)(2,1)S(1)}, u32[]{:S(2)}, u32[]{:S(2)}) collective-permute-start(bf16[64,1024]{1,0:T(8,128)(2,1)S(1)} %get-tuple-element.88), channel_id=1, source_target_pairs={{0,3},{1,2},{2,1},{3,0},{4,7},{5,6},{6,5},{7,4},{8,11},{9,10},{10,... | collective-permute-start | bytes 393224 | tf_op jit(solution)/shard_map/ppermute | solution.py:31
  56.3 1.6 %collective-permute-start.20 = (bf16[2,2,32,1024]{3,2,1,0:T(8,128)(2,1)S(1)}, bf16[2,2,32,1024]{3,2,1,0:T(8,128)(2,1)S(1)}, u32[]{:S(2)}, u32[]{:S(2)}) collective-permute-start(bf16[2,2,32,1024]{3,2,1,0:T(8,128)(2,1)S(1)} %get-tuple-element.90), channel_id=1, source_target_pairs={{0,1},{1,0},{2,3},{3,2},{4,5},{5,4},{6,7},{7,6},{8,9},{9,8},{10,11... | collective-permute-start | bytes 786440 | tf_op jit(solution)/shard_map/ppermute | solution.py:31
  56.4 9.8 %collective-permute-start.24 = (bf16[32,32,128]{2,1,0:T(8,128)(2,1)S(1)}, bf16[32,32,128]{2,1,0:T(8,128)(2,1)S(1)}, u32[]{:S(2)}, u32[]{:S(2)}) collective-permute-start(bf16[32,32,128]{2,1,0:T(8,128)(2,1)S(1)} %shard_map.78.refs_0_), channel_id=1, source_target_pairs={{0,1},{1,0},{2,3},{3,2},{4,5},{5,4},{6,7},{7,6},{8,9},{9,8},{10,11... | collective-permute-start | bytes 786440 | tf_op jit(solution)/shard_map/ppermute | solution.py:31
  56.9 5.5 %collective-permute-start.22 = (bf16[64,1024]{1,0:T(8,128)(2,1)S(1)}, bf16[64,1024]{1,0:T(8,128)(2,1)S(1)}, u32[]{:S(2)}, u32[]{:S(2)}) collective-permute-start(bf16[64,1024]{1,0:T(8,128)(2,1)S(1)} %shard_map.80), channel_id=1, source_target_pairs={{0,16},{1,17},{2,18},{3,19},{4,20},{5,21},{6,22},{7,23},{8,24},{9,... | collective-permute-start | bytes 393224 | tf_op jit(solution)/shard_map/ppermute | solution.py:31
  58.0 5.6 %collective-permute-start.21 = (bf16[2,1,32,1024]{3,2,1,0:T(8,128)(2,1)S(1)}, bf16[2,1,32,1024]{3,2,1,0:T(8,128)(2,1)S(1)}, u32[]{:S(2)}, u32[]{:S(2)}) collective-permute-start(bf16[2,1,32,1024]{3,2,1,0:T(8,128)(2,1)S(1)} %get-tuple-element.92), channel_id=1, source_target_pairs={{0,2},{1,3},{2,0},{3,1},{4,6},{5,7},{6,4},{7,5},{8,10},{9,11},{10,... | collective-permute-start | bytes 393224 | tf_op jit(solution)/shard_map/ppermute | solution.py:31
  59.5 8.0 %collective-permute-start.25 = (bf16[32,32,128]{2,1,0:T(8,128)(2,1)S(1)}, bf16[32,32,128]{2,1,0:T(8,128)(2,1)S(1)}, u32[]{:S(2)}, u32[]{:S(2)}) collective-permute-start(bf16[32,32,128]{2,1,0:T(8,128)(2,1)S(1)} %collective-permute-done.16.refs_2_), channel_id=1, source_target_pairs={{0,1},{1,0},{2,3},{3,2},{4,5},{5,4},{6,7},{7,6},{8,9},{9,8},{10,11... | collective-permute-start | bytes 786440 | tf_op jit(solution)/shard_map/ppermute | solution.py:31
  59.6 8.0 %collective-permute-start.26 = (bf16[32,32,128]{2,1,0:T(8,128)(2,1)S(1)}, bf16[32,32,128]{2,1,0:T(8,128)(2,1)S(1)}, u32[]{:S(2)}, u32[]{:S(2)}) collective-permute-start(bf16[32,32,128]{2,1,0:T(8,128)(2,1)S(1)} %shard_map.83.refs_4_), channel_id=1, source_target_pairs={{0,1},{1,0},{2,3},{3,2},{4,5},{5,4},{6,7},{7,6},{8,9},{9,8},{10,11... | collective-permute-start | bytes 786440 | tf_op jit(solution)/shard_map/ppermute | solution.py:31
  63.6 9.4 %collective-permute-start.27 = (bf16[64,1024]{1,0:T(8,128)(2,1)S(1)}, bf16[64,1024]{1,0:T(8,128)(2,1)S(1)}, u32[]{:S(2)}, u32[]{:S(2)}) collective-permute-start(bf16[64,1024]{1,0:T(8,128)(2,1)S(1)} %get-tuple-element.104), channel_id=1, source_target_pairs={{0,16},{1,17},{2,18},{3,19},{4,20},{5,21},{6,22},{7,23},{8,24},{9,... | collective-permute-start | bytes 393224 | tf_op jit(solution)/shard_map/ppermute | solution.py:31
  64.3 8.7 %collective-permute-start.28 = (bf16[64,1024]{1,0:T(8,128)(2,1)S(1)}, bf16[64,1024]{1,0:T(8,128)(2,1)S(1)}, u32[]{:S(2)}, u32[]{:S(2)}) collective-permute-start(bf16[64,1024]{1,0:T(8,128)(2,1)S(1)} %get-tuple-element.107), channel_id=1, source_target_pairs={{0,16},{1,17},{2,18},{3,19},{4,20},{5,21},{6,22},{7,23},{8,24},{9,... | collective-permute-start | bytes 393224 | tf_op jit(solution)/shard_map/ppermute | solution.py:31
  66.2 6.9 %collective-permute-start.23 = (bf16[64,1024]{1,0:T(8,128)(2,1)S(1)}, bf16[64,1024]{1,0:T(8,128)(2,1)S(1)}, u32[]{:S(2)}, u32[]{:S(2)}) collective-permute-start(bf16[64,1024]{1,0:T(8,128)(2,1)S(1)} %collective-permute-done.22), channel_id=1, source_target_pairs={{0,12},{1,13},{2,14},{3,15},{4,8},{5,9},{6,10},{7,11},{8,4},{9,5},... | collective-permute-start | bytes 393224 | tf_op jit(solution)/shard_map/ppermute | solution.py:31

commit v6 on v5

--- a/solution.py
+++ b/solution.py
@@ -431,9 +431,10 @@
     keep, give = product((a, at), (b, at), flops=2 * tokens * hidden * width)
     passed = call(passed_kernel, [(rows, replicas * width)], base, zero)[0]
     x_far, give, out, passed = together(x_far, give, out, passed)
-    two = returned(out, 0)
     keep, give = fold(2, keep, across(give, 1))
     got = across(give, 2)
+    out, _ = together(out, give)
+    two = returned(out, 0)
     x_near = [v for pair in ((v, across(v, 1)) for v in x_near) for v in pair]
     places = [(i, 0, x_count, i, 2) for i in range(2)] + [(2, 2 * x_count, 2 * x_count, 2 * x_count, 1)]
     x_far = stacked(4 * x_count, places, a_parts[2], b_parts[2], x_far)
@@ -441,7 +442,6 @@
     x_far = [x_far, across(x_far, 1)]
 
     parts = [v for pair_of in zip(a_parts, b_parts) for v in pair_of]
-    keep, got, two = together(keep, got, two)
     step = 4
     while step < shards:
         keep, give = fold(step, keep, got)

time: 74 us -> 74 us (level)
  starting transfers between devices: 28.2 us -> 29.1 us
  waiting for transfers between devices: 31.4 us -> 30.5 us
    ppermute x29, waiting for transfers between devices: 31.4 us -> 30.5 us  [moved(): return lax.ppermute(value, AXES, pairs)]
    ppermute x29, starting transfers between devices: 28.2 us -> 29.1 us  [moved(): return lax.ppermute(value, AXES, pairs)]
  transfers between devices with their start and end apart: 29 -> 29, of which waited for: 12 -> 11; matrix products, arithmetic and copies ran while one was open for 0% -> 0% of each run, Pallas kernels for 13% -> 13%
where the time goes in v6:
time: 74 us; the launch traced here: 73.8 us
  waiting for transfers between devices  30.5 us (41%)
  starting transfers between devices  29.1 us (39%)
  Pallas kernels  11.8 us (16%)
  local copies, waits for them, and re-layouts  1.57 us (2%)
  between operations  0.85 us (1%)
    ppermute x29, waiting for transfers between devices, moved(): return lax.ppermute(value, AXES, pairs)  30.5 us
    ppermute x29, starting transfers between devices, moved(): return lax.ppermute(value, AXES, pairs)  29.1 us
    pallas_call x19, Pallas kernels, call(): pl.pallas_call(kernel, out_shape=[v if hasattr(v, 'dtype') else jax.Shape...  11.8 us
    unnamed x2, local copies, waits for them, and re-layouts  1.5 us
  transfers between devices with their start and end apart: 29, of which 11 were waited for; matrix products, arithmetic and copies ran while one was open for 0% of the time, Pallas kernels for 13%

profile of v6, /device:TPU:0, one launch (start us, length us, event | category | flops | bytes accessed | tf_op | source)
XLA Modules:
  0.0 73.8 jit_solution(12949520313627441325)
XLA Ops:
  0.6 1.6 %shard_map.68 = (bf16[52,32,128]{2,1,0:T(8,128)(2,1)S(1)}, bf16[52,32,128]{2,1,0:T(8,128)(2,1)S(1)}, bf16[16,32,128]{2,1,0:T(8,128)(2,1)S(1)}) custom-call(bf16[256,896]{1,0:T(8,128)(2,1)} %bitcast.11, bf16[256,896]{1,0:T(8,128)(2,1)} %bitcast.12, bf16[64,4096]{1,0:T(8,128)(2,1)} %bitcast.10), custom_call_target="tpu_custom_call" | custom-call | tf_op jit(solution)/shard_map/pallas_call | solution.py:50
  2.3 3.0 %collective-permute-start.2 = (bf16[64,4096]{1,0:T(8,128)(2,1)}, bf16[64,4096]{1,0:T(8,128)(2,1)S(1)}, u32[]{:S(2)}, u32[]{:S(2)}) collective-permute-start(bf16[64,4096]{1,0:T(8,128)(2,1)} %bitcast.13), channel_id=1, source_target_pairs={{0,16},{1,17},{2,18},{3,19},{4,20},{5,21},{6,22},{7,23},{8,24},{9,... | collective-permute-start | bytes 1572872 | tf_op jit(solution)/shard_map/ppermute | solution.py:31
  5.3 1.6 %collective-permute-start = (bf16[52,32,128]{2,1,0:T(8,128)(2,1)S(1)}, bf16[52,32,128]{2,1,0:T(8,128)(2,1)S(1)}, u32[]{:S(2)}, u32[]{:S(2)}) collective-permute-start(bf16[52,32,128]{2,1,0:T(8,128)(2,1)S(1)} %get-tuple-element.55.refs_0_.refs_2_), channel_id=1, source_target_pairs={{0,4},{1,5},{2,6},{3,7},{4,12},{5,13},{6,14},{7,15},{8,0},{9,1},{1... | collective-permute-start | bytes 1277960 | tf_op jit(solution)/shard_map/ppermute | solution.py:31
  6.9 1.3 %collective-permute-start.1 = (bf16[52,32,128]{2,1,0:T(8,128)(2,1)S(1)}, bf16[52,32,128]{2,1,0:T(8,128)(2,1)S(1)}, u32[]{:S(2)}, u32[]{:S(2)}) collective-permute-start(bf16[52,32,128]{2,1,0:T(8,128)(2,1)S(1)} %get-tuple-element.56.refs_1_.refs_3_), channel_id=1, source_target_pairs={{0,8},{1,9},{2,10},{3,11},{4,0},{5,1},{6,2},{7,3},{8,12},{9,13},{1... | collective-permute-start | bytes 1277960 | tf_op jit(solution)/shard_map/ppermute | solution.py:31
  8.2 1.5 %collective-permute-start.6 = (bf16[16,32,128]{2,1,0:T(8,128)(2,1)S(1)}, bf16[16,32,128]{2,1,0:T(8,128)(2,1)S(1)}, u32[]{:S(2)}, u32[]{:S(2)}) collective-permute-start(bf16[16,32,128]{2,1,0:T(8,128)(2,1)S(1)} %get-tuple-element.62.refs_0_), channel_id=1, source_target_pairs={{0,2},{1,3},{2,0},{3,1},{4,6},{5,7},{6,4},{7,5},{8,10},{9,11},{10,... | collective-permute-start | bytes 393224 | tf_op jit(solution)/shard_map/ppermute | solution.py:31
  9.7 1.5 %copy-done = bf16[1,1024,896]{2,1,0:T(8,128)(2,1)S(1)} copy-done((bf16[1,1024,896]{2,1,0:T(8,128)(2,1)S(1)}, bf16[1,1024,896]{2,1,0:T(8,128)(2,1)}, u32[]{:S(2)}) %copy-start) | copy-done | bytes 1835032
  11.4 0.7 %shard_map.70 = (bf16[64,1024]{1,0:T(8,128)(2,1)S(1)}, bf16[64,1024]{1,0:T(8,128)(2,1)S(1)}, bf16[64,1024]{1,0:T(8,128)(2,1)S(1)}, bf16[64,1024]{1,0:T(8,128)(2,1)S(1)}) custom-call(bf16[52,32,128]{2,1,0:T(8,128)(2,1)S(1)} %get-tuple-element.55.refs_0_.refs_2_, bf16[52,32,128]{2,1,0:T(8,128)(2,1)S(1)} %get-tuple-element.56.refs_1_.refs_3_, ...), custom_call_target="tpu_custom_call" | custom-call | tf_op jit(solution)/shard_map/pallas_call | solution.py:50
  12.2 1.0 %collective-permute-done.6.refs_1_ = bf16[16,32,128]{2,1,0:T(8,128)(2,1)S(1)} collective-permute-done((bf16[16,32,128]{2,1,0:T(8,128)(2,1)S(1)}, bf16[16,32,128]{2,1,0:T(8,128)(2,1)S(1)}, u32[]{:S(2)}, u32[]{:S(2)}) %collective-permute-start.6) | collective-permute-done | bytes 131104 | tf_op jit(solution)/shard_map/ppermute | solution.py:31
  13.2 1.5 %collective-permute-start.4 = (bf16[64,1024]{1,0:T(8,128)(2,1)S(1)}, bf16[64,1024]{1,0:T(8,128)(2,1)S(1)}, u32[]{:S(2)}, u32[]{:S(2)}) collective-permute-start(bf16[64,1024]{1,0:T(8,128)(2,1)S(1)} %get-tuple-element.60), channel_id=1, source_target_pairs={{0,2},{1,3},{2,0},{3,1},{4,6},{5,7},{6,4},{7,5},{8,10},{9,11},{10,... | collective-permute-start | bytes 393224 | tf_op jit(solution)/shard_map/ppermute | solution.py:31
  14.8 3.3 %collective-permute-done.4.refs_2_ = bf16[64,1024]{1,0:T(8,128)(2,1)S(1)} collective-permute-done((bf16[64,1024]{1,0:T(8,128)(2,1)S(1)}, bf16[64,1024]{1,0:T(8,128)(2,1)S(1)}, u32[]{:S(2)}, u32[]{:S(2)}) %collective-permute-start.4) | collective-permute-done | bytes 131104 | tf_op jit(solution)/shard_map/ppermute | solution.py:31
  18.2 5.7 %collective-permute-done.5.refs_3_ = bf16[64,1024]{1,0:T(8,128)(2,1)S(1)} collective-permute-done((bf16[64,1024]{1,0:T(8,128)(2,1)S(1)}, bf16[64,1024]{1,0:T(8,128)(2,1)S(1)}, u32[]{:S(2)}, u32[]{:S(2)}) %collective-permute-start.5) | collective-permute-done | bytes 131104 | tf_op jit(solution)/shard_map/ppermute | solution.py:31
  24.0 2.6 %collective-permute-done.1.refs_1_.refs_7_ = bf16[52,32,128]{2,1,0:T(8,128)(2,1)S(1)} collective-permute-done((bf16[52,32,128]{2,1,0:T(8,128)(2,1)S(1)}, bf16[52,32,128]{2,1,0:T(8,128)(2,1)S(1)}, u32[]{:S(2)}, u32[]{:S(2)}) %collective-permute-start.1) | collective-permute-done | bytes 426016 | tf_op jit(solution)/shard_map/ppermute | solution.py:31
  26.6 1.7 %collective-permute-start.8 = (bf16[36,32,128]{2,1,0:T(8,128)(2,1)S(1)}, bf16[36,32,128]{2,1,0:T(8,128)(2,1)S(1)}, u32[]{:S(2)}, u32[]{:S(2)}) collective-permute-start(bf16[36,32,128]{2,1,0:T(8,128)(2,1)S(1)} %slice.12), channel_id=1, source_target_pairs={{0,4},{1,5},{2,6},{3,7},{4,12},{5,13},{6,14},{7,15},{8,0},{9,1},{1... | collective-permute-start | bytes 884744 | tf_op jit(solution)/shard_map/ppermute | solution.py:31
  28.4 1.3 %collective-permute-start.9 = (bf16[36,32,128]{2,1,0:T(8,128)(2,1)S(1)}, bf16[36,32,128]{2,1,0:T(8,128)(2,1)S(1)}, u32[]{:S(2)}, u32[]{:S(2)}) collective-permute-start(bf16[36,32,128]{2,1,0:T(8,128)(2,1)S(1)} %slice.13), channel_id=1, source_target_pairs={{0,8},{1,9},{2,10},{3,11},{4,0},{5,1},{6,2},{7,3},{8,12},{9,13},{1... | collective-permute-start | bytes 884744 | tf_op jit(solution)/shard_map/ppermute | solution.py:31
  31.0 1.6 %collective-permute-start.14 = (bf16[32,32,128]{2,1,0:T(8,128)(2,1)S(1)}, bf16[32,32,128]{2,1,0:T(8,128)(2,1)S(1)}, u32[]{:S(2)}, u32[]{:S(2)}) collective-permute-start(bf16[32,32,128]{2,1,0:T(8,128)(2,1)S(1)} %shard_map.77.refs_0_), channel_id=1, source_target_pairs={{0,2},{1,3},{2,0},{3,1},{4,6},{5,7},{6,4},{7,5},{8,10},{9,11},{10,... | collective-permute-start | bytes 786440 | tf_op jit(solution)/shard_map/ppermute | solution.py:31
  32.7 1.0 %collective-permute-start.13 = (bf16[2,1,32,1024]{3,2,1,0:T(8,128)(2,1)S(1)}, bf16[2,1,32,1024]{3,2,1,0:T(8,128)(2,1)S(1)}, u32[]{:S(2)}, u32[]{:S(2)}) collective-permute-start(bf16[2,1,32,1024]{3,2,1,0:T(8,128)(2,1)S(1)} %get-tuple-element.74), channel_id=1, source_target_pairs={{0,2},{1,3},{2,0},{3,1},{4,6},{5,7},{6,4},{7,5},{8,10},{9,11},{10,... | collective-permute-start | bytes 393224 | tf_op jit(solution)/shard_map/ppermute | solution.py:31
  34.2 1.4 %shard_map.73.refs_12_ = f32[1024,896]{1,0:T(8,128)S(1)} custom-call(bf16[32,32,128]{2,1,0:T(8,128)(2,1)S(1)} %shard_map.72.refs_0_, bf16[32,32,128]{2,1,0:T(8,128)(2,1)S(1)} %collective-permute-done.7.refs_1_, bf16[52,32,128]{2,1,0:T(8,128)(2,1)S(1)} %get-tuple-element.55.refs_0_.refs_2_, bf16[52,32,128]{2,1,0:T(8,128)(2,1)S(1)} %get-tuple-element.56.refs_1_.refs_3_), custom_call_target="tpu_custom_call" | custom-call | tf_op jit(solution)/shard_map/pallas_call | solution.py:50
  35.6 6.6 %collective-permute-done.13.got = bf16[2,1,32,1024]{3,2,1,0:T(8,128)(2,1)S(1)} collective-permute-done((bf16[2,1,32,1024]{3,2,1,0:T(8,128)(2,1)S(1)}, bf16[2,1,32,1024]{3,2,1,0:T(8,128)(2,1)S(1)}, u32[]{:S(2)}, u32[]{:S(2)}) %collective-permute-start.13) | collective-permute-done | bytes 131104 | tf_op jit(solution)/shard_map/ppermute | solution.py:31
  42.9 0.7 %collective-permute-start.16 = (bf16[28,32,128]{2,1,0:T(8,128)(2,1)S(1)}, bf16[28,32,128]{2,1,0:T(8,128)(2,1)S(1)}, u32[]{:S(2)}, u32[]{:S(2)}) collective-permute-start(bf16[28,32,128]{2,1,0:T(8,128)(2,1)S(1)} %slice.14), channel_id=1, source_target_pairs={{0,4},{1,5},{2,6},{3,7},{4,12},{5,13},{6,14},{7,15},{8,0},{9,1},{1... | collective-permute-start | bytes 688136 | tf_op jit(solution)/shard_map/ppermute | solution.py:31
  43.7 2.3 %collective-permute-start.17 = (bf16[28,32,128]{2,1,0:T(8,128)(2,1)S(1)}, bf16[28,32,128]{2,1,0:T(8,128)(2,1)S(1)}, u32[]{:S(2)}, u32[]{:S(2)}) collective-permute-start(bf16[28,32,128]{2,1,0:T(8,128)(2,1)S(1)} %slice.15), channel_id=1, source_target_pairs={{0,8},{1,9},{2,10},{3,11},{4,0},{5,1},{6,2},{7,3},{8,12},{9,13},{1... | collective-permute-start | bytes 688136 | tf_op jit(solution)/shard_map/ppermute | solution.py:31
  46.7 1.6 %collective-permute-start.15 = (bf16[32,32,128]{2,1,0:T(8,128)(2,1)S(1)}, bf16[32,32,128]{2,1,0:T(8,128)(2,1)S(1)}, u32[]{:S(2)}, u32[]{:S(2)}) collective-permute-start(bf16[32,32,128]{2,1,0:T(8,128)(2,1)S(1)} %get-tuple-element.81), channel_id=1, source_target_pairs={{0,2},{1,3},{2,0},{3,1},{4,6},{5,7},{6,4},{7,5},{8,10},{9,11},{10,... | collective-permute-start | bytes 786440 | tf_op jit(solution)/shard_map/ppermute | solution.py:31
  48.9 0.9 %shard_map.81.refs_3_ = bf16[64,4096]{1,0:T(8,128)(2,1)} custom-call(bf16[64,4096]{1,0:T(8,128)(2,1)S(1)} %collective-permute-done.2.base, bf16[64,1024]{1,0:T(8,128)(2,1)S(1)} %collective-permute-done.10.piece), custom_call_target="tpu_custom_call" | custom-call | tf_op jit(solution)/shard_map/pallas_call | solution.py:50
  49.8 1.9 %collective-permute-done.16.refs_0_.refs_10_ = bf16[28,32,128]{2,1,0:T(8,128)(2,1)S(1)} collective-permute-done((bf16[28,32,128]{2,1,0:T(8,128)(2,1)S(1)}, bf16[28,32,128]{2,1,0:T(8,128)(2,1)S(1)}, u32[]{:S(2)}, u32[]{:S(2)}) %collective-permute-start.16) | collective-permute-done | bytes 229408 | tf_op jit(solution)/shard_map/ppermute | solution.py:31
  51.6 3.8 %collective-permute-done.17.refs_1_.refs_11_ = bf16[28,32,128]{2,1,0:T(8,128)(2,1)S(1)} collective-permute-done((bf16[28,32,128]{2,1,0:T(8,128)(2,1)S(1)}, bf16[28,32,128]{2,1,0:T(8,128)(2,1)S(1)}, u32[]{:S(2)}, u32[]{:S(2)}) %collective-permute-start.17) | collective-permute-done | bytes 229408 | tf_op jit(solution)/shard_map/ppermute | solution.py:31
  55.4 0.7 %shard_map.79 = (bf16[2,2,32,1024]{3,2,1,0:T(8,128)(2,1)S(1)}, bf16[2,2,32,1024]{3,2,1,0:T(8,128)(2,1)S(1)}) custom-call(bf16[28,32,128]{2,1,0:T(8,128)(2,1)S(1)} %collective-permute-done.16.refs_0_.refs_10_, bf16[28,32,128]{2,1,0:T(8,128)(2,1)S(1)} %collective-permute-done.17.refs_1_.refs_11_, bf16[1024,896]{1,0:T(8,128)(2,1)S(1)} %shard_map.69.refs_2_), custom_call_target="tpu_custom_call" | custom-call | flops 469762048 | bytes 2293760 | tf_op jit(solution)/shard_map/pallas_call | solution.py:50
  56.9 0.9 %collective-permute-done.20.refs_1_ = bf16[2,2,32,1024]{3,2,1,0:T(8,128)(2,1)S(1)} collective-permute-done((bf16[2,2,32,1024]{3,2,1,0:T(8,128)(2,1)S(1)}, bf16[2,2,32,1024]{3,2,1,0:T(8,128)(2,1)S(1)}, u32[]{:S(2)}, u32[]{:S(2)}) %collective-permute-start.20) | collective-permute-done | bytes 262176 | tf_op jit(solution)/shard_map/ppermute | solution.py:31
  58.0 1.6 %collective-permute-start.26 = (bf16[2,1,32,1024]{3,2,1,0:T(8,128)(2,1)S(1)}, bf16[2,1,32,1024]{3,2,1,0:T(8,128)(2,1)S(1)}, u32[]{:S(2)}, u32[]{:S(2)}) collective-permute-start(bf16[2,1,32,1024]{3,2,1,0:T(8,128)(2,1)S(1)} %get-tuple-element.90), channel_id=1, source_target_pairs={{0,2},{1,3},{2,0},{3,1},{4,6},{5,7},{6,4},{7,5},{8,10},{9,11},{10,... | collective-permute-start | bytes 393224 | tf_op jit(solution)/shard_map/ppermute | solution.py:31
  60.2 3.3 %collective-permute-done.26.got = bf16[2,1,32,1024]{3,2,1,0:T(8,128)(2,1)S(1)} collective-permute-done((bf16[2,1,32,1024]{3,2,1,0:T(8,128)(2,1)S(1)}, bf16[2,1,32,1024]{3,2,1,0:T(8,128)(2,1)S(1)}, u32[]{:S(2)}, u32[]{:S(2)}) %collective-permute-start.26) | collective-permute-done | bytes 131104 | tf_op jit(solution)/shard_map/ppermute | solution.py:31
  64.1 2.0 %collective-permute-start.28 = (bf16[64,1024]{1,0:T(8,128)(2,1)S(1)}, bf16[64,1024]{1,0:T(8,128)(2,1)S(1)}, u32[]{:S(2)}, u32[]{:S(2)}) collective-permute-start(bf16[64,1024]{1,0:T(8,128)(2,1)S(1)} %get-tuple-element.103), channel_id=1, source_target_pairs={{0,16},{1,17},{2,18},{3,19},{4,20},{5,21},{6,22},{7,23},{8,24},{9,... | collective-permute-start | bytes 393224 | tf_op jit(solution)/shard_map/ppermute | solution.py:31
  66.2 2.6 %collective-permute-start.22 = (bf16[64,1024]{1,0:T(8,128)(2,1)S(1)}, bf16[64,1024]{1,0:T(8,128)(2,1)S(1)}, u32[]{:S(2)}, u32[]{:S(2)}) collective-permute-start(bf16[64,1024]{1,0:T(8,128)(2,1)S(1)} %collective-permute-done.21), channel_id=1, source_target_pairs={{0,12},{1,13},{2,14},{3,15},{4,8},{5,9},{6,10},{7,11},{8,4},{9,5},... | collective-permute-start | bytes 393224 | tf_op jit(solution)/shard_map/ppermute | solution.py:31
  68.7 3.6 %shard_map.85 = bf16[1024,896]{1,0:T(8,128)(2,1)} custom-call(bf16[32,32,128]{2,1,0:T(8,128)(2,1)S(1)} %shard_map.77.refs_0_, bf16[32,32,128]{2,1,0:T(8,128)(2,1)S(1)} %collective-permute-done.23.refs_1_, bf16[32,32,128]{2,1,0:T(8,128)(2,1)S(1)} %collective-permute-done.14.refs_2_, bf16[32,32,128]{2,1,0:T(8,128)(2,1)S(1)} %collective-permute-done.24.refs_3_, ...), custom_call_target="tpu_custom_call" | custom-call | tf_op jit(solution)/shard_map/pallas_call | solution.py:50
  73.0 0.8 %shard_map.86 = bf16[64,4096]{1,0:T(8,128)(2,1)} custom-call(bf16[64,4096]{1,0:T(8,128)(2,1)S(1)} %collective-permute-done.2.base, bf16[64,1024]{1,0:T(8,128)(2,1)S(1)} %collective-permute-done.22.refs_0_, bf16[64,1024]{1,0:T(8,128)(2,1)S(1)} %collective-permute-done.27.refs_1_, ...), custom_call_target="tpu_custom_call", output_to_operand_aliasing={{}: (4, {})} | custom-call | tf_op jit(solution)/shard_map/pallas_call | solution.py:50
  (51 shorter events, 7.1 us)
Async XLA Ops:
  2.3 24.3 %collective-permute-start.2 = (bf16[64,4096]{1,0:T(8,128)(2,1)}, bf16[64,4096]{1,0:T(8,128)(2,1)S(1)}, u32[]{:S(2)}, u32[]{:S(2)}) collective-permute-start(bf16[64,4096]{1,0:T(8,128)(2,1)} %bitcast.13), channel_id=1, source_target_pairs={{0,16},{1,17},{2,18},{3,19},{4,20},{5,21},{6,22},{7,23},{8,24},{9,... | collective-permute-start | bytes 1572872 | tf_op jit(solution)/shard_map/ppermute | solution.py:31
  5.3 18.7 %collective-permute-start = (bf16[52,32,128]{2,1,0:T(8,128)(2,1)S(1)}, bf16[52,32,128]{2,1,0:T(8,128)(2,1)S(1)}, u32[]{:S(2)}, u32[]{:S(2)}) collective-permute-start(bf16[52,32,128]{2,1,0:T(8,128)(2,1)S(1)} %get-tuple-element.55.refs_0_.refs_2_), channel_id=1, source_target_pairs={{0,4},{1,5},{2,6},{3,7},{4,12},{5,13},{6,14},{7,15},{8,0},{9,1},{1... | collective-permute-start | bytes 1277960 | tf_op jit(solution)/shard_map/ppermute | solution.py:31
  6.9 19.7 %collective-permute-start.1 = (bf16[52,32,128]{2,1,0:T(8,128)(2,1)S(1)}, bf16[52,32,128]{2,1,0:T(8,128)(2,1)S(1)}, u32[]{:S(2)}, u32[]{:S(2)}) collective-permute-start(bf16[52,32,128]{2,1,0:T(8,128)(2,1)S(1)} %get-tuple-element.56.refs_1_.refs_3_), channel_id=1, source_target_pairs={{0,8},{1,9},{2,10},{3,11},{4,0},{5,1},{6,2},{7,3},{8,12},{9,13},{1... | collective-permute-start | bytes 1277960 | tf_op jit(solution)/shard_map/ppermute | solution.py:31
  8.2 5.0 %collective-permute-start.6 = (bf16[16,32,128]{2,1,0:T(8,128)(2,1)S(1)}, bf16[16,32,128]{2,1,0:T(8,128)(2,1)S(1)}, u32[]{:S(2)}, u32[]{:S(2)}) collective-permute-start(bf16[16,32,128]{2,1,0:T(8,128)(2,1)S(1)} %get-tuple-element.62.refs_0_), channel_id=1, source_target_pairs={{0,2},{1,3},{2,0},{3,1},{4,6},{5,7},{6,4},{7,5},{8,10},{9,11},{10,... | collective-permute-start | bytes 393224 | tf_op jit(solution)/shard_map/ppermute | solution.py:31
  9.7 1.5 %copy-start = (bf16[1,1024,896]{2,1,0:T(8,128)(2,1)S(1)}, bf16[1,1024,896]{2,1,0:T(8,128)(2,1)}, u32[]{:S(2)}) copy-start(bf16[1,1024,896]{2,1,0:T(8,128)(2,1)} %param.9) | copy-start | bytes 5505028
  12.1 2.6 %collective-permute-start.3 = (bf16[64,1024]{1,0:T(8,128)(2,1)S(1)}, bf16[64,1024]{1,0:T(8,128)(2,1)S(1)}, u32[]{:S(2)}, u32[]{:S(2)}) collective-permute-start(bf16[64,1024]{1,0:T(8,128)(2,1)S(1)} %get-tuple-element.59), channel_id=1, source_target_pairs={{0,1},{1,0},{2,3},{3,2},{4,5},{5,4},{6,7},{7,6},{8,9},{9,8},{10,11... | collective-permute-start | bytes 393224 | tf_op jit(solution)/shard_map/ppermute | solution.py:31
  13.2 5.0 %collective-permute-start.4 = (bf16[64,1024]{1,0:T(8,128)(2,1)S(1)}, bf16[64,1024]{1,0:T(8,128)(2,1)S(1)}, u32[]{:S(2)}, u32[]{:S(2)}) collective-permute-start(bf16[64,1024]{1,0:T(8,128)(2,1)S(1)} %get-tuple-element.60), channel_id=1, source_target_pairs={{0,2},{1,3},{2,0},{3,1},{4,6},{5,7},{6,4},{7,5},{8,10},{9,11},{10,... | collective-permute-start | bytes 393224 | tf_op jit(solution)/shard_map/ppermute | solution.py:31
  14.7 9.2 %collective-permute-start.7 = (bf16[32,32,128]{2,1,0:T(8,128)(2,1)S(1)}, bf16[32,32,128]{2,1,0:T(8,128)(2,1)S(1)}, u32[]{:S(2)}, u32[]{:S(2)}) collective-permute-start(bf16[32,32,128]{2,1,0:T(8,128)(2,1)S(1)} %shard_map.72.refs_0_), channel_id=1, source_target_pairs={{0,1},{1,0},{2,3},{3,2},{4,5},{5,4},{6,7},{7,6},{8,9},{9,8},{10,11... | collective-permute-start | bytes 786440 | tf_op jit(solution)/shard_map/ppermute | solution.py:31
  18.1 5.7 %collective-permute-start.5 = (bf16[64,1024]{1,0:T(8,128)(2,1)S(1)}, bf16[64,1024]{1,0:T(8,128)(2,1)S(1)}, u32[]{:S(2)}, u32[]{:S(2)}) collective-permute-start(bf16[64,1024]{1,0:T(8,128)(2,1)S(1)} %get-tuple-element.61), channel_id=1, source_target_pairs={{0,3},{1,2},{2,1},{3,0},{4,7},{5,6},{6,5},{7,4},{8,11},{9,10},{10,... | collective-permute-start | bytes 393224 | tf_op jit(solution)/shard_map/ppermute | solution.py:31
  26.6 16.2 %collective-permute-start.8 = (bf16[36,32,128]{2,1,0:T(8,128)(2,1)S(1)}, bf16[36,32,128]{2,1,0:T(8,128)(2,1)S(1)}, u32[]{:S(2)}, u32[]{:S(2)}) collective-permute-start(bf16[36,32,128]{2,1,0:T(8,128)(2,1)S(1)} %slice.12), channel_id=1, source_target_pairs={{0,4},{1,5},{2,6},{3,7},{4,12},{5,13},{6,14},{7,15},{8,0},{9,1},{1... | collective-permute-start | bytes 884744 | tf_op jit(solution)/shard_map/ppermute | solution.py:31
  28.4 14.5 %collective-permute-start.9 = (bf16[36,32,128]{2,1,0:T(8,128)(2,1)S(1)}, bf16[36,32,128]{2,1,0:T(8,128)(2,1)S(1)}, u32[]{:S(2)}, u32[]{:S(2)}) collective-permute-start(bf16[36,32,128]{2,1,0:T(8,128)(2,1)S(1)} %slice.13), channel_id=1, source_target_pairs={{0,8},{1,9},{2,10},{3,11},{4,0},{5,1},{6,2},{7,3},{8,12},{9,13},{1... | collective-permute-start | bytes 884744 | tf_op jit(solution)/shard_map/ppermute | solution.py:31
  30.4 2.2 %collective-permute-start.11 = (bf16[1,2,32,1024]{3,2,1,0:T(8,128)(2,1)S(1)}, bf16[1,2,32,1024]{3,2,1,0:T(8,128)(2,1)S(1)}, u32[]{:S(2)}, u32[]{:S(2)}) collective-permute-start(bf16[1,2,32,1024]{3,2,1,0:T(8,128)(2,1)S(1)} %get-tuple-element.70), channel_id=1, source_target_pairs={{0,1},{1,0},{2,3},{3,2},{4,5},{5,4},{6,7},{7,6},{8,9},{9,8},{10,11... | collective-permute-start | bytes 393224 | tf_op jit(solution)/shard_map/ppermute | solution.py:31
  30.5 2.1 %collective-permute-start.12 = (bf16[1,2,32,1024]{3,2,1,0:T(8,128)(2,1)S(1)}, bf16[1,2,32,1024]{3,2,1,0:T(8,128)(2,1)S(1)}, u32[]{:S(2)}, u32[]{:S(2)}) collective-permute-start(bf16[1,2,32,1024]{3,2,1,0:T(8,128)(2,1)S(1)} %get-tuple-element.72), channel_id=1, source_target_pairs={{0,1},{1,0},{2,3},{3,2},{4,5},{5,4},{6,7},{7,6},{8,9},{9,8},{10,11... | collective-permute-start | bytes 393224 | tf_op jit(solution)/shard_map/ppermute | solution.py:31
  31.0 14.9 %collective-permute-start.14 = (bf16[32,32,128]{2,1,0:T(8,128)(2,1)S(1)}, bf16[32,32,128]{2,1,0:T(8,128)(2,1)S(1)}, u32[]{:S(2)}, u32[]{:S(2)}) collective-permute-start(bf16[32,32,128]{2,1,0:T(8,128)(2,1)S(1)} %shard_map.77.refs_0_), channel_id=1, source_target_pairs={{0,2},{1,3},{2,0},{3,1},{4,6},{5,7},{6,4},{7,5},{8,10},{9,11},{10,... | collective-permute-start | bytes 786440 | tf_op jit(solution)/shard_map/ppermute | solution.py:31
  32.7 9.5 %collective-permute-start.13 = (bf16[2,1,32,1024]{3,2,1,0:T(8,128)(2,1)S(1)}, bf16[2,1,32,1024]{3,2,1,0:T(8,128)(2,1)S(1)}, u32[]{:S(2)}, u32[]{:S(2)}) collective-permute-start(bf16[2,1,32,1024]{3,2,1,0:T(8,128)(2,1)S(1)} %get-tuple-element.74), channel_id=1, source_target_pairs={{0,2},{1,3},{2,0},{3,1},{4,6},{5,7},{6,4},{7,5},{8,10},{9,11},{10,... | collective-permute-start | bytes 393224 | tf_op jit(solution)/shard_map/ppermute | solution.py:31
  33.7 8.5 %collective-permute-start.10 = (bf16[64,1024]{1,0:T(8,128)(2,1)S(1)}, bf16[64,1024]{1,0:T(8,128)(2,1)S(1)}, u32[]{:S(2)}, u32[]{:S(2)}) collective-permute-start(bf16[64,1024]{1,0:T(8,128)(2,1)S(1)} %shard_map.71), channel_id=1, source_target_pairs={{0,16},{1,17},{2,18},{3,19},{4,20},{5,21},{6,22},{7,23},{8,24},{9,... | collective-permute-start | bytes 393224 | tf_op jit(solution)/shard_map/ppermute | solution.py:31
  42.9 8.8 %collective-permute-start.16 = (bf16[28,32,128]{2,1,0:T(8,128)(2,1)S(1)}, bf16[28,32,128]{2,1,0:T(8,128)(2,1)S(1)}, u32[]{:S(2)}, u32[]{:S(2)}) collective-permute-start(bf16[28,32,128]{2,1,0:T(8,128)(2,1)S(1)} %slice.14), channel_id=1, source_target_pairs={{0,4},{1,5},{2,6},{3,7},{4,12},{5,13},{6,14},{7,15},{8,0},{9,1},{1... | collective-permute-start | bytes 688136 | tf_op jit(solution)/shard_map/ppermute | solution.py:31
  43.7 11.8 %collective-permute-start.17 = (bf16[28,32,128]{2,1,0:T(8,128)(2,1)S(1)}, bf16[28,32,128]{2,1,0:T(8,128)(2,1)S(1)}, u32[]{:S(2)}, u32[]{:S(2)}) collective-permute-start(bf16[28,32,128]{2,1,0:T(8,128)(2,1)S(1)} %slice.15), channel_id=1, source_target_pairs={{0,8},{1,9},{2,10},{3,11},{4,0},{5,1},{6,2},{7,3},{8,12},{9,13},{1... | collective-permute-start | bytes 688136 | tf_op jit(solution)/shard_map/ppermute | solution.py:31
  46.7 9.5 %collective-permute-start.15 = (bf16[32,32,128]{2,1,0:T(8,128)(2,1)S(1)}, bf16[32,32,128]{2,1,0:T(8,128)(2,1)S(1)}, u32[]{:S(2)}, u32[]{:S(2)}) collective-permute-start(bf16[32,32,128]{2,1,0:T(8,128)(2,1)S(1)} %get-tuple-element.81), channel_id=1, source_target_pairs={{0,2},{1,3},{2,0},{3,1},{4,6},{5,7},{6,4},{7,5},{8,10},{9,11},{10,... | collective-permute-start | bytes 786440 | tf_op jit(solution)/shard_map/ppermute | solution.py:31
  48.3 7.9 %collective-permute-start.18 = (bf16[64,1024]{1,0:T(8,128)(2,1)S(1)}, bf16[64,1024]{1,0:T(8,128)(2,1)S(1)}, u32[]{:S(2)}, u32[]{:S(2)}) collective-permute-start(bf16[64,1024]{1,0:T(8,128)(2,1)S(1)} %get-tuple-element.84), channel_id=1, source_target_pairs={{0,1},{1,0},{2,3},{3,2},{4,5},{5,4},{6,7},{7,6},{8,9},{9,8},{10,11... | collective-permute-start | bytes 393224 | tf_op jit(solution)/shard_map/ppermute | solution.py:31
  48.3 7.9 %collective-permute-start.19 = (bf16[64,1024]{1,0:T(8,128)(2,1)S(1)}, bf16[64,1024]{1,0:T(8,128)(2,1)S(1)}, u32[]{:S(2)}, u32[]{:S(2)}) collective-permute-start(bf16[64,1024]{1,0:T(8,128)(2,1)S(1)} %get-tuple-element.85), channel_id=1, source_target_pairs={{0,3},{1,2},{2,1},{3,0},{4,7},{5,6},{6,5},{7,4},{8,11},{9,10},{10,... | collective-permute-start | bytes 393224 | tf_op jit(solution)/shard_map/ppermute | solution.py:31
  56.3 1.6 %collective-permute-start.20 = (bf16[2,2,32,1024]{3,2,1,0:T(8,128)(2,1)S(1)}, bf16[2,2,32,1024]{3,2,1,0:T(8,128)(2,1)S(1)}, u32[]{:S(2)}, u32[]{:S(2)}) collective-permute-start(bf16[2,2,32,1024]{3,2,1,0:T(8,128)(2,1)S(1)} %get-tuple-element.89), channel_id=1, source_target_pairs={{0,1},{1,0},{2,3},{3,2},{4,5},{5,4},{6,7},{7,6},{8,9},{9,8},{10,11... | collective-permute-start | bytes 786440 | tf_op jit(solution)/shard_map/ppermute | solution.py:31
  56.4 7.8 %collective-permute-start.23 = (bf16[32,32,128]{2,1,0:T(8,128)(2,1)S(1)}, bf16[32,32,128]{2,1,0:T(8,128)(2,1)S(1)}, u32[]{:S(2)}, u32[]{:S(2)}) collective-permute-start(bf16[32,32,128]{2,1,0:T(8,128)(2,1)S(1)} %shard_map.77.refs_0_), channel_id=1, source_target_pairs={{0,1},{1,0},{2,3},{3,2},{4,5},{5,4},{6,7},{7,6},{8,9},{9,8},{10,11... | collective-permute-start | bytes 786440 | tf_op jit(solution)/shard_map/ppermute | solution.py:31
  56.9 11.8 %collective-permute-start.24 = (bf16[32,32,128]{2,1,0:T(8,128)(2,1)S(1)}, bf16[32,32,128]{2,1,0:T(8,128)(2,1)S(1)}, u32[]{:S(2)}, u32[]{:S(2)}) collective-permute-start(bf16[32,32,128]{2,1,0:T(8,128)(2,1)S(1)} %collective-permute-done.14.refs_2_), channel_id=1, source_target_pairs={{0,1},{1,0},{2,3},{3,2},{4,5},{5,4},{6,7},{7,6},{8,9},{9,8},{10,11... | collective-permute-start | bytes 786440 | tf_op jit(solution)/shard_map/ppermute | solution.py:31
  58.0 5.6 %collective-permute-start.26 = (bf16[2,1,32,1024]{3,2,1,0:T(8,128)(2,1)S(1)}, bf16[2,1,32,1024]{3,2,1,0:T(8,128)(2,1)S(1)}, u32[]{:S(2)}, u32[]{:S(2)}) collective-permute-start(bf16[2,1,32,1024]{3,2,1,0:T(8,128)(2,1)S(1)} %get-tuple-element.90), channel_id=1, source_target_pairs={{0,2},{1,3},{2,0},{3,1},{4,6},{5,7},{6,4},{7,5},{8,10},{9,11},{10,... | collective-permute-start | bytes 393224 | tf_op jit(solution)/shard_map/ppermute | solution.py:31
  59.6 9.2 %collective-permute-start.25 = (bf16[32,32,128]{2,1,0:T(8,128)(2,1)S(1)}, bf16[32,32,128]{2,1,0:T(8,128)(2,1)S(1)}, u32[]{:S(2)}, u32[]{:S(2)}) collective-permute-start(bf16[32,32,128]{2,1,0:T(8,128)(2,1)S(1)} %shard_map.83.refs_4_), channel_id=1, source_target_pairs={{0,1},{1,0},{2,3},{3,2},{4,5},{5,4},{6,7},{7,6},{8,9},{9,8},{10,11... | collective-permute-start | bytes 786440 | tf_op jit(solution)/shard_map/ppermute | solution.py:31
  59.6 6.5 %collective-permute-start.21 = (bf16[64,1024]{1,0:T(8,128)(2,1)S(1)}, bf16[64,1024]{1,0:T(8,128)(2,1)S(1)}, u32[]{:S(2)}, u32[]{:S(2)}) collective-permute-start(bf16[64,1024]{1,0:T(8,128)(2,1)S(1)} %shard_map.80), channel_id=1, source_target_pairs={{0,16},{1,17},{2,18},{3,19},{4,20},{5,21},{6,22},{7,23},{8,24},{9,... | collective-permute-start | bytes 393224 | tf_op jit(solution)/shard_map/ppermute | solution.py:31
  63.6 9.4 %collective-permute-start.27 = (bf16[64,1024]{1,0:T(8,128)(2,1)S(1)}, bf16[64,1024]{1,0:T(8,128)(2,1)S(1)}, u32[]{:S(2)}, u32[]{:S(2)}) collective-permute-start(bf16[64,1024]{1,0:T(8,128)(2,1)S(1)} %get-tuple-element.100), channel_id=1, source_target_pairs={{0,16},{1,17},{2,18},{3,19},{4,20},{5,21},{6,22},{7,23},{8,24},{9,... | collective-permute-start | bytes 393224 | tf_op jit(solution)/shard_map/ppermute | solution.py:31
  64.1 8.8 %collective-permute-start.28 = (bf16[64,1024]{1,0:T(8,128)(2,1)S(1)}, bf16[64,1024]{1,0:T(8,128)(2,1)S(1)}, u32[]{:S(2)}, u32[]{:S(2)}) collective-permute-start(bf16[64,1024]{1,0:T(8,128)(2,1)S(1)} %get-tuple-element.103), channel_id=1, source_target_pairs={{0,16},{1,17},{2,18},{3,19},{4,20},{5,21},{6,22},{7,23},{8,24},{9,... | collective-permute-start | bytes 393224 | tf_op jit(solution)/shard_map/ppermute | solution.py:31
  66.2 6.8 %collective-permute-start.22 = (bf16[64,1024]{1,0:T(8,128)(2,1)S(1)}, bf16[64,1024]{1,0:T(8,128)(2,1)S(1)}, u32[]{:S(2)}, u32[]{:S(2)}) collective-permute-start(bf16[64,1024]{1,0:T(8,128)(2,1)S(1)} %collective-permute-done.21), channel_id=1, source_target_pairs={{0,12},{1,13},{2,14},{3,15},{4,8},{5,9},{6,10},{7,11},{8,4},{9,5},... | collective-permute-start | bytes 393224 | tf_op jit(solution)/shard_map/ppermute | solution.py:31

commit v7 on v6

--- a/solution.py
+++ b/solution.py
@@ -240,24 +240,44 @@
     out[...] = (total / scale).astype(out.dtype)
 
 
-def passed_kernel(base, piece, out):
+def apart_kernel(carried, out, done):
+    _, _, width = out.shape
+    copies = []
+    for i in range(out.shape[0]):
+        device = shifted(lax.axis_index("dp"), i + 1, out.shape[0] + 1)
+        columns = pl.ds(pl.multiple_of(device * width, width), width)
+        copies.append(pltpu.make_async_copy(carried.at[:, columns], out.at[i], done.at[i]))
+        copies[-1].start()
+    for copy in copies:
+        copy.wait()
+
+
+def merged_kernel(carried, piece, out):
     width = piece.shape[1]
+    columns = pl.ds(pl.multiple_of(lax.axis_index("dp") * width, width), width)
+    out[...] = added(carried[:, columns], piece[...])
+
+
+def first_kernel(piece, out, total, done):
+    width = piece.shape[1]
+    columns = pl.ds(pl.multiple_of(lax.axis_index("dp") * width, width), width)
     sent = lax.axis_index("section") < lax.axis_size("section") - 1
-    out[...] = jnp.where(sent, base[...], jnp.zeros(base.shape, BF16))
-    here = (slice(None), pl.ds(pl.multiple_of(lax.axis_index("dp") * width, width), width))
-    out[here] = jnp.where(sent, added(base[here], piece[...]), jnp.zeros(piece.shape, BF16))
+    total[...] = jnp.where(sent, piece[...], jnp.zeros(piece.shape, BF16))
+    copy = pltpu.make_async_copy(total, out.at[:, columns], done)
+    copy.start()
+    copy.wait()
 
 
 def last_kernel(blocks, base, *refs):
     *pieces, _, out, total, done = refs
     width = pieces[0].shape[1]
-    replicas = base.shape[1] // width
+    replicas = base.shape[0] + 1
     sent = lax.axis_index("section") < lax.axis_size("section") - 1
     copies = []
     for i, (block, piece) in enumerate(zip(blocks, pieces)):
         device = shifted(lax.axis_index("dp"), block, replicas)
         columns = pl.ds(pl.multiple_of(device * width, width), width)
-        total[i] = jnp.where(sent, added(base[:, columns], piece[...]), jnp.zeros(piece.shape, BF16))
+        total[i] = jnp.where(sent, added(base[block - 1], piece[...]), jnp.zeros(piece.shape, BF16))
         copies.append(pltpu.make_async_copy(total.at[i], out.at[:, columns], done.at[i]))
         copies[-1].start()
     for copy in copies:
@@ -385,7 +405,14 @@
     )
     a_next, b_next = up(a), down(b)
     carried, *_ = together(carried_grad[0, 0], a, b)
-    base = returned(carried, 0)
+    base = call(
+        apart_kernel,
+        [(last, rows, width)],
+        carried,
+        in_specs=[HBM],
+        scratch_shapes=[pltpu.SemaphoreType.DMA((last,))],
+    )[0]
+    base = returned(base, 0)
     w = call(held_kernel, [w.shape], w, in_specs=[HBM], scratch_shapes=[pltpu.SemaphoreType.DMA])[0]
     at = a.shape[0] - up_count
     a_parts, b_parts, ats = [a], [b], [at]
@@ -398,7 +425,7 @@
     b_parts.append(b)
     ats.append(at)
     a_next, b_next = up(a[2 * x_count :]), down(b[2 * x_count :])
-    zero = returned(out, 0)
+    zero = returned(call(merged_kernel, [(rows, width)], carried_grad[0, 0], out)[0], 0)
     keep_a, give_a, keep_b, give_b = product((a, at), (b, at), groups=2)
     keep, give = fold(2, keep_a, across(give_a, 1), keep_b, across(give_b, 1))
     nears = finished(keep, across(give, 2), 1, 1)
@@ -429,7 +456,13 @@
     b_parts.append(b)
     ats.append(at)
     keep, give = product((a, at), (b, at), flops=2 * tokens * hidden * width)
-    passed = call(passed_kernel, [(rows, replicas * width)], base, zero)[0]
+    passed = call(
+        first_kernel,
+        [(rows, replicas * width)],
+        zero,
+        out_specs=[HBM],
+        scratch_shapes=[pltpu.VMEM((rows, width), BF16), pltpu.SemaphoreType.DMA],
+    )[0]
     x_far, give, out, passed = together(x_far, give, out, passed)
     keep, give = fold(2, keep, across(give, 1))
     got = across(give, 2)

time: 74 us -> 72.8 us (0.984)
  waiting for transfers between devices: 30.5 us -> 27.3 us
  starting transfers between devices: 29.1 us -> 30.9 us
    ppermute x29, waiting for transfers between devices: 30.5 us -> 27.3 us  [moved(): return lax.ppermute(value, AXES, pairs)]
    ppermute x29, starting transfers between devices: 29.1 us -> 30.9 us  [moved(): return lax.ppermute(value, AXES, pairs)]
    unnamed x2 -> x4, local copies, waits for them, and re-layouts: 1.5 us -> 1.71 us
    pallas_call x19 -> x21, Pallas kernels: 11.8 us -> 11.8 us  [call(): pl.pallas_call(kernel, out_shape=[v if hasattr(v, 'dtype') else jax.Shape...]
  transfers between devices with their start and end apart: 29 -> 29, of which waited for: 11 -> 10; matrix products, arithmetic and copies ran while one was open for 0% -> 0% of each run, Pallas kernels for 13% -> 13%
where the time goes in v7:
time: 72.8 us; the launch traced here: 72.6 us
  starting transfers between devices  30.9 us (42%)
  waiting for transfers between devices  27.3 us (38%)
  Pallas kernels  11.8 us (16%)
  local copies, waits for them, and re-layouts  1.78 us (2%)
  between operations  0.88 us (1%)
    ppermute x29, starting transfers between devices, moved(): return lax.ppermute(value, AXES, pairs)  30.9 us
    ppermute x29, waiting for transfers between devices, moved(): return lax.ppermute(value, AXES, pairs)  27.3 us
    pallas_call x21, Pallas kernels, call(): pl.pallas_call(kernel, out_shape=[v if hasattr(v, 'dtype') else jax.Shape...  11.8 us
    unnamed x4, local copies, waits for them, and re-layouts  1.71 us
  transfers between devices with their start and end apart: 29, of which 10 were waited for; matrix products, arithmetic and copies ran while one was open for 0% of the time, Pallas kernels for 13%

profile of v7, /device:TPU:0, one launch (start us, length us, event | category | flops | bytes accessed | tf_op | source)
XLA Modules:
  0.0 72.6 jit_solution(5349744044154992704)
XLA Ops:
  0.6 1.6 %shard_map.68 = (bf16[52,32,128]{2,1,0:T(8,128)(2,1)S(1)}, bf16[52,32,128]{2,1,0:T(8,128)(2,1)S(1)}, bf16[16,32,128]{2,1,0:T(8,128)(2,1)S(1)}) custom-call(bf16[256,896]{1,0:T(8,128)(2,1)} %bitcast.13, bf16[256,896]{1,0:T(8,128)(2,1)} %bitcast.14, bf16[64,4096]{1,0:T(8,128)(2,1)} %bitcast.12), custom_call_target="tpu_custom_call" | custom-call | tf_op jit(solution)/shard_map/pallas_call | solution.py:50
  2.3 3.1 %collective-permute-start = (bf16[52,32,128]{2,1,0:T(8,128)(2,1)S(1)}, bf16[52,32,128]{2,1,0:T(8,128)(2,1)S(1)}, u32[]{:S(2)}, u32[]{:S(2)}) collective-permute-start(bf16[52,32,128]{2,1,0:T(8,128)(2,1)S(1)} %get-tuple-element.55.refs_0_.refs_2_), channel_id=1, source_target_pairs={{0,4},{1,5},{2,6},{3,7},{4,12},{5,13},{6,14},{7,15},{8,0},{9,1},{1... | collective-permute-start | bytes 1277960 | tf_op jit(solution)/shard_map/ppermute | solution.py:31
  5.4 1.1 %collective-permute-start.1 = (bf16[52,32,128]{2,1,0:T(8,128)(2,1)S(1)}, bf16[52,32,128]{2,1,0:T(8,128)(2,1)S(1)}, u32[]{:S(2)}, u32[]{:S(2)}) collective-permute-start(bf16[52,32,128]{2,1,0:T(8,128)(2,1)S(1)} %get-tuple-element.56.refs_1_.refs_3_), channel_id=1, source_target_pairs={{0,8},{1,9},{2,10},{3,11},{4,0},{5,1},{6,2},{7,3},{8,12},{9,13},{1... | collective-permute-start | bytes 1277960 | tf_op jit(solution)/shard_map/ppermute | solution.py:31
  6.4 1.8 %collective-permute-start.6 = (bf16[16,32,128]{2,1,0:T(8,128)(2,1)S(1)}, bf16[16,32,128]{2,1,0:T(8,128)(2,1)S(1)}, u32[]{:S(2)}, u32[]{:S(2)}) collective-permute-start(bf16[16,32,128]{2,1,0:T(8,128)(2,1)S(1)} %get-tuple-element.62.refs_0_), channel_id=1, source_target_pairs={{0,2},{1,3},{2,0},{3,1},{4,6},{5,7},{6,4},{7,5},{8,10},{9,11},{10,... | collective-permute-start | bytes 393224 | tf_op jit(solution)/shard_map/ppermute | solution.py:31
  8.2 1.5 %copy-done.1 = bf16[1,1024,896]{2,1,0:T(8,128)(2,1)S(1)} copy-done((bf16[1,1024,896]{2,1,0:T(8,128)(2,1)S(1)}, bf16[1,1024,896]{2,1,0:T(8,128)(2,1)}, u32[]{:S(2)}) %copy-start.1) | copy-done | bytes 1835032
  11.0 1.6 %collective-permute-start.2 = (bf16[3,64,1024]{2,1,0:T(8,128)(2,1)S(1)}, bf16[3,64,1024]{2,1,0:T(8,128)(2,1)S(1)}, u32[]{:S(2)}, u32[]{:S(2)}) collective-permute-start(bf16[3,64,1024]{2,1,0:T(8,128)(2,1)S(1)} %shard_map.69), channel_id=1, source_target_pairs={{0,16},{1,17},{2,18},{3,19},{4,20},{5,21},{6,22},{7,23},{8,24},{9,... | collective-permute-start | bytes 1179656 | tf_op jit(solution)/shard_map/ppermute | solution.py:31
  13.3 4.7 %collective-permute-done.4.refs_2_ = bf16[64,1024]{1,0:T(8,128)(2,1)S(1)} collective-permute-done((bf16[64,1024]{1,0:T(8,128)(2,1)S(1)}, bf16[64,1024]{1,0:T(8,128)(2,1)S(1)}, u32[]{:S(2)}, u32[]{:S(2)}) %collective-permute-start.4) | collective-permute-done | bytes 131104 | tf_op jit(solution)/shard_map/ppermute | solution.py:31
  18.0 5.2 %collective-permute-done.5.refs_3_ = bf16[64,1024]{1,0:T(8,128)(2,1)S(1)} collective-permute-done((bf16[64,1024]{1,0:T(8,128)(2,1)S(1)}, bf16[64,1024]{1,0:T(8,128)(2,1)S(1)}, u32[]{:S(2)}, u32[]{:S(2)}) %collective-permute-start.5) | collective-permute-done | bytes 131104 | tf_op jit(solution)/shard_map/ppermute | solution.py:31
  23.3 2.1 %collective-permute-done.1.refs_1_.refs_7_ = bf16[52,32,128]{2,1,0:T(8,128)(2,1)S(1)} collective-permute-done((bf16[52,32,128]{2,1,0:T(8,128)(2,1)S(1)}, bf16[52,32,128]{2,1,0:T(8,128)(2,1)S(1)}, u32[]{:S(2)}, u32[]{:S(2)}) %collective-permute-start.1) | collective-permute-done | bytes 426016 | tf_op jit(solution)/shard_map/ppermute | solution.py:31
  25.3 1.8 %collective-permute-start.8 = (bf16[36,32,128]{2,1,0:T(8,128)(2,1)S(1)}, bf16[36,32,128]{2,1,0:T(8,128)(2,1)S(1)}, u32[]{:S(2)}, u32[]{:S(2)}) collective-permute-start(bf16[36,32,128]{2,1,0:T(8,128)(2,1)S(1)} %slice.12), channel_id=1, source_target_pairs={{0,4},{1,5},{2,6},{3,7},{4,12},{5,13},{6,14},{7,15},{8,0},{9,1},{1... | collective-permute-start | bytes 884744 | tf_op jit(solution)/shard_map/ppermute | solution.py:31
  27.2 1.2 %collective-permute-start.9 = (bf16[36,32,128]{2,1,0:T(8,128)(2,1)S(1)}, bf16[36,32,128]{2,1,0:T(8,128)(2,1)S(1)}, u32[]{:S(2)}, u32[]{:S(2)}) collective-permute-start(bf16[36,32,128]{2,1,0:T(8,128)(2,1)S(1)} %slice.13), channel_id=1, source_target_pairs={{0,8},{1,9},{2,10},{3,11},{4,0},{5,1},{6,2},{7,3},{8,12},{9,13},{1... | collective-permute-start | bytes 884744 | tf_op jit(solution)/shard_map/ppermute | solution.py:31
  28.4 0.7 %shard_map.76 = (bf16[1,2,32,1024]{3,2,1,0:T(8,128)(2,1)S(1)}, bf16[1,2,32,1024]{3,2,1,0:T(8,128)(2,1)S(1)}, bf16[1,2,32,1024]{3,2,1,0:T(8,128)(2,1)S(1)}, bf16[1,2,32,1024]{3,2,1,0:T(8,128)(2,1)S(1)}) custom-call(bf16[52,32,128]{2,1,0:T(8,128)(2,1)S(1)} %collective-permute-done.refs_0_.refs_6_, ...), custom_call_target="tpu_custom_call" | custom-call | tf_op jit(solution)/shard_map/pallas_call | solution.py:50
  29.7 1.6 %collective-permute-start.14 = (bf16[32,32,128]{2,1,0:T(8,128)(2,1)S(1)}, bf16[32,32,128]{2,1,0:T(8,128)(2,1)S(1)}, u32[]{:S(2)}, u32[]{:S(2)}) collective-permute-start(bf16[32,32,128]{2,1,0:T(8,128)(2,1)S(1)} %shard_map.79.refs_0_), channel_id=1, source_target_pairs={{0,2},{1,3},{2,0},{3,1},{4,6},{5,7},{6,4},{7,5},{8,10},{9,11},{10,... | collective-permute-start | bytes 786440 | tf_op jit(solution)/shard_map/ppermute | solution.py:31
  31.4 1.0 %collective-permute-start.13 = (bf16[2,1,32,1024]{3,2,1,0:T(8,128)(2,1)S(1)}, bf16[2,1,32,1024]{3,2,1,0:T(8,128)(2,1)S(1)}, u32[]{:S(2)}, u32[]{:S(2)}) collective-permute-start(bf16[2,1,32,1024]{3,2,1,0:T(8,128)(2,1)S(1)} %get-tuple-element.74), channel_id=1, source_target_pairs={{0,2},{1,3},{2,0},{3,1},{4,6},{5,7},{6,4},{7,5},{8,10},{9,11},{10,... | collective-permute-start | bytes 393224 | tf_op jit(solution)/shard_map/ppermute | solution.py:31
  32.5 1.6 %collective-permute-start.10 = (bf16[64,1024]{1,0:T(8,128)(2,1)S(1)}, bf16[64,1024]{1,0:T(8,128)(2,1)S(1)}, u32[]{:S(2)}, u32[]{:S(2)}) collective-permute-start(bf16[64,1024]{1,0:T(8,128)(2,1)S(1)} %shard_map.74), channel_id=1, source_target_pairs={{0,16},{1,17},{2,18},{3,19},{4,20},{5,21},{6,22},{7,23},{8,24},{9,... | collective-permute-start | bytes 393224 | tf_op jit(solution)/shard_map/ppermute | solution.py:31
  34.0 1.4 %shard_map.75.refs_12_ = f32[1024,896]{1,0:T(8,128)S(1)} custom-call(bf16[32,32,128]{2,1,0:T(8,128)(2,1)S(1)} %shard_map.73.refs_0_, bf16[32,32,128]{2,1,0:T(8,128)(2,1)S(1)} %collective-permute-done.7.refs_1_, bf16[52,32,128]{2,1,0:T(8,128)(2,1)S(1)} %get-tuple-element.55.refs_0_.refs_2_, bf16[52,32,128]{2,1,0:T(8,128)(2,1)S(1)} %get-tuple-element.56.refs_1_.refs_3_), custom_call_target="tpu_custom_call" | custom-call | tf_op jit(solution)/shard_map/pallas_call | solution.py:50
  35.4 5.5 %collective-permute-done.13.got = bf16[2,1,32,1024]{3,2,1,0:T(8,128)(2,1)S(1)} collective-permute-done((bf16[2,1,32,1024]{3,2,1,0:T(8,128)(2,1)S(1)}, bf16[2,1,32,1024]{3,2,1,0:T(8,128)(2,1)S(1)}, u32[]{:S(2)}, u32[]{:S(2)}) %collective-permute-start.13) | collective-permute-done | bytes 131104 | tf_op jit(solution)/shard_map/ppermute | solution.py:31
  41.6 0.8 %collective-permute-start.16 = (bf16[28,32,128]{2,1,0:T(8,128)(2,1)S(1)}, bf16[28,32,128]{2,1,0:T(8,128)(2,1)S(1)}, u32[]{:S(2)}, u32[]{:S(2)}) collective-permute-start(bf16[28,32,128]{2,1,0:T(8,128)(2,1)S(1)} %slice.14), channel_id=1, source_target_pairs={{0,4},{1,5},{2,6},{3,7},{4,12},{5,13},{6,14},{7,15},{8,0},{9,1},{1... | collective-permute-start | bytes 688136 | tf_op jit(solution)/shard_map/ppermute | solution.py:31
  42.4 2.2 %collective-permute-start.17 = (bf16[28,32,128]{2,1,0:T(8,128)(2,1)S(1)}, bf16[28,32,128]{2,1,0:T(8,128)(2,1)S(1)}, u32[]{:S(2)}, u32[]{:S(2)}) collective-permute-start(bf16[28,32,128]{2,1,0:T(8,128)(2,1)S(1)} %slice.15), channel_id=1, source_target_pairs={{0,8},{1,9},{2,10},{3,11},{4,0},{5,1},{6,2},{7,3},{8,12},{9,13},{1... | collective-permute-start | bytes 688136 | tf_op jit(solution)/shard_map/ppermute | solution.py:31
  44.7 0.7 %shard_map.80 = (bf16[64,1024]{1,0:T(8,128)(2,1)S(1)}, bf16[64,1024]{1,0:T(8,128)(2,1)S(1)}, bf16[32,32,128]{2,1,0:T(8,128)(2,1)S(1)}, bf16[64,1024]{1,0:T(8,128)(2,1)S(1)}) custom-call(bf16[36,32,128]{2,1,0:T(8,128)(2,1)S(1)} %collective-permute-done.8.refs_0_.refs_8_, bf16[36,32,128]{2,1,0:T(8,128)(2,1)S(1)} %collective-permute-done.9.refs_1_.refs_9_, ...), custom_call_target="tpu_custom_call" | custom-call | tf_op jit(solution)/shard_map/pallas_call | solution.py:50
  45.4 1.6 %collective-permute-start.15 = (bf16[32,32,128]{2,1,0:T(8,128)(2,1)S(1)}, bf16[32,32,128]{2,1,0:T(8,128)(2,1)S(1)}, u32[]{:S(2)}, u32[]{:S(2)}) collective-permute-start(bf16[32,32,128]{2,1,0:T(8,128)(2,1)S(1)} %get-tuple-element.81), channel_id=1, source_target_pairs={{0,2},{1,3},{2,0},{3,1},{4,6},{5,7},{6,4},{7,5},{8,10},{9,11},{10,... | collective-permute-start | bytes 786440 | tf_op jit(solution)/shard_map/ppermute | solution.py:31
  48.3 0.9 %collective-permute-done.16.refs_0_.refs_10_ = bf16[28,32,128]{2,1,0:T(8,128)(2,1)S(1)} collective-permute-done((bf16[28,32,128]{2,1,0:T(8,128)(2,1)S(1)}, bf16[28,32,128]{2,1,0:T(8,128)(2,1)S(1)}, u32[]{:S(2)}, u32[]{:S(2)}) %collective-permute-start.16) | collective-permute-done | bytes 229408 | tf_op jit(solution)/shard_map/ppermute | solution.py:31
  49.2 4.4 %collective-permute-done.17.refs_1_.refs_11_ = bf16[28,32,128]{2,1,0:T(8,128)(2,1)S(1)} collective-permute-done((bf16[28,32,128]{2,1,0:T(8,128)(2,1)S(1)}, bf16[28,32,128]{2,1,0:T(8,128)(2,1)S(1)}, u32[]{:S(2)}, u32[]{:S(2)}) %collective-permute-start.17) | collective-permute-done | bytes 229408 | tf_op jit(solution)/shard_map/ppermute | solution.py:31
  55.1 0.9 %collective-permute-done.20.refs_1_ = bf16[2,2,32,1024]{3,2,1,0:T(8,128)(2,1)S(1)} collective-permute-done((bf16[2,2,32,1024]{3,2,1,0:T(8,128)(2,1)S(1)}, bf16[2,2,32,1024]{3,2,1,0:T(8,128)(2,1)S(1)}, u32[]{:S(2)}, u32[]{:S(2)}) %collective-permute-start.20) | collective-permute-done | bytes 262176 | tf_op jit(solution)/shard_map/ppermute | solution.py:31
  56.1 1.6 %collective-permute-start.26 = (bf16[2,1,32,1024]{3,2,1,0:T(8,128)(2,1)S(1)}, bf16[2,1,32,1024]{3,2,1,0:T(8,128)(2,1)S(1)}, u32[]{:S(2)}, u32[]{:S(2)}) collective-permute-start(bf16[2,1,32,1024]{3,2,1,0:T(8,128)(2,1)S(1)} %get-tuple-element.90), channel_id=1, source_target_pairs={{0,2},{1,3},{2,0},{3,1},{4,6},{5,7},{6,4},{7,5},{8,10},{9,11},{10,... | collective-permute-start | bytes 393224 | tf_op jit(solution)/shard_map/ppermute | solution.py:31
  57.9 1.6 %collective-permute-start.21 = (bf16[64,1024]{1,0:T(8,128)(2,1)S(1)}, bf16[64,1024]{1,0:T(8,128)(2,1)S(1)}, u32[]{:S(2)}, u32[]{:S(2)}) collective-permute-start(bf16[64,1024]{1,0:T(8,128)(2,1)S(1)} %shard_map.82), channel_id=1, source_target_pairs={{0,16},{1,17},{2,18},{3,19},{4,20},{5,21},{6,22},{7,23},{8,24},{9,... | collective-permute-start | bytes 393224 | tf_op jit(solution)/shard_map/ppermute | solution.py:31
  59.4 2.3 %collective-permute-done.26.got = bf16[2,1,32,1024]{3,2,1,0:T(8,128)(2,1)S(1)} collective-permute-done((bf16[2,1,32,1024]{3,2,1,0:T(8,128)(2,1)S(1)}, bf16[2,1,32,1024]{3,2,1,0:T(8,128)(2,1)S(1)}, u32[]{:S(2)}, u32[]{:S(2)}) %collective-permute-start.26) | collective-permute-done | bytes 131104 | tf_op jit(solution)/shard_map/ppermute | solution.py:31
  61.8 1.6 %collective-permute-start.27 = (bf16[64,1024]{1,0:T(8,128)(2,1)S(1)}, bf16[64,1024]{1,0:T(8,128)(2,1)S(1)}, u32[]{:S(2)}, u32[]{:S(2)}) collective-permute-start(bf16[64,1024]{1,0:T(8,128)(2,1)S(1)} %get-tuple-element.100), channel_id=1, source_target_pairs={{0,16},{1,17},{2,18},{3,19},{4,20},{5,21},{6,22},{7,23},{8,24},{9,... | collective-permute-start | bytes 393224 | tf_op jit(solution)/shard_map/ppermute | solution.py:31
  63.4 1.5 %collective-permute-start.28 = (bf16[64,1024]{1,0:T(8,128)(2,1)S(1)}, bf16[64,1024]{1,0:T(8,128)(2,1)S(1)}, u32[]{:S(2)}, u32[]{:S(2)}) collective-permute-start(bf16[64,1024]{1,0:T(8,128)(2,1)S(1)} %get-tuple-element.103), channel_id=1, source_target_pairs={{0,16},{1,17},{2,18},{3,19},{4,20},{5,21},{6,22},{7,23},{8,24},{9,... | collective-permute-start | bytes 393224 | tf_op jit(solution)/shard_map/ppermute | solution.py:31
  64.9 2.6 %collective-permute-start.22 = (bf16[64,1024]{1,0:T(8,128)(2,1)S(1)}, bf16[64,1024]{1,0:T(8,128)(2,1)S(1)}, u32[]{:S(2)}, u32[]{:S(2)}) collective-permute-start(bf16[64,1024]{1,0:T(8,128)(2,1)S(1)} %collective-permute-done.21), channel_id=1, source_target_pairs={{0,12},{1,13},{2,14},{3,15},{4,8},{5,9},{6,10},{7,11},{8,4},{9,5},... | collective-permute-start | bytes 393224 | tf_op jit(solution)/shard_map/ppermute | solution.py:31
  67.5 3.6 %shard_map.87 = bf16[1024,896]{1,0:T(8,128)(2,1)} custom-call(bf16[32,32,128]{2,1,0:T(8,128)(2,1)S(1)} %shard_map.79.refs_0_, bf16[32,32,128]{2,1,0:T(8,128)(2,1)S(1)} %collective-permute-done.23.refs_1_, bf16[32,32,128]{2,1,0:T(8,128)(2,1)S(1)} %collective-permute-done.14.refs_2_, bf16[32,32,128]{2,1,0:T(8,128)(2,1)S(1)} %collective-permute-done.24.refs_3_, ...), custom_call_target="tpu_custom_call" | custom-call | tf_op jit(solution)/shard_map/pallas_call | solution.py:50
  71.8 0.8 %shard_map.88 = bf16[64,4096]{1,0:T(8,128)(2,1)} custom-call(bf16[3,64,1024]{2,1,0:T(8,128)(2,1)S(1)} %collective-permute-done.2.base, bf16[64,1024]{1,0:T(8,128)(2,1)S(1)} %collective-permute-done.22.refs_0_, bf16[64,1024]{1,0:T(8,128)(2,1)S(1)} %collective-permute-done.27.refs_1_, ...), custom_call_target="tpu_custom_call", output_to_operand_aliasing={{}: (4, {})} | custom-call | tf_op jit(solution)/shard_map/pallas_call | solution.py:50
  (55 shorter events, 7.1 us)
Async XLA Ops:
  2.3 21.0 %collective-permute-start = (bf16[52,32,128]{2,1,0:T(8,128)(2,1)S(1)}, bf16[52,32,128]{2,1,0:T(8,128)(2,1)S(1)}, u32[]{:S(2)}, u32[]{:S(2)}) collective-permute-start(bf16[52,32,128]{2,1,0:T(8,128)(2,1)S(1)} %get-tuple-element.55.refs_0_.refs_2_), channel_id=1, source_target_pairs={{0,4},{1,5},{2,6},{3,7},{4,12},{5,13},{6,14},{7,15},{8,0},{9,1},{1... | collective-permute-start | bytes 1277960 | tf_op jit(solution)/shard_map/ppermute | solution.py:31
  5.4 20.0 %collective-permute-start.1 = (bf16[52,32,128]{2,1,0:T(8,128)(2,1)S(1)}, bf16[52,32,128]{2,1,0:T(8,128)(2,1)S(1)}, u32[]{:S(2)}, u32[]{:S(2)}) collective-permute-start(bf16[52,32,128]{2,1,0:T(8,128)(2,1)S(1)} %get-tuple-element.56.refs_1_.refs_3_), channel_id=1, source_target_pairs={{0,8},{1,9},{2,10},{3,11},{4,0},{5,1},{6,2},{7,3},{8,12},{9,13},{1... | collective-permute-start | bytes 1277960 | tf_op jit(solution)/shard_map/ppermute | solution.py:31
  6.4 6.1 %collective-permute-start.6 = (bf16[16,32,128]{2,1,0:T(8,128)(2,1)S(1)}, bf16[16,32,128]{2,1,0:T(8,128)(2,1)S(1)}, u32[]{:S(2)}, u32[]{:S(2)}) collective-permute-start(bf16[16,32,128]{2,1,0:T(8,128)(2,1)S(1)} %get-tuple-element.62.refs_0_), channel_id=1, source_target_pairs={{0,2},{1,3},{2,0},{3,1},{4,6},{5,7},{6,4},{7,5},{8,10},{9,11},{10,... | collective-permute-start | bytes 393224 | tf_op jit(solution)/shard_map/ppermute | solution.py:31
  8.2 1.5 %copy-start.1 = (bf16[1,1024,896]{2,1,0:T(8,128)(2,1)S(1)}, bf16[1,1024,896]{2,1,0:T(8,128)(2,1)}, u32[]{:S(2)}) copy-start(bf16[1,1024,896]{2,1,0:T(8,128)(2,1)} %param.9) | copy-start | bytes 5505028
  9.9 1.0 %copy-start = (bf16[1,1,64,4096]{3,2,1,0:T(8,128)(2,1)S(1)}, bf16[1,1,64,4096]{3,2,1,0:T(8,128)(2,1)}, u32[]{:S(2)}) copy-start(bf16[1,1,64,4096]{3,2,1,0:T(8,128)(2,1)} %param.6) | copy-start | bytes 1572868
  10.6 2.6 %collective-permute-start.3 = (bf16[64,1024]{1,0:T(8,128)(2,1)S(1)}, bf16[64,1024]{1,0:T(8,128)(2,1)S(1)}, u32[]{:S(2)}, u32[]{:S(2)}) collective-permute-start(bf16[64,1024]{1,0:T(8,128)(2,1)S(1)} %get-tuple-element.59), channel_id=1, source_target_pairs={{0,1},{1,0},{2,3},{3,2},{4,5},{5,4},{6,7},{7,6},{8,9},{9,8},{10,11... | collective-permute-start | bytes 393224 | tf_op jit(solution)/shard_map/ppermute | solution.py:31
  11.0 12.2 %collective-permute-start.2 = (bf16[3,64,1024]{2,1,0:T(8,128)(2,1)S(1)}, bf16[3,64,1024]{2,1,0:T(8,128)(2,1)S(1)}, u32[]{:S(2)}, u32[]{:S(2)}) collective-permute-start(bf16[3,64,1024]{2,1,0:T(8,128)(2,1)S(1)} %shard_map.69), channel_id=1, source_target_pairs={{0,16},{1,17},{2,18},{3,19},{4,20},{5,21},{6,22},{7,23},{8,24},{9,... | collective-permute-start | bytes 1179656 | tf_op jit(solution)/shard_map/ppermute | solution.py:31
  12.6 5.4 %collective-permute-start.4 = (bf16[64,1024]{1,0:T(8,128)(2,1)S(1)}, bf16[64,1024]{1,0:T(8,128)(2,1)S(1)}, u32[]{:S(2)}, u32[]{:S(2)}) collective-permute-start(bf16[64,1024]{1,0:T(8,128)(2,1)S(1)} %get-tuple-element.60), channel_id=1, source_target_pairs={{0,2},{1,3},{2,0},{3,1},{4,6},{5,7},{6,4},{7,5},{8,10},{9,11},{10,... | collective-permute-start | bytes 393224 | tf_op jit(solution)/shard_map/ppermute | solution.py:31
  13.2 10.0 %collective-permute-start.7 = (bf16[32,32,128]{2,1,0:T(8,128)(2,1)S(1)}, bf16[32,32,128]{2,1,0:T(8,128)(2,1)S(1)}, u32[]{:S(2)}, u32[]{:S(2)}) collective-permute-start(bf16[32,32,128]{2,1,0:T(8,128)(2,1)S(1)} %shard_map.73.refs_0_), channel_id=1, source_target_pairs={{0,1},{1,0},{2,3},{3,2},{4,5},{5,4},{6,7},{7,6},{8,9},{9,8},{10,11... | collective-permute-start | bytes 786440 | tf_op jit(solution)/shard_map/ppermute | solution.py:31
  18.0 5.2 %collective-permute-start.5 = (bf16[64,1024]{1,0:T(8,128)(2,1)S(1)}, bf16[64,1024]{1,0:T(8,128)(2,1)S(1)}, u32[]{:S(2)}, u32[]{:S(2)}) collective-permute-start(bf16[64,1024]{1,0:T(8,128)(2,1)S(1)} %get-tuple-element.61), channel_id=1, source_target_pairs={{0,3},{1,2},{2,1},{3,0},{4,7},{5,6},{6,5},{7,4},{8,11},{9,10},{10,... | collective-permute-start | bytes 393224 | tf_op jit(solution)/shard_map/ppermute | solution.py:31
  25.3 16.2 %collective-permute-start.8 = (bf16[36,32,128]{2,1,0:T(8,128)(2,1)S(1)}, bf16[36,32,128]{2,1,0:T(8,128)(2,1)S(1)}, u32[]{:S(2)}, u32[]{:S(2)}) collective-permute-start(bf16[36,32,128]{2,1,0:T(8,128)(2,1)S(1)} %slice.12), channel_id=1, source_target_pairs={{0,4},{1,5},{2,6},{3,7},{4,12},{5,13},{6,14},{7,15},{8,0},{9,1},{1... | collective-permute-start | bytes 884744 | tf_op jit(solution)/shard_map/ppermute | solution.py:31
  27.2 14.4 %collective-permute-start.9 = (bf16[36,32,128]{2,1,0:T(8,128)(2,1)S(1)}, bf16[36,32,128]{2,1,0:T(8,128)(2,1)S(1)}, u32[]{:S(2)}, u32[]{:S(2)}) collective-permute-start(bf16[36,32,128]{2,1,0:T(8,128)(2,1)S(1)} %slice.13), channel_id=1, source_target_pairs={{0,8},{1,9},{2,10},{3,11},{4,0},{5,1},{6,2},{7,3},{8,12},{9,13},{1... | collective-permute-start | bytes 884744 | tf_op jit(solution)/shard_map/ppermute | solution.py:31
  29.1 2.2 %collective-permute-start.11 = (bf16[1,2,32,1024]{3,2,1,0:T(8,128)(2,1)S(1)}, bf16[1,2,32,1024]{3,2,1,0:T(8,128)(2,1)S(1)}, u32[]{:S(2)}, u32[]{:S(2)}) collective-permute-start(bf16[1,2,32,1024]{3,2,1,0:T(8,128)(2,1)S(1)} %get-tuple-element.70), channel_id=1, source_target_pairs={{0,1},{1,0},{2,3},{3,2},{4,5},{5,4},{6,7},{7,6},{8,9},{9,8},{10,11... | collective-permute-start | bytes 393224 | tf_op jit(solution)/shard_map/ppermute | solution.py:31
  29.2 2.2 %collective-permute-start.12 = (bf16[1,2,32,1024]{3,2,1,0:T(8,128)(2,1)S(1)}, bf16[1,2,32,1024]{3,2,1,0:T(8,128)(2,1)S(1)}, u32[]{:S(2)}, u32[]{:S(2)}) collective-permute-start(bf16[1,2,32,1024]{3,2,1,0:T(8,128)(2,1)S(1)} %get-tuple-element.72), channel_id=1, source_target_pairs={{0,1},{1,0},{2,3},{3,2},{4,5},{5,4},{6,7},{7,6},{8,9},{9,8},{10,11... | collective-permute-start | bytes 393224 | tf_op jit(solution)/shard_map/ppermute | solution.py:31
  29.7 14.9 %collective-permute-start.14 = (bf16[32,32,128]{2,1,0:T(8,128)(2,1)S(1)}, bf16[32,32,128]{2,1,0:T(8,128)(2,1)S(1)}, u32[]{:S(2)}, u32[]{:S(2)}) collective-permute-start(bf16[32,32,128]{2,1,0:T(8,128)(2,1)S(1)} %shard_map.79.refs_0_), channel_id=1, source_target_pairs={{0,2},{1,3},{2,0},{3,1},{4,6},{5,7},{6,4},{7,5},{8,10},{9,11},{10,... | collective-permute-start | bytes 786440 | tf_op jit(solution)/shard_map/ppermute | solution.py:31
  31.4 9.5 %collective-permute-start.13 = (bf16[2,1,32,1024]{3,2,1,0:T(8,128)(2,1)S(1)}, bf16[2,1,32,1024]{3,2,1,0:T(8,128)(2,1)S(1)}, u32[]{:S(2)}, u32[]{:S(2)}) collective-permute-start(bf16[2,1,32,1024]{3,2,1,0:T(8,128)(2,1)S(1)} %get-tuple-element.74), channel_id=1, source_target_pairs={{0,2},{1,3},{2,0},{3,1},{4,6},{5,7},{6,4},{7,5},{8,10},{9,11},{10,... | collective-permute-start | bytes 393224 | tf_op jit(solution)/shard_map/ppermute | solution.py:31
  32.5 8.5 %collective-permute-start.10 = (bf16[64,1024]{1,0:T(8,128)(2,1)S(1)}, bf16[64,1024]{1,0:T(8,128)(2,1)S(1)}, u32[]{:S(2)}, u32[]{:S(2)}) collective-permute-start(bf16[64,1024]{1,0:T(8,128)(2,1)S(1)} %shard_map.74), channel_id=1, source_target_pairs={{0,16},{1,17},{2,18},{3,19},{4,20},{5,21},{6,22},{7,23},{8,24},{9,... | collective-permute-start | bytes 393224 | tf_op jit(solution)/shard_map/ppermute | solution.py:31
  41.6 7.6 %collective-permute-start.16 = (bf16[28,32,128]{2,1,0:T(8,128)(2,1)S(1)}, bf16[28,32,128]{2,1,0:T(8,128)(2,1)S(1)}, u32[]{:S(2)}, u32[]{:S(2)}) collective-permute-start(bf16[28,32,128]{2,1,0:T(8,128)(2,1)S(1)} %slice.14), channel_id=1, source_target_pairs={{0,4},{1,5},{2,6},{3,7},{4,12},{5,13},{6,14},{7,15},{8,0},{9,1},{1... | collective-permute-start | bytes 688136 | tf_op jit(solution)/shard_map/ppermute | solution.py:31
  42.4 11.2 %collective-permute-start.17 = (bf16[28,32,128]{2,1,0:T(8,128)(2,1)S(1)}, bf16[28,32,128]{2,1,0:T(8,128)(2,1)S(1)}, u32[]{:S(2)}, u32[]{:S(2)}) collective-permute-start(bf16[28,32,128]{2,1,0:T(8,128)(2,1)S(1)} %slice.15), channel_id=1, source_target_pairs={{0,8},{1,9},{2,10},{3,11},{4,0},{5,1},{6,2},{7,3},{8,12},{9,13},{1... | collective-permute-start | bytes 688136 | tf_op jit(solution)/shard_map/ppermute | solution.py:31
  45.4 9.0 %collective-permute-start.15 = (bf16[32,32,128]{2,1,0:T(8,128)(2,1)S(1)}, bf16[32,32,128]{2,1,0:T(8,128)(2,1)S(1)}, u32[]{:S(2)}, u32[]{:S(2)}) collective-permute-start(bf16[32,32,128]{2,1,0:T(8,128)(2,1)S(1)} %get-tuple-element.81), channel_id=1, source_target_pairs={{0,2},{1,3},{2,0},{3,1},{4,6},{5,7},{6,4},{7,5},{8,10},{9,11},{10,... | collective-permute-start | bytes 786440 | tf_op jit(solution)/shard_map/ppermute | solution.py:31
  47.1 7.3 %collective-permute-start.18 = (bf16[64,1024]{1,0:T(8,128)(2,1)S(1)}, bf16[64,1024]{1,0:T(8,128)(2,1)S(1)}, u32[]{:S(2)}, u32[]{:S(2)}) collective-permute-start(bf16[64,1024]{1,0:T(8,128)(2,1)S(1)} %get-tuple-element.84), channel_id=1, source_target_pairs={{0,1},{1,0},{2,3},{3,2},{4,5},{5,4},{6,7},{7,6},{8,9},{9,8},{10,11... | collective-permute-start | bytes 393224 | tf_op jit(solution)/shard_map/ppermute | solution.py:31
  47.1 7.3 %collective-permute-start.19 = (bf16[64,1024]{1,0:T(8,128)(2,1)S(1)}, bf16[64,1024]{1,0:T(8,128)(2,1)S(1)}, u32[]{:S(2)}, u32[]{:S(2)}) collective-permute-start(bf16[64,1024]{1,0:T(8,128)(2,1)S(1)} %get-tuple-element.85), channel_id=1, source_target_pairs={{0,3},{1,2},{2,1},{3,0},{4,7},{5,6},{6,5},{7,4},{8,11},{9,10},{10,... | collective-permute-start | bytes 393224 | tf_op jit(solution)/shard_map/ppermute | solution.py:31
  54.5 1.6 %collective-permute-start.20 = (bf16[2,2,32,1024]{3,2,1,0:T(8,128)(2,1)S(1)}, bf16[2,2,32,1024]{3,2,1,0:T(8,128)(2,1)S(1)}, u32[]{:S(2)}, u32[]{:S(2)}) collective-permute-start(bf16[2,2,32,1024]{3,2,1,0:T(8,128)(2,1)S(1)} %get-tuple-element.89), channel_id=1, source_target_pairs={{0,1},{1,0},{2,3},{3,2},{4,5},{5,4},{6,7},{7,6},{8,9},{9,8},{10,11... | collective-permute-start | bytes 786440 | tf_op jit(solution)/shard_map/ppermute | solution.py:31
  54.6 8.7 %collective-permute-start.23 = (bf16[32,32,128]{2,1,0:T(8,128)(2,1)S(1)}, bf16[32,32,128]{2,1,0:T(8,128)(2,1)S(1)}, u32[]{:S(2)}, u32[]{:S(2)}) collective-permute-start(bf16[32,32,128]{2,1,0:T(8,128)(2,1)S(1)} %shard_map.79.refs_0_), channel_id=1, source_target_pairs={{0,1},{1,0},{2,3},{3,2},{4,5},{5,4},{6,7},{7,6},{8,9},{9,8},{10,11... | collective-permute-start | bytes 786440 | tf_op jit(solution)/shard_map/ppermute | solution.py:31
  55.0 12.4 %collective-permute-start.24 = (bf16[32,32,128]{2,1,0:T(8,128)(2,1)S(1)}, bf16[32,32,128]{2,1,0:T(8,128)(2,1)S(1)}, u32[]{:S(2)}, u32[]{:S(2)}) collective-permute-start(bf16[32,32,128]{2,1,0:T(8,128)(2,1)S(1)} %collective-permute-done.14.refs_2_), channel_id=1, source_target_pairs={{0,1},{1,0},{2,3},{3,2},{4,5},{5,4},{6,7},{7,6},{8,9},{9,8},{10,11... | collective-permute-start | bytes 786440 | tf_op jit(solution)/shard_map/ppermute | solution.py:31
  56.1 5.6 %collective-permute-start.26 = (bf16[2,1,32,1024]{3,2,1,0:T(8,128)(2,1)S(1)}, bf16[2,1,32,1024]{3,2,1,0:T(8,128)(2,1)S(1)}, u32[]{:S(2)}, u32[]{:S(2)}) collective-permute-start(bf16[2,1,32,1024]{3,2,1,0:T(8,128)(2,1)S(1)} %get-tuple-element.90), channel_id=1, source_target_pairs={{0,2},{1,3},{2,0},{3,1},{4,6},{5,7},{6,4},{7,5},{8,10},{9,11},{10,... | collective-permute-start | bytes 393224 | tf_op jit(solution)/shard_map/ppermute | solution.py:31
  57.8 9.7 %collective-permute-start.25 = (bf16[32,32,128]{2,1,0:T(8,128)(2,1)S(1)}, bf16[32,32,128]{2,1,0:T(8,128)(2,1)S(1)}, u32[]{:S(2)}, u32[]{:S(2)}) collective-permute-start(bf16[32,32,128]{2,1,0:T(8,128)(2,1)S(1)} %shard_map.85.refs_4_), channel_id=1, source_target_pairs={{0,1},{1,0},{2,3},{3,2},{4,5},{5,4},{6,7},{7,6},{8,9},{9,8},{10,11... | collective-permute-start | bytes 786440 | tf_op jit(solution)/shard_map/ppermute | solution.py:31
  57.9 7.1 %collective-permute-start.21 = (bf16[64,1024]{1,0:T(8,128)(2,1)S(1)}, bf16[64,1024]{1,0:T(8,128)(2,1)S(1)}, u32[]{:S(2)}, u32[]{:S(2)}) collective-permute-start(bf16[64,1024]{1,0:T(8,128)(2,1)S(1)} %shard_map.82), channel_id=1, source_target_pairs={{0,16},{1,17},{2,18},{3,19},{4,20},{5,21},{6,22},{7,23},{8,24},{9,... | collective-permute-start | bytes 393224 | tf_op jit(solution)/shard_map/ppermute | solution.py:31
  61.8 9.3 %collective-permute-start.27 = (bf16[64,1024]{1,0:T(8,128)(2,1)S(1)}, bf16[64,1024]{1,0:T(8,128)(2,1)S(1)}, u32[]{:S(2)}, u32[]{:S(2)}) collective-permute-start(bf16[64,1024]{1,0:T(8,128)(2,1)S(1)} %get-tuple-element.100), channel_id=1, source_target_pairs={{0,16},{1,17},{2,18},{3,19},{4,20},{5,21},{6,22},{7,23},{8,24},{9,... | collective-permute-start | bytes 393224 | tf_op jit(solution)/shard_map/ppermute | solution.py:31
  63.4 7.8 %collective-permute-start.28 = (bf16[64,1024]{1,0:T(8,128)(2,1)S(1)}, bf16[64,1024]{1,0:T(8,128)(2,1)S(1)}, u32[]{:S(2)}, u32[]{:S(2)}) collective-permute-start(bf16[64,1024]{1,0:T(8,128)(2,1)S(1)} %get-tuple-element.103), channel_id=1, source_target_pairs={{0,16},{1,17},{2,18},{3,19},{4,20},{5,21},{6,22},{7,23},{8,24},{9,... | collective-permute-start | bytes 393224 | tf_op jit(solution)/shard_map/ppermute | solution.py:31
  64.9 6.9 %collective-permute-start.22 = (bf16[64,1024]{1,0:T(8,128)(2,1)S(1)}, bf16[64,1024]{1,0:T(8,128)(2,1)S(1)}, u32[]{:S(2)}, u32[]{:S(2)}) collective-permute-start(bf16[64,1024]{1,0:T(8,128)(2,1)S(1)} %collective-permute-done.21), channel_id=1, source_target_pairs={{0,12},{1,13},{2,14},{3,15},{4,8},{5,9},{6,10},{7,11},{8,4},{9,5},... | collective-permute-start | bytes 393224 | tf_op jit(solution)/shard_map/ppermute | solution.py:31

commit v8 on v7

--- a/solution.py
+++ b/solution.py
@@ -357,7 +357,7 @@
     for i in range(steps - 1):
         order += [j + (far_step >> i) for j in order]
 
-    tile = 256
+    tile = 512
 
     def weight_product(xs, pairs, parts, *so_far, final):
         groups, at = [], 0

time: 72.8 us -> 72.8 us (level)
  Pallas kernels: 11.8 us -> 11 us
  waiting for transfers between devices: 27.3 us -> 28.1 us
    ppermute x29, waiting for transfers between devices: 27.3 us -> 28.1 us  [moved(): return lax.ppermute(value, AXES, pairs)]
    pallas_call x21, Pallas kernels: 11.8 us -> 11 us  [call(): pl.pallas_call(kernel, out_shape=[v if hasattr(v, 'dtype') else jax.Shape...]
  transfers between devices with their start and end apart: 29 -> 29, of which waited for: 10 -> 11; matrix products, arithmetic and copies ran while one was open for 0% -> 0% of each run, Pallas kernels for 13% -> 12%
where the time goes in v8:
time: 72.8 us; the launch traced here: 72.6 us
  starting transfers between devices  30.9 us (42%)
  waiting for transfers between devices  28.1 us (39%)
  Pallas kernels  11 us (15%)
  local copies, waits for them, and re-layouts  1.78 us (2%)
  between operations  0.88 us (1%)
    ppermute x29, starting transfers between devices, moved(): return lax.ppermute(value, AXES, pairs)  30.9 us
    ppermute x29, waiting for transfers between devices, moved(): return lax.ppermute(value, AXES, pairs)  28.1 us
    pallas_call x21, Pallas kernels, call(): pl.pallas_call(kernel, out_shape=[v if hasattr(v, 'dtype') else jax.Shape...  11 us
    unnamed x4, local copies, waits for them, and re-layouts  1.71 us
  transfers between devices with their start and end apart: 29, of which 11 were waited for; matrix products, arithmetic and copies ran while one was open for 0% of the time, Pallas kernels for 12%

profile of v8, /device:TPU:0, one launch (start us, length us, event | category | flops | bytes accessed | tf_op | source)
XLA Modules:
  0.0 72.6 jit_solution(9127824511471457280)
XLA Ops:
  0.6 1.6 %shard_map.68 = (bf16[52,32,128]{2,1,0:T(8,128)(2,1)S(1)}, bf16[52,32,128]{2,1,0:T(8,128)(2,1)S(1)}, bf16[16,32,128]{2,1,0:T(8,128)(2,1)S(1)}) custom-call(bf16[256,896]{1,0:T(8,128)(2,1)} %bitcast.13, bf16[256,896]{1,0:T(8,128)(2,1)} %bitcast.14, bf16[64,4096]{1,0:T(8,128)(2,1)} %bitcast.12), custom_call_target="tpu_custom_call" | custom-call | tf_op jit(solution)/shard_map/pallas_call | solution.py:50
  2.3 3.1 %collective-permute-start = (bf16[52,32,128]{2,1,0:T(8,128)(2,1)S(1)}, bf16[52,32,128]{2,1,0:T(8,128)(2,1)S(1)}, u32[]{:S(2)}, u32[]{:S(2)}) collective-permute-start(bf16[52,32,128]{2,1,0:T(8,128)(2,1)S(1)} %get-tuple-element.55.refs_0_.refs_2_), channel_id=1, source_target_pairs={{0,4},{1,5},{2,6},{3,7},{4,12},{5,13},{6,14},{7,15},{8,0},{9,1},{1... | collective-permute-start | bytes 1277960 | tf_op jit(solution)/shard_map/ppermute | solution.py:31
  5.4 1.1 %collective-permute-start.1 = (bf16[52,32,128]{2,1,0:T(8,128)(2,1)S(1)}, bf16[52,32,128]{2,1,0:T(8,128)(2,1)S(1)}, u32[]{:S(2)}, u32[]{:S(2)}) collective-permute-start(bf16[52,32,128]{2,1,0:T(8,128)(2,1)S(1)} %get-tuple-element.56.refs_1_.refs_3_), channel_id=1, source_target_pairs={{0,8},{1,9},{2,10},{3,11},{4,0},{5,1},{6,2},{7,3},{8,12},{9,13},{1... | collective-permute-start | bytes 1277960 | tf_op jit(solution)/shard_map/ppermute | solution.py:31
  6.4 1.8 %collective-permute-start.6 = (bf16[16,32,128]{2,1,0:T(8,128)(2,1)S(1)}, bf16[16,32,128]{2,1,0:T(8,128)(2,1)S(1)}, u32[]{:S(2)}, u32[]{:S(2)}) collective-permute-start(bf16[16,32,128]{2,1,0:T(8,128)(2,1)S(1)} %get-tuple-element.62.refs_0_), channel_id=1, source_target_pairs={{0,2},{1,3},{2,0},{3,1},{4,6},{5,7},{6,4},{7,5},{8,10},{9,11},{10,... | collective-permute-start | bytes 393224 | tf_op jit(solution)/shard_map/ppermute | solution.py:31
  8.2 1.5 %copy-done.1 = bf16[1,1024,896]{2,1,0:T(8,128)(2,1)S(1)} copy-done((bf16[1,1024,896]{2,1,0:T(8,128)(2,1)S(1)}, bf16[1,1024,896]{2,1,0:T(8,128)(2,1)}, u32[]{:S(2)}) %copy-start.1) | copy-done | bytes 1835032
  11.0 1.6 %collective-permute-start.2 = (bf16[3,64,1024]{2,1,0:T(8,128)(2,1)S(1)}, bf16[3,64,1024]{2,1,0:T(8,128)(2,1)S(1)}, u32[]{:S(2)}, u32[]{:S(2)}) collective-permute-start(bf16[3,64,1024]{2,1,0:T(8,128)(2,1)S(1)} %shard_map.69), channel_id=1, source_target_pairs={{0,16},{1,17},{2,18},{3,19},{4,20},{5,21},{6,22},{7,23},{8,24},{9,... | collective-permute-start | bytes 1179656 | tf_op jit(solution)/shard_map/ppermute | solution.py:31
  13.3 4.7 %collective-permute-done.4.refs_2_ = bf16[64,1024]{1,0:T(8,128)(2,1)S(1)} collective-permute-done((bf16[64,1024]{1,0:T(8,128)(2,1)S(1)}, bf16[64,1024]{1,0:T(8,128)(2,1)S(1)}, u32[]{:S(2)}, u32[]{:S(2)}) %collective-permute-start.4) | collective-permute-done | bytes 131104 | tf_op jit(solution)/shard_map/ppermute | solution.py:31
  18.0 5.2 %collective-permute-done.5.refs_3_ = bf16[64,1024]{1,0:T(8,128)(2,1)S(1)} collective-permute-done((bf16[64,1024]{1,0:T(8,128)(2,1)S(1)}, bf16[64,1024]{1,0:T(8,128)(2,1)S(1)}, u32[]{:S(2)}, u32[]{:S(2)}) %collective-permute-start.5) | collective-permute-done | bytes 131104 | tf_op jit(solution)/shard_map/ppermute | solution.py:31
  23.3 2.1 %collective-permute-done.1.refs_1_.refs_7_ = bf16[52,32,128]{2,1,0:T(8,128)(2,1)S(1)} collective-permute-done((bf16[52,32,128]{2,1,0:T(8,128)(2,1)S(1)}, bf16[52,32,128]{2,1,0:T(8,128)(2,1)S(1)}, u32[]{:S(2)}, u32[]{:S(2)}) %collective-permute-start.1) | collective-permute-done | bytes 426016 | tf_op jit(solution)/shard_map/ppermute | solution.py:31
  25.3 1.8 %collective-permute-start.8 = (bf16[36,32,128]{2,1,0:T(8,128)(2,1)S(1)}, bf16[36,32,128]{2,1,0:T(8,128)(2,1)S(1)}, u32[]{:S(2)}, u32[]{:S(2)}) collective-permute-start(bf16[36,32,128]{2,1,0:T(8,128)(2,1)S(1)} %slice.12), channel_id=1, source_target_pairs={{0,4},{1,5},{2,6},{3,7},{4,12},{5,13},{6,14},{7,15},{8,0},{9,1},{1... | collective-permute-start | bytes 884744 | tf_op jit(solution)/shard_map/ppermute | solution.py:31
  27.2 1.2 %collective-permute-start.9 = (bf16[36,32,128]{2,1,0:T(8,128)(2,1)S(1)}, bf16[36,32,128]{2,1,0:T(8,128)(2,1)S(1)}, u32[]{:S(2)}, u32[]{:S(2)}) collective-permute-start(bf16[36,32,128]{2,1,0:T(8,128)(2,1)S(1)} %slice.13), channel_id=1, source_target_pairs={{0,8},{1,9},{2,10},{3,11},{4,0},{5,1},{6,2},{7,3},{8,12},{9,13},{1... | collective-permute-start | bytes 884744 | tf_op jit(solution)/shard_map/ppermute | solution.py:31
  28.4 0.7 %shard_map.76 = (bf16[1,2,32,1024]{3,2,1,0:T(8,128)(2,1)S(1)}, bf16[1,2,32,1024]{3,2,1,0:T(8,128)(2,1)S(1)}, bf16[1,2,32,1024]{3,2,1,0:T(8,128)(2,1)S(1)}, bf16[1,2,32,1024]{3,2,1,0:T(8,128)(2,1)S(1)}) custom-call(bf16[52,32,128]{2,1,0:T(8,128)(2,1)S(1)} %collective-permute-done.refs_0_.refs_6_, ...), custom_call_target="tpu_custom_call" | custom-call | tf_op jit(solution)/shard_map/pallas_call | solution.py:50
  29.7 1.6 %collective-permute-start.14 = (bf16[32,32,128]{2,1,0:T(8,128)(2,1)S(1)}, bf16[32,32,128]{2,1,0:T(8,128)(2,1)S(1)}, u32[]{:S(2)}, u32[]{:S(2)}) collective-permute-start(bf16[32,32,128]{2,1,0:T(8,128)(2,1)S(1)} %shard_map.79.refs_0_), channel_id=1, source_target_pairs={{0,2},{1,3},{2,0},{3,1},{4,6},{5,7},{6,4},{7,5},{8,10},{9,11},{10,... | collective-permute-start | bytes 786440 | tf_op jit(solution)/shard_map/ppermute | solution.py:31
  31.4 1.0 %collective-permute-start.13 = (bf16[2,1,32,1024]{3,2,1,0:T(8,128)(2,1)S(1)}, bf16[2,1,32,1024]{3,2,1,0:T(8,128)(2,1)S(1)}, u32[]{:S(2)}, u32[]{:S(2)}) collective-permute-start(bf16[2,1,32,1024]{3,2,1,0:T(8,128)(2,1)S(1)} %get-tuple-element.74), channel_id=1, source_target_pairs={{0,2},{1,3},{2,0},{3,1},{4,6},{5,7},{6,4},{7,5},{8,10},{9,11},{10,... | collective-permute-start | bytes 393224 | tf_op jit(solution)/shard_map/ppermute | solution.py:31
  32.5 1.6 %collective-permute-start.10 = (bf16[64,1024]{1,0:T(8,128)(2,1)S(1)}, bf16[64,1024]{1,0:T(8,128)(2,1)S(1)}, u32[]{:S(2)}, u32[]{:S(2)}) collective-permute-start(bf16[64,1024]{1,0:T(8,128)(2,1)S(1)} %shard_map.74), channel_id=1, source_target_pairs={{0,16},{1,17},{2,18},{3,19},{4,20},{5,21},{6,22},{7,23},{8,24},{9,... | collective-permute-start | bytes 393224 | tf_op jit(solution)/shard_map/ppermute | solution.py:31
  34.0 1.0 %shard_map.75.refs_12_ = f32[1024,896]{1,0:T(8,128)S(1)} custom-call(bf16[32,32,128]{2,1,0:T(8,128)(2,1)S(1)} %shard_map.73.refs_0_, bf16[32,32,128]{2,1,0:T(8,128)(2,1)S(1)} %collective-permute-done.7.refs_1_, bf16[52,32,128]{2,1,0:T(8,128)(2,1)S(1)} %get-tuple-element.55.refs_0_.refs_2_, bf16[52,32,128]{2,1,0:T(8,128)(2,1)S(1)} %get-tuple-element.56.refs_1_.refs_3_), custom_call_target="tpu_custom_call" | custom-call | tf_op jit(solution)/shard_map/pallas_call | solution.py:50
  35.1 5.9 %collective-permute-done.13.got = bf16[2,1,32,1024]{3,2,1,0:T(8,128)(2,1)S(1)} collective-permute-done((bf16[2,1,32,1024]{3,2,1,0:T(8,128)(2,1)S(1)}, bf16[2,1,32,1024]{3,2,1,0:T(8,128)(2,1)S(1)}, u32[]{:S(2)}, u32[]{:S(2)}) %collective-permute-start.13) | collective-permute-done | bytes 131104 | tf_op jit(solution)/shard_map/ppermute | solution.py:31
  41.6 0.8 %collective-permute-start.16 = (bf16[28,32,128]{2,1,0:T(8,128)(2,1)S(1)}, bf16[28,32,128]{2,1,0:T(8,128)(2,1)S(1)}, u32[]{:S(2)}, u32[]{:S(2)}) collective-permute-start(bf16[28,32,128]{2,1,0:T(8,128)(2,1)S(1)} %slice.14), channel_id=1, source_target_pairs={{0,4},{1,5},{2,6},{3,7},{4,12},{5,13},{6,14},{7,15},{8,0},{9,1},{1... | collective-permute-start | bytes 688136 | tf_op jit(solution)/shard_map/ppermute | solution.py:31
  42.4 2.2 %collective-permute-start.17 = (bf16[28,32,128]{2,1,0:T(8,128)(2,1)S(1)}, bf16[28,32,128]{2,1,0:T(8,128)(2,1)S(1)}, u32[]{:S(2)}, u32[]{:S(2)}) collective-permute-start(bf16[28,32,128]{2,1,0:T(8,128)(2,1)S(1)} %slice.15), channel_id=1, source_target_pairs={{0,8},{1,9},{2,10},{3,11},{4,0},{5,1},{6,2},{7,3},{8,12},{9,13},{1... | collective-permute-start | bytes 688136 | tf_op jit(solution)/shard_map/ppermute | solution.py:31
  44.7 0.7 %shard_map.80 = (bf16[64,1024]{1,0:T(8,128)(2,1)S(1)}, bf16[64,1024]{1,0:T(8,128)(2,1)S(1)}, bf16[32,32,128]{2,1,0:T(8,128)(2,1)S(1)}, bf16[64,1024]{1,0:T(8,128)(2,1)S(1)}) custom-call(bf16[36,32,128]{2,1,0:T(8,128)(2,1)S(1)} %collective-permute-done.8.refs_0_.refs_8_, bf16[36,32,128]{2,1,0:T(8,128)(2,1)S(1)} %collective-permute-done.9.refs_1_.refs_9_, ...), custom_call_target="tpu_custom_call" | custom-call | tf_op jit(solution)/shard_map/pallas_call | solution.py:50
  45.4 1.6 %collective-permute-start.15 = (bf16[32,32,128]{2,1,0:T(8,128)(2,1)S(1)}, bf16[32,32,128]{2,1,0:T(8,128)(2,1)S(1)}, u32[]{:S(2)}, u32[]{:S(2)}) collective-permute-start(bf16[32,32,128]{2,1,0:T(8,128)(2,1)S(1)} %get-tuple-element.81), channel_id=1, source_target_pairs={{0,2},{1,3},{2,0},{3,1},{4,6},{5,7},{6,4},{7,5},{8,10},{9,11},{10,... | collective-permute-start | bytes 786440 | tf_op jit(solution)/shard_map/ppermute | solution.py:31
  48.3 0.9 %collective-permute-done.16.refs_0_.refs_10_ = bf16[28,32,128]{2,1,0:T(8,128)(2,1)S(1)} collective-permute-done((bf16[28,32,128]{2,1,0:T(8,128)(2,1)S(1)}, bf16[28,32,128]{2,1,0:T(8,128)(2,1)S(1)}, u32[]{:S(2)}, u32[]{:S(2)}) %collective-permute-start.16) | collective-permute-done | bytes 229408 | tf_op jit(solution)/shard_map/ppermute | solution.py:31
  49.2 4.4 %collective-permute-done.17.refs_1_.refs_11_ = bf16[28,32,128]{2,1,0:T(8,128)(2,1)S(1)} collective-permute-done((bf16[28,32,128]{2,1,0:T(8,128)(2,1)S(1)}, bf16[28,32,128]{2,1,0:T(8,128)(2,1)S(1)}, u32[]{:S(2)}, u32[]{:S(2)}) %collective-permute-start.17) | collective-permute-done | bytes 229408 | tf_op jit(solution)/shard_map/ppermute | solution.py:31
  55.1 0.9 %collective-permute-done.20.refs_1_ = bf16[2,2,32,1024]{3,2,1,0:T(8,128)(2,1)S(1)} collective-permute-done((bf16[2,2,32,1024]{3,2,1,0:T(8,128)(2,1)S(1)}, bf16[2,2,32,1024]{3,2,1,0:T(8,128)(2,1)S(1)}, u32[]{:S(2)}, u32[]{:S(2)}) %collective-permute-start.20) | collective-permute-done | bytes 262176 | tf_op jit(solution)/shard_map/ppermute | solution.py:31
  56.1 1.6 %collective-permute-start.26 = (bf16[2,1,32,1024]{3,2,1,0:T(8,128)(2,1)S(1)}, bf16[2,1,32,1024]{3,2,1,0:T(8,128)(2,1)S(1)}, u32[]{:S(2)}, u32[]{:S(2)}) collective-permute-start(bf16[2,1,32,1024]{3,2,1,0:T(8,128)(2,1)S(1)} %get-tuple-element.90), channel_id=1, source_target_pairs={{0,2},{1,3},{2,0},{3,1},{4,6},{5,7},{6,4},{7,5},{8,10},{9,11},{10,... | collective-permute-start | bytes 393224 | tf_op jit(solution)/shard_map/ppermute | solution.py:31
  57.9 1.6 %collective-permute-start.21 = (bf16[64,1024]{1,0:T(8,128)(2,1)S(1)}, bf16[64,1024]{1,0:T(8,128)(2,1)S(1)}, u32[]{:S(2)}, u32[]{:S(2)}) collective-permute-start(bf16[64,1024]{1,0:T(8,128)(2,1)S(1)} %shard_map.82), channel_id=1, source_target_pairs={{0,16},{1,17},{2,18},{3,19},{4,20},{5,21},{6,22},{7,23},{8,24},{9,... | collective-permute-start | bytes 393224 | tf_op jit(solution)/shard_map/ppermute | solution.py:31
  59.4 2.3 %collective-permute-done.26.got = bf16[2,1,32,1024]{3,2,1,0:T(8,128)(2,1)S(1)} collective-permute-done((bf16[2,1,32,1024]{3,2,1,0:T(8,128)(2,1)S(1)}, bf16[2,1,32,1024]{3,2,1,0:T(8,128)(2,1)S(1)}, u32[]{:S(2)}, u32[]{:S(2)}) %collective-permute-start.26) | collective-permute-done | bytes 131104 | tf_op jit(solution)/shard_map/ppermute | solution.py:31
  61.8 1.6 %collective-permute-start.27 = (bf16[64,1024]{1,0:T(8,128)(2,1)S(1)}, bf16[64,1024]{1,0:T(8,128)(2,1)S(1)}, u32[]{:S(2)}, u32[]{:S(2)}) collective-permute-start(bf16[64,1024]{1,0:T(8,128)(2,1)S(1)} %get-tuple-element.100), channel_id=1, source_target_pairs={{0,16},{1,17},{2,18},{3,19},{4,20},{5,21},{6,22},{7,23},{8,24},{9,... | collective-permute-start | bytes 393224 | tf_op jit(solution)/shard_map/ppermute | solution.py:31
  63.4 1.5 %collective-permute-start.28 = (bf16[64,1024]{1,0:T(8,128)(2,1)S(1)}, bf16[64,1024]{1,0:T(8,128)(2,1)S(1)}, u32[]{:S(2)}, u32[]{:S(2)}) collective-permute-start(bf16[64,1024]{1,0:T(8,128)(2,1)S(1)} %get-tuple-element.103), channel_id=1, source_target_pairs={{0,16},{1,17},{2,18},{3,19},{4,20},{5,21},{6,22},{7,23},{8,24},{9,... | collective-permute-start | bytes 393224 | tf_op jit(solution)/shard_map/ppermute | solution.py:31
  64.9 2.6 %collective-permute-start.22 = (bf16[64,1024]{1,0:T(8,128)(2,1)S(1)}, bf16[64,1024]{1,0:T(8,128)(2,1)S(1)}, u32[]{:S(2)}, u32[]{:S(2)}) collective-permute-start(bf16[64,1024]{1,0:T(8,128)(2,1)S(1)} %collective-permute-done.21), channel_id=1, source_target_pairs={{0,12},{1,13},{2,14},{3,15},{4,8},{5,9},{6,10},{7,11},{8,4},{9,5},... | collective-permute-start | bytes 393224 | tf_op jit(solution)/shard_map/ppermute | solution.py:31
  67.5 3.2 %shard_map.87 = bf16[1024,896]{1,0:T(8,128)(2,1)} custom-call(bf16[32,32,128]{2,1,0:T(8,128)(2,1)S(1)} %shard_map.79.refs_0_, bf16[32,32,128]{2,1,0:T(8,128)(2,1)S(1)} %collective-permute-done.23.refs_1_, bf16[32,32,128]{2,1,0:T(8,128)(2,1)S(1)} %collective-permute-done.14.refs_2_, bf16[32,32,128]{2,1,0:T(8,128)(2,1)S(1)} %collective-permute-done.24.refs_3_, ...), custom_call_target="tpu_custom_call" | custom-call | tf_op jit(solution)/shard_map/pallas_call | solution.py:50
  71.8 0.8 %shard_map.88 = bf16[64,4096]{1,0:T(8,128)(2,1)} custom-call(bf16[3,64,1024]{2,1,0:T(8,128)(2,1)S(1)} %collective-permute-done.2.base, bf16[64,1024]{1,0:T(8,128)(2,1)S(1)} %collective-permute-done.22.refs_0_, bf16[64,1024]{1,0:T(8,128)(2,1)S(1)} %collective-permute-done.27.refs_1_, ...), custom_call_target="tpu_custom_call", output_to_operand_aliasing={{}: (4, {})} | custom-call | tf_op jit(solution)/shard_map/pallas_call | solution.py:50
  (55 shorter events, 7.5 us)
Async XLA Ops:
  2.3 21.0 %collective-permute-start = (bf16[52,32,128]{2,1,0:T(8,128)(2,1)S(1)}, bf16[52,32,128]{2,1,0:T(8,128)(2,1)S(1)}, u32[]{:S(2)}, u32[]{:S(2)}) collective-permute-start(bf16[52,32,128]{2,1,0:T(8,128)(2,1)S(1)} %get-tuple-element.55.refs_0_.refs_2_), channel_id=1, source_target_pairs={{0,4},{1,5},{2,6},{3,7},{4,12},{5,13},{6,14},{7,15},{8,0},{9,1},{1... | collective-permute-start | bytes 1277960 | tf_op jit(solution)/shard_map/ppermute | solution.py:31
  5.4 20.0 %collective-permute-start.1 = (bf16[52,32,128]{2,1,0:T(8,128)(2,1)S(1)}, bf16[52,32,128]{2,1,0:T(8,128)(2,1)S(1)}, u32[]{:S(2)}, u32[]{:S(2)}) collective-permute-start(bf16[52,32,128]{2,1,0:T(8,128)(2,1)S(1)} %get-tuple-element.56.refs_1_.refs_3_), channel_id=1, source_target_pairs={{0,8},{1,9},{2,10},{3,11},{4,0},{5,1},{6,2},{7,3},{8,12},{9,13},{1... | collective-permute-start | bytes 1277960 | tf_op jit(solution)/shard_map/ppermute | solution.py:31
  6.4 6.1 %collective-permute-start.6 = (bf16[16,32,128]{2,1,0:T(8,128)(2,1)S(1)}, bf16[16,32,128]{2,1,0:T(8,128)(2,1)S(1)}, u32[]{:S(2)}, u32[]{:S(2)}) collective-permute-start(bf16[16,32,128]{2,1,0:T(8,128)(2,1)S(1)} %get-tuple-element.62.refs_0_), channel_id=1, source_target_pairs={{0,2},{1,3},{2,0},{3,1},{4,6},{5,7},{6,4},{7,5},{8,10},{9,11},{10,... | collective-permute-start | bytes 393224 | tf_op jit(solution)/shard_map/ppermute | solution.py:31
  8.2 1.5 %copy-start.1 = (bf16[1,1024,896]{2,1,0:T(8,128)(2,1)S(1)}, bf16[1,1024,896]{2,1,0:T(8,128)(2,1)}, u32[]{:S(2)}) copy-start(bf16[1,1024,896]{2,1,0:T(8,128)(2,1)} %param.9) | copy-start | bytes 5505028
  9.9 1.0 %copy-start = (bf16[1,1,64,4096]{3,2,1,0:T(8,128)(2,1)S(1)}, bf16[1,1,64,4096]{3,2,1,0:T(8,128)(2,1)}, u32[]{:S(2)}) copy-start(bf16[1,1,64,4096]{3,2,1,0:T(8,128)(2,1)} %param.6) | copy-start | bytes 1572868
  10.6 2.6 %collective-permute-start.3 = (bf16[64,1024]{1,0:T(8,128)(2,1)S(1)}, bf16[64,1024]{1,0:T(8,128)(2,1)S(1)}, u32[]{:S(2)}, u32[]{:S(2)}) collective-permute-start(bf16[64,1024]{1,0:T(8,128)(2,1)S(1)} %get-tuple-element.59), channel_id=1, source_target_pairs={{0,1},{1,0},{2,3},{3,2},{4,5},{5,4},{6,7},{7,6},{8,9},{9,8},{10,11... | collective-permute-start | bytes 393224 | tf_op jit(solution)/shard_map/ppermute | solution.py:31
  11.0 12.2 %collective-permute-start.2 = (bf16[3,64,1024]{2,1,0:T(8,128)(2,1)S(1)}, bf16[3,64,1024]{2,1,0:T(8,128)(2,1)S(1)}, u32[]{:S(2)}, u32[]{:S(2)}) collective-permute-start(bf16[3,64,1024]{2,1,0:T(8,128)(2,1)S(1)} %shard_map.69), channel_id=1, source_target_pairs={{0,16},{1,17},{2,18},{3,19},{4,20},{5,21},{6,22},{7,23},{8,24},{9,... | collective-permute-start | bytes 1179656 | tf_op jit(solution)/shard_map/ppermute | solution.py:31
  12.6 5.4 %collective-permute-start.4 = (bf16[64,1024]{1,0:T(8,128)(2,1)S(1)}, bf16[64,1024]{1,0:T(8,128)(2,1)S(1)}, u32[]{:S(2)}, u32[]{:S(2)}) collective-permute-start(bf16[64,1024]{1,0:T(8,128)(2,1)S(1)} %get-tuple-element.60), channel_id=1, source_target_pairs={{0,2},{1,3},{2,0},{3,1},{4,6},{5,7},{6,4},{7,5},{8,10},{9,11},{10,... | collective-permute-start | bytes 393224 | tf_op jit(solution)/shard_map/ppermute | solution.py:31
  13.2 10.0 %collective-permute-start.7 = (bf16[32,32,128]{2,1,0:T(8,128)(2,1)S(1)}, bf16[32,32,128]{2,1,0:T(8,128)(2,1)S(1)}, u32[]{:S(2)}, u32[]{:S(2)}) collective-permute-start(bf16[32,32,128]{2,1,0:T(8,128)(2,1)S(1)} %shard_map.73.refs_0_), channel_id=1, source_target_pairs={{0,1},{1,0},{2,3},{3,2},{4,5},{5,4},{6,7},{7,6},{8,9},{9,8},{10,11... | collective-permute-start | bytes 786440 | tf_op jit(solution)/shard_map/ppermute | solution.py:31
  18.0 5.2 %collective-permute-start.5 = (bf16[64,1024]{1,0:T(8,128)(2,1)S(1)}, bf16[64,1024]{1,0:T(8,128)(2,1)S(1)}, u32[]{:S(2)}, u32[]{:S(2)}) collective-permute-start(bf16[64,1024]{1,0:T(8,128)(2,1)S(1)} %get-tuple-element.61), channel_id=1, source_target_pairs={{0,3},{1,2},{2,1},{3,0},{4,7},{5,6},{6,5},{7,4},{8,11},{9,10},{10,... | collective-permute-start | bytes 393224 | tf_op jit(solution)/shard_map/ppermute | solution.py:31
  25.3 16.2 %collective-permute-start.8 = (bf16[36,32,128]{2,1,0:T(8,128)(2,1)S(1)}, bf16[36,32,128]{2,1,0:T(8,128)(2,1)S(1)}, u32[]{:S(2)}, u32[]{:S(2)}) collective-permute-start(bf16[36,32,128]{2,1,0:T(8,128)(2,1)S(1)} %slice.12), channel_id=1, source_target_pairs={{0,4},{1,5},{2,6},{3,7},{4,12},{5,13},{6,14},{7,15},{8,0},{9,1},{1... | collective-permute-start | bytes 884744 | tf_op jit(solution)/shard_map/ppermute | solution.py:31
  27.2 14.4 %collective-permute-start.9 = (bf16[36,32,128]{2,1,0:T(8,128)(2,1)S(1)}, bf16[36,32,128]{2,1,0:T(8,128)(2,1)S(1)}, u32[]{:S(2)}, u32[]{:S(2)}) collective-permute-start(bf16[36,32,128]{2,1,0:T(8,128)(2,1)S(1)} %slice.13), channel_id=1, source_target_pairs={{0,8},{1,9},{2,10},{3,11},{4,0},{5,1},{6,2},{7,3},{8,12},{9,13},{1... | collective-permute-start | bytes 884744 | tf_op jit(solution)/shard_map/ppermute | solution.py:31
  29.1 2.2 %collective-permute-start.11 = (bf16[1,2,32,1024]{3,2,1,0:T(8,128)(2,1)S(1)}, bf16[1,2,32,1024]{3,2,1,0:T(8,128)(2,1)S(1)}, u32[]{:S(2)}, u32[]{:S(2)}) collective-permute-start(bf16[1,2,32,1024]{3,2,1,0:T(8,128)(2,1)S(1)} %get-tuple-element.70), channel_id=1, source_target_pairs={{0,1},{1,0},{2,3},{3,2},{4,5},{5,4},{6,7},{7,6},{8,9},{9,8},{10,11... | collective-permute-start | bytes 393224 | tf_op jit(solution)/shard_map/ppermute | solution.py:31
  29.2 2.2 %collective-permute-start.12 = (bf16[1,2,32,1024]{3,2,1,0:T(8,128)(2,1)S(1)}, bf16[1,2,32,1024]{3,2,1,0:T(8,128)(2,1)S(1)}, u32[]{:S(2)}, u32[]{:S(2)}) collective-permute-start(bf16[1,2,32,1024]{3,2,1,0:T(8,128)(2,1)S(1)} %get-tuple-element.72), channel_id=1, source_target_pairs={{0,1},{1,0},{2,3},{3,2},{4,5},{5,4},{6,7},{7,6},{8,9},{9,8},{10,11... | collective-permute-start | bytes 393224 | tf_op jit(solution)/shard_map/ppermute | solution.py:31
  29.7 14.9 %collective-permute-start.14 = (bf16[32,32,128]{2,1,0:T(8,128)(2,1)S(1)}, bf16[32,32,128]{2,1,0:T(8,128)(2,1)S(1)}, u32[]{:S(2)}, u32[]{:S(2)}) collective-permute-start(bf16[32,32,128]{2,1,0:T(8,128)(2,1)S(1)} %shard_map.79.refs_0_), channel_id=1, source_target_pairs={{0,2},{1,3},{2,0},{3,1},{4,6},{5,7},{6,4},{7,5},{8,10},{9,11},{10,... | collective-permute-start | bytes 786440 | tf_op jit(solution)/shard_map/ppermute | solution.py:31
  31.4 9.5 %collective-permute-start.13 = (bf16[2,1,32,1024]{3,2,1,0:T(8,128)(2,1)S(1)}, bf16[2,1,32,1024]{3,2,1,0:T(8,128)(2,1)S(1)}, u32[]{:S(2)}, u32[]{:S(2)}) collective-permute-start(bf16[2,1,32,1024]{3,2,1,0:T(8,128)(2,1)S(1)} %get-tuple-element.74), channel_id=1, source_target_pairs={{0,2},{1,3},{2,0},{3,1},{4,6},{5,7},{6,4},{7,5},{8,10},{9,11},{10,... | collective-permute-start | bytes 393224 | tf_op jit(solution)/shard_map/ppermute | solution.py:31
  32.5 8.5 %collective-permute-start.10 = (bf16[64,1024]{1,0:T(8,128)(2,1)S(1)}, bf16[64,1024]{1,0:T(8,128)(2,1)S(1)}, u32[]{:S(2)}, u32[]{:S(2)}) collective-permute-start(bf16[64,1024]{1,0:T(8,128)(2,1)S(1)} %shard_map.74), channel_id=1, source_target_pairs={{0,16},{1,17},{2,18},{3,19},{4,20},{5,21},{6,22},{7,23},{8,24},{9,... | collective-permute-start | bytes 393224 | tf_op jit(solution)/shard_map/ppermute | solution.py:31
  41.6 7.6 %collective-permute-start.16 = (bf16[28,32,128]{2,1,0:T(8,128)(2,1)S(1)}, bf16[28,32,128]{2,1,0:T(8,128)(2,1)S(1)}, u32[]{:S(2)}, u32[]{:S(2)}) collective-permute-start(bf16[28,32,128]{2,1,0:T(8,128)(2,1)S(1)} %slice.14), channel_id=1, source_target_pairs={{0,4},{1,5},{2,6},{3,7},{4,12},{5,13},{6,14},{7,15},{8,0},{9,1},{1... | collective-permute-start | bytes 688136 | tf_op jit(solution)/shard_map/ppermute | solution.py:31
  42.4 11.2 %collective-permute-start.17 = (bf16[28,32,128]{2,1,0:T(8,128)(2,1)S(1)}, bf16[28,32,128]{2,1,0:T(8,128)(2,1)S(1)}, u32[]{:S(2)}, u32[]{:S(2)}) collective-permute-start(bf16[28,32,128]{2,1,0:T(8,128)(2,1)S(1)} %slice.15), channel_id=1, source_target_pairs={{0,8},{1,9},{2,10},{3,11},{4,0},{5,1},{6,2},{7,3},{8,12},{9,13},{1... | collective-permute-start | bytes 688136 | tf_op jit(solution)/shard_map/ppermute | solution.py:31
  45.4 9.0 %collective-permute-start.15 = (bf16[32,32,128]{2,1,0:T(8,128)(2,1)S(1)}, bf16[32,32,128]{2,1,0:T(8,128)(2,1)S(1)}, u32[]{:S(2)}, u32[]{:S(2)}) collective-permute-start(bf16[32,32,128]{2,1,0:T(8,128)(2,1)S(1)} %get-tuple-element.81), channel_id=1, source_target_pairs={{0,2},{1,3},{2,0},{3,1},{4,6},{5,7},{6,4},{7,5},{8,10},{9,11},{10,... | collective-permute-start | bytes 786440 | tf_op jit(solution)/shard_map/ppermute | solution.py:31
  47.1 7.3 %collective-permute-start.18 = (bf16[64,1024]{1,0:T(8,128)(2,1)S(1)}, bf16[64,1024]{1,0:T(8,128)(2,1)S(1)}, u32[]{:S(2)}, u32[]{:S(2)}) collective-permute-start(bf16[64,1024]{1,0:T(8,128)(2,1)S(1)} %get-tuple-element.84), channel_id=1, source_target_pairs={{0,1},{1,0},{2,3},{3,2},{4,5},{5,4},{6,7},{7,6},{8,9},{9,8},{10,11... | collective-permute-start | bytes 393224 | tf_op jit(solution)/shard_map/ppermute | solution.py:31
  47.1 7.3 %collective-permute-start.19 = (bf16[64,1024]{1,0:T(8,128)(2,1)S(1)}, bf16[64,1024]{1,0:T(8,128)(2,1)S(1)}, u32[]{:S(2)}, u32[]{:S(2)}) collective-permute-start(bf16[64,1024]{1,0:T(8,128)(2,1)S(1)} %get-tuple-element.85), channel_id=1, source_target_pairs={{0,3},{1,2},{2,1},{3,0},{4,7},{5,6},{6,5},{7,4},{8,11},{9,10},{10,... | collective-permute-start | bytes 393224 | tf_op jit(solution)/shard_map/ppermute | solution.py:31
  54.5 1.6 %collective-permute-start.20 = (bf16[2,2,32,1024]{3,2,1,0:T(8,128)(2,1)S(1)}, bf16[2,2,32,1024]{3,2,1,0:T(8,128)(2,1)S(1)}, u32[]{:S(2)}, u32[]{:S(2)}) collective-permute-start(bf16[2,2,32,1024]{3,2,1,0:T(8,128)(2,1)S(1)} %get-tuple-element.89), channel_id=1, source_target_pairs={{0,1},{1,0},{2,3},{3,2},{4,5},{5,4},{6,7},{7,6},{8,9},{9,8},{10,11... | collective-permute-start | bytes 786440 | tf_op jit(solution)/shard_map/ppermute | solution.py:31
  54.6 8.7 %collective-permute-start.23 = (bf16[32,32,128]{2,1,0:T(8,128)(2,1)S(1)}, bf16[32,32,128]{2,1,0:T(8,128)(2,1)S(1)}, u32[]{:S(2)}, u32[]{:S(2)}) collective-permute-start(bf16[32,32,128]{2,1,0:T(8,128)(2,1)S(1)} %shard_map.79.refs_0_), channel_id=1, source_target_pairs={{0,1},{1,0},{2,3},{3,2},{4,5},{5,4},{6,7},{7,6},{8,9},{9,8},{10,11... | collective-permute-start | bytes 786440 | tf_op jit(solution)/shard_map/ppermute | solution.py:31
  55.0 12.4 %collective-permute-start.24 = (bf16[32,32,128]{2,1,0:T(8,128)(2,1)S(1)}, bf16[32,32,128]{2,1,0:T(8,128)(2,1)S(1)}, u32[]{:S(2)}, u32[]{:S(2)}) collective-permute-start(bf16[32,32,128]{2,1,0:T(8,128)(2,1)S(1)} %collective-permute-done.14.refs_2_), channel_id=1, source_target_pairs={{0,1},{1,0},{2,3},{3,2},{4,5},{5,4},{6,7},{7,6},{8,9},{9,8},{10,11... | collective-permute-start | bytes 786440 | tf_op jit(solution)/shard_map/ppermute | solution.py:31
  56.1 5.6 %collective-permute-start.26 = (bf16[2,1,32,1024]{3,2,1,0:T(8,128)(2,1)S(1)}, bf16[2,1,32,1024]{3,2,1,0:T(8,128)(2,1)S(1)}, u32[]{:S(2)}, u32[]{:S(2)}) collective-permute-start(bf16[2,1,32,1024]{3,2,1,0:T(8,128)(2,1)S(1)} %get-tuple-element.90), channel_id=1, source_target_pairs={{0,2},{1,3},{2,0},{3,1},{4,6},{5,7},{6,4},{7,5},{8,10},{9,11},{10,... | collective-permute-start | bytes 393224 | tf_op jit(solution)/shard_map/ppermute | solution.py:31
  57.8 9.7 %collective-permute-start.25 = (bf16[32,32,128]{2,1,0:T(8,128)(2,1)S(1)}, bf16[32,32,128]{2,1,0:T(8,128)(2,1)S(1)}, u32[]{:S(2)}, u32[]{:S(2)}) collective-permute-start(bf16[32,32,128]{2,1,0:T(8,128)(2,1)S(1)} %shard_map.85.refs_4_), channel_id=1, source_target_pairs={{0,1},{1,0},{2,3},{3,2},{4,5},{5,4},{6,7},{7,6},{8,9},{9,8},{10,11... | collective-permute-start | bytes 786440 | tf_op jit(solution)/shard_map/ppermute | solution.py:31
  57.9 7.1 %collective-permute-start.21 = (bf16[64,1024]{1,0:T(8,128)(2,1)S(1)}, bf16[64,1024]{1,0:T(8,128)(2,1)S(1)}, u32[]{:S(2)}, u32[]{:S(2)}) collective-permute-start(bf16[64,1024]{1,0:T(8,128)(2,1)S(1)} %shard_map.82), channel_id=1, source_target_pairs={{0,16},{1,17},{2,18},{3,19},{4,20},{5,21},{6,22},{7,23},{8,24},{9,... | collective-permute-start | bytes 393224 | tf_op jit(solution)/shard_map/ppermute | solution.py:31
  61.8 8.9 %collective-permute-start.27 = (bf16[64,1024]{1,0:T(8,128)(2,1)S(1)}, bf16[64,1024]{1,0:T(8,128)(2,1)S(1)}, u32[]{:S(2)}, u32[]{:S(2)}) collective-permute-start(bf16[64,1024]{1,0:T(8,128)(2,1)S(1)} %get-tuple-element.100), channel_id=1, source_target_pairs={{0,16},{1,17},{2,18},{3,19},{4,20},{5,21},{6,22},{7,23},{8,24},{9,... | collective-permute-start | bytes 393224 | tf_op jit(solution)/shard_map/ppermute | solution.py:31
  63.4 7.8 %collective-permute-start.28 = (bf16[64,1024]{1,0:T(8,128)(2,1)S(1)}, bf16[64,1024]{1,0:T(8,128)(2,1)S(1)}, u32[]{:S(2)}, u32[]{:S(2)}) collective-permute-start(bf16[64,1024]{1,0:T(8,128)(2,1)S(1)} %get-tuple-element.103), channel_id=1, source_target_pairs={{0,16},{1,17},{2,18},{3,19},{4,20},{5,21},{6,22},{7,23},{8,24},{9,... | collective-permute-start | bytes 393224 | tf_op jit(solution)/shard_map/ppermute | solution.py:31
  64.9 6.9 %collective-permute-start.22 = (bf16[64,1024]{1,0:T(8,128)(2,1)S(1)}, bf16[64,1024]{1,0:T(8,128)(2,1)S(1)}, u32[]{:S(2)}, u32[]{:S(2)}) collective-permute-start(bf16[64,1024]{1,0:T(8,128)(2,1)S(1)} %collective-permute-done.21), channel_id=1, source_target_pairs={{0,12},{1,13},{2,14},{3,15},{4,8},{5,9},{6,10},{7,11},{8,4},{9,5},... | collective-permute-start | bytes 393224 | tf_op jit(solution)/shard_map/ppermute | solution.py:31
